TPU v7x, 256 devices: a whole 4x4x8 slice. The times are simulated.
256 devices in a mesh: blk: 128 (over x, z, y_lo, core), rep: 2 (over y_hi).
Axes of the slice: x: 4, y: 4 (y_hi: 2, y_lo: 2; y = y_hi * 2 + y_lo), z: 8, core: 2. Of those that a mesh axis runs over, the one named last changes fastest.
Arguments:
- image_emb: bfloat16 [131072, 1152], P(('blk', 'rep')), may hold values from -0.19921875 to 0.19921875
- text_emb: bfloat16 [131072, 1152], P(('blk', 'rep')), may hold values from -0.19921875 to 0.19921875
- log_temp: float32 [], replicated, may hold values from 1 to 2
- bias: float32 [], replicated, may hold values from -2 to 0
Outputs:
- row_loss: float32 [131072], P(('blk', 'rep'))
- grad_image: float32 [131072, 1152], P(('blk', 'rep'))
- grad_text: float32 [131072, 1152], P(('blk', 'rep'))
All inputs are finite; a program needn't handle non-finite values.
Results may differ from a plain program's by a relative error of at most 0.0042.
Values may be sent and summed in bfloat16 or wider, within the bound.
No kernel may reach another device: no remote copies, remote signals or barrier semaphores. Data moves between devices by JAX's collectives and lax.ppermute only.
A program may use at most 64 MiB of HBM per device.

v0:
```python
import functools

import jax
import jax.numpy as jnp
from jax import lax
from jax.experimental import pallas as pl
from jax.experimental.pallas import tpu as pltpu
from jax.sharding import PartitionSpec as P

AXES = ("blk", "rep")
EPSILON = 1e-06
CHUNK = 256
STRIP = 64
LANES = 128


def by_role(steps):
    def pairs():
        count = lax.axis_size(AXES)
        return [(b, (b + steps[b % 8]) % count) for b in range(count) if b % 8 in steps]

    return pairs


SWAP = by_role({0: 2, 1: 2, 4: 2, 5: 2, 2: -2, 3: -2, 6: -2, 7: -2})
SECOND = by_role({0: -2, 1: -2, 4: -2, 5: -2, 2: 2, 3: 2, 6: 2, 7: 2})
OF_OTHER = by_role({1: 3, 5: 3, 2: -3, 6: -3, 0: 1, 4: 1, 3: -1, 7: -1})
NEAR_OF_MAIN = by_role({0: -1, 4: -1, 3: 1, 7: 1})
ON_BY_TWO = by_role({0: -2, 4: -2, 3: 2, 7: 2})
FAR_OR_ON_BY_ONE = by_role({1: -3, 5: -3, 2: 3, 6: 3, 0: -1, 4: -1, 3: 1, 7: 1})


def send(x, pairs):
    return lax.ppermute(x, AXES, pairs())


def together(*arrays):
    return lax.optimization_barrier(arrays)


def strips(count, step):
    def at(k, carry):
        step(pl.ds(pl.multiple_of(k * STRIP, STRIP), STRIP))
        return carry

    lax.fori_loop(0, count // STRIP, at, 0)


def unit_of(raw_ref, rows):
    values = raw_ref[rows, :].astype(jnp.float32)
    scale = lax.rsqrt(jnp.sum(values * values, axis=-1, keepdims=True) + EPSILON)
    return values * scale, scale


def lower(raw_ref, low_ref):
    def step(rows):
        low_ref[rows, :] = unit_of(raw_ref, rows)[0].astype(jnp.bfloat16)

    strips(raw_ref.shape[0], step)


def lower_one_of(chosen, this_ref, that_ref, low_ref):
    @pl.when(chosen)
    def _():
        lower(this_ref, low_ref)

    @pl.when(jnp.logical_not(chosen))
    def _():
        lower(that_ref, low_ref)


def terms(logits):
    shrunk = jnp.exp(-jnp.abs(logits))
    total = 1.0 + shrunk
    losses = jnp.maximum(logits, 0.0) + jnp.log(total)
    return losses, jnp.where(logits >= 0.0, 1.0, shrunk) / total


def folded(losses):
    out = losses[:, :LANES]
    for at in range(LANES, losses.shape[1], LANES):
        out = out + losses[:, at : at + LANES]
    return out


def product(left, right, left_dim, right_dim):
    return lax.dot_general(
        left, right, (((left_dim,), (right_dim,)), ((), ())), preferred_element_type=jnp.float32
    )


def partner_grad(numbers_ref, own_ref, partner_ref, loss_from, loss_to, counts, rows):
    temper, bias = numbers_ref[0], numbers_ref[1]
    logits = temper * product(own_ref[rows, :], partner_ref[...], 1, 1) + bias
    losses, chances = terms(logits)
    loss_to[rows, :] = loss_from[rows, :] + counts * folded(losses)
    weights = (chances * temper).astype(jnp.bfloat16)
    return product(weights, partner_ref[...], 1, 0)


def pair(numbers_ref, own_ref, partner_ref, acc_from, acc_to, loss_from, loss_to, counts):
    for at in range(0, own_ref.shape[0], CHUNK):
        rows = pl.ds(at, CHUNK)
        grad = partner_grad(numbers_ref, own_ref, partner_ref, loss_from, loss_to, counts, rows)
        acc_to[rows, :] = acc_from[rows, :] + grad


def first_kernel(
    role_ref, numbers_ref, main, other, swapped,
    lows, units, scales, accs, loss_ref, weights_ref, low_ref,
):
    temper, bias = numbers_ref[0], numbers_ref[1]
    core = role_ref[0]
    count = main.shape[0]
    for side, raw in enumerate((main, other)):

        def step(rows, side=side, raw=raw):
            unit, scale = unit_of(raw, rows)
            units[side, rows, :] = unit
            scales[side, rows, :] = scale
            lows[side, rows, :] = unit.astype(jnp.bfloat16)

        strips(count, step)
    image_low, text_low = lows.at[core], lows.at[1 - core]
    for at in range(0, count, CHUNK):
        rows = pl.ds(at, CHUNK)
        logits = temper * product(image_low[rows, :], text_low[...], 1, 1) + bias
        row = lax.broadcasted_iota(jnp.int32, (CHUNK, count), 0) + at
        column = lax.broadcasted_iota(jnp.int32, (CHUNK, count), 1)
        same = row == column
        losses, chances = terms(jnp.where(same, -logits, logits))
        loss_ref[rows, :] = folded(losses)
        weights = (jnp.where(same, -chances, chances) * temper).astype(jnp.bfloat16)
        weights_ref[rows, :] = weights
        accs[core, rows, :] = product(weights, text_low[...], 1, 0)
    accs[1 - core] = product(weights_ref[...], image_low[...], 0, 0)
    lower(swapped, low_ref)
    pair(
        numbers_ref, lows.at[1], low_ref, accs.at[1], accs.at[1], loss_ref, loss_ref, core.astype(jnp.float32)
    )


def sent_kernel(role_ref, lows, second, near_main, of_other, near_low, late_low):
    outer = role_ref[0] == role_ref[1]
    lower_one_of(outer, near_main, of_other, near_low)

    @pl.when(outer)
    def _():
        lower(second, late_low)

    @pl.when(jnp.logical_not(outer))
    def _():
        late_low[...] = lows[0]


def middle_kernel(
    role_ref, numbers_ref, lows, second, near_low, swapped, accs_in, loss_in, accs, loss_ref, low_ref
):
    on_other = role_ref[0].astype(jnp.float32)
    on_main = 1.0 - on_other
    pair(numbers_ref, lows.at[0], near_low, accs_in.at[0], accs.at[0], loss_in, loss_ref, on_main)
    lower(second, low_ref)
    pair(numbers_ref, lows.at[0], low_ref, accs.at[0], accs.at[0], loss_ref, loss_ref, on_main)
    pair(numbers_ref, lows.at[1], swapped, accs_in.at[1], accs.at[1], loss_ref, loss_ref, on_other)


def close_side(
    side, core, numbers_ref, lows, units, scales, accs, partner_ref, loss_from, loss_to,
    image_out, text_out, done_ref, sems,
):
    counts = (side == core).astype(jnp.float32)
    own_low = lows.at[side]

    parts = done_ref.shape[0] // CHUNK

    def copy(k, out):
        rows = pl.ds(k * CHUNK, CHUNK)
        return pltpu.make_async_copy(done_ref.at[rows, :], out.at[rows, :], sems.at[k])

    for k in range(parts):
        rows = pl.ds(k * CHUNK, CHUNK)
        grad = accs[side, rows, :] + partner_grad(
            numbers_ref, own_low, partner_ref, loss_from, loss_to, counts, rows
        )
        unit = units[side, rows, :]
        along = jnp.sum(unit * grad, axis=-1, keepdims=True)
        done_ref[rows, :] = scales[side, rows, :] * (grad - unit * along)

        @pl.when(side == core)
        def _():
            copy(k, image_out).start()

        @pl.when(side != core)
        def _():
            copy(k, text_out).start()

    @pl.when(side == core)
    def _():
        for k in range(parts):
            copy(k, image_out).wait()

    @pl.when(side != core)
    def _():
        for k in range(parts):
            copy(k, text_out).wait()


def early_kernel(
    role_ref, numbers_ref, lows, units, scales, accs, of_other, by_two, loss_in,
    image_out, text_out, loss_ref, low_ref, done_ref, sems,
):
    outer = role_ref[0] == role_ref[1]
    lower_one_of(outer, of_other, by_two, low_ref)
    close_side(
        jnp.where(outer, 0, 1), role_ref[0], numbers_ref, lows, units, scales, accs, low_ref,
        loss_in, loss_ref, image_out, text_out, done_ref, sems,
    )


def late_kernel(
    role_ref, numbers_ref, lows, units, scales, accs, late_low, loss_in, image_in, text_in,
    image_out, text_out, row_loss, loss_ref, done_ref, sems,
):
    outer = role_ref[0] == role_ref[1]
    close_side(
        jnp.where(outer, 1, 0), role_ref[0], numbers_ref, lows, units, scales, accs, late_low,
        loss_in, loss_ref, image_out, text_out, done_ref, sems,
    )
    row_loss[...] = jnp.sum(loss_ref[...].T, axis=0, keepdims=True)


def call(kernel, in_kinds, outs, scratch=(), aliases=None):
    kinds = {
        "s": pl.BlockSpec(memory_space=pltpu.SMEM),
        "v": pl.BlockSpec(memory_space=pltpu.VMEM),
        "a": pl.BlockSpec(memory_space=pl.ANY),
    }
    return pl.pallas_call(
        kernel,
        in_specs=[kinds[k] for k in in_kinds],
        out_specs=[kinds[k] for k, _, _ in outs],
        out_shape=[jax.ShapeDtypeStruct(shape, dtype) for _, shape, dtype in outs],
        scratch_shapes=list(scratch),
        input_output_aliases=aliases or {},
        compiler_params=pltpu.CompilerParams(vmem_limit_bytes=24 * 1024 * 1024),
    )


def body(image_emb, text_emb, log_temp, bias):
    rows, width = image_emb.shape
    place = lax.axis_index(AXES)
    core = (place // 2) % 2
    role = jnp.stack([core, place % 2]).astype(jnp.int32)
    numbers = jnp.stack([jnp.exp(log_temp), bias])
    is_core_1 = core == 1
    other, image_late, text_late = together(jnp.where(is_core_1, image_emb, text_emb), image_emb, text_emb)
    main = jnp.where(is_core_1, text_late, image_late)

    swapped = send(other, SWAP)
    of_other = send(other, OF_OTHER)
    second = send(main, SECOND)
    near_main = send(main, NEAR_OF_MAIN)

    f32, low = jnp.float32, jnp.bfloat16
    whole, partial, both = (rows, width), (rows, LANES), (2, rows, width)
    lows, units, scales, accs, loss = call(
        first_kernel,
        "ssvvv",
        [("v", both, low), ("v", both, f32), ("v", (2, rows, 1), f32), ("v", both, f32), ("v", partial, f32)],
        [pltpu.VMEM((rows, rows), low), pltpu.VMEM(whole, low)],
    )(role, numbers, main, other, swapped)

    of_other, second, near_main, loss = together(of_other, second, near_main, loss)
    by_two = send(of_other, ON_BY_TWO)
    near_low, late_low = call(sent_kernel, "svvvv", [("v", whole, low), ("v", whole, low)])(
        role, lows, second, near_main, of_other
    )
    late_low = send(late_low, FAR_OR_ON_BY_ONE)
    swapped = send(near_low, SWAP)

    accs, loss = call(
        middle_kernel,
        "ssvvvvvv",
        [("v", both, f32), ("v", partial, f32)],
        [pltpu.VMEM(whole, low)],
        {6: 0, 7: 1},
    )(role, numbers, lows, second, near_low, swapped, accs, loss)

    copy_sems = pltpu.SemaphoreType.DMA((rows // CHUNK,))
    grad_image, grad_text, loss = call(
        early_kernel,
        "ssvvvvvvv",
        [("a", whole, f32), ("a", whole, f32), ("v", partial, f32)],
        [pltpu.VMEM(whole, low), pltpu.VMEM(whole, f32), copy_sems],
        {8: 2},
    )(role, numbers, lows, units, scales, accs, of_other, by_two, loss)
    grad_image, grad_text, row_loss = call(
        late_kernel,
        "ssvvvvvvaa",
        [("a", whole, f32), ("a", whole, f32), ("v", (1, rows), f32)],
        [pltpu.VMEM(partial, f32), pltpu.VMEM(whole, f32), copy_sems],
        {8: 0, 9: 1},
    )(role, numbers, lows, units, scales, accs, late_low, loss, grad_image, grad_text)
    return (row_loss.reshape(rows), grad_image, grad_text)


def solution(mesh):
    return jax.shard_map(
        body,
        mesh=mesh,
        in_specs=(P(AXES, None), P(AXES, None), P(), P()),
        out_specs=(P(AXES), P(AXES, None), P(AXES, None)),
        check_vma=False,
    )
```

profile of v0, /device:TPU:0, one launch (start us, length us, event | category | flops | bytes accessed | tf_op | source)
XLA Modules:
  0.0 95.9 jit_solution(18211219919744432916)
XLA Ops:
  0.7 1.6 %broadcast_select_fusion.1.other = bf16[512,1152]{1,0:T(8,128)(2,1)S(1)} fusion(bf16[512,1152]{1,0:T(8,128)(2,1)} %param.4, bf16[512,1152]{1,0:T(8,128)(2,1)} %param.5, pred[]{:T(512)S(6)} %eq.6), kind=kLoop, calls=%fused_computation.1 | loop fusion | flops 589824 | bytes 3538945 | tf_op jit(solution)/shard_map/jit(_where)/select_n | solution.py:256
  2.3 0.1 collective-permute-start
  2.4 0.3 copy-done.1
  2.6 0.1 broadcast_select_fusion.main
  2.8 10.5 %collective-permute-start.3 = (bf16[512,1152]{1,0:T(8,128)(2,1)S(1)}, bf16[512,1152]{1,0:T(8,128)(2,1)}, u32[]{:S(2)}, u32[]{:S(2)}) collective-permute-start(bf16[512,1152]{1,0:T(8,128)(2,1)S(1)} %broadcast_select_fusion.main), channel_id=1, source_target_pairs={{0,255},{3,4},{4,3},{7,8},{8,7},{11,12},{12,11},{15,16},{16,15},{1... | collective-permute-start | bytes 3538952 | tf_op jit(solution)/shard_map/ppermute | solution.py:34
  13.3 0.1 collective-permute-start.2
  13.4 1.5 %collective-permute-start.1 = (bf16[512,1152]{1,0:T(8,128)(2,1)S(1)}, bf16[512,1152]{1,0:T(8,128)(2,1)}, u32[]{:S(2)}, u32[]{:S(2)}) collective-permute-start(bf16[512,1152]{1,0:T(8,128)(2,1)S(1)} %broadcast_select_fusion.1.other), channel_id=1, source_target_pairs={{0,1},{1,4},{2,255},{3,2},{4,5},{5,8},{6,3},{7,6},{8,9},{9,12},{10... | collective-permute-start | bytes 3538952 | tf_op jit(solution)/shard_map/ppermute | solution.py:34
  16.2 0.1 pad_add_fusion.role_ref
  16.3 0.1 pad_maximum_fusion.numbers_ref
  16.3 0.0 collective-permute-done.swapped
  16.3 9.4 %shard_map.67 = (bf16[2,512,1152]{2,1,0:T(8,128)(2,1)S(1)}, f32[2,512,1152]{2,1,0:T(8,128)S(1)}, f32[2,512,1]{2,1,0:T(8,128)S(1)}, f32[2,512,1152]{2,1,0:T(8,128)S(1)}, f32[512,128]{1,0:T(8,128)S(1)}) custom-call(s32[2]{0:T(128)S(1)} %pad_add_fusion.role_ref, f32[2]{0:T(128)S(1)} %pad_maximum_fusion.numbers_ref, ...), custom_call_target="tpu_custom_call" | custom-call | tf_op jit(solution)/shard_map/pallas_call | solution.py:266
  25.8 13.5 %collective-permute-done.3.near_main = bf16[512,1152]{1,0:T(8,128)(2,1)} collective-permute-done((bf16[512,1152]{1,0:T(8,128)(2,1)S(1)}, bf16[512,1152]{1,0:T(8,128)(2,1)}, u32[]{:S(2)}, u32[]{:S(2)}) %collective-permute-start.3) | collective-permute-done | bytes 1179680 | tf_op jit(solution)/shard_map/ppermute | solution.py:34
  39.3 14.0 %collective-permute-done.2.second = bf16[512,1152]{1,0:T(8,128)(2,1)S(1)} collective-permute-done((bf16[512,1152]{1,0:T(8,128)(2,1)S(1)}, bf16[512,1152]{1,0:T(8,128)(2,1)S(1)}, u32[]{:S(2)}, u32[]{:S(2)}) %collective-permute-start.2) | collective-permute-done | bytes 1179680 | tf_op jit(solution)/shard_map/ppermute | solution.py:34
  53.3 0.0 collective-permute-done.1.of_other
  53.3 3.6 %shard_map.68 = (bf16[512,1152]{1,0:T(8,128)(2,1)S(1)}, bf16[512,1152]{1,0:T(8,128)(2,1)S(1)}) custom-call(s32[2]{0:T(128)S(1)} %pad_add_fusion.role_ref, bf16[2,512,1152]{2,1,0:T(8,128)(2,1)S(1)} %get-tuple-element.28.lows, bf16[512,1152]{1,0:T(8,128)(2,1)S(1)} %collective-permute-done.2.second, bf16[512,1152]{1,0:T(8,128)(2,1)} %collective-permute-done.3.near_main, ...), custom_call_target="tpu_custom_call" | custom-call | tf_op jit(solution)/shard_map/pallas_call | solution.py:275
  56.9 0.1 collective-permute-start.4
  57.0 7.3 %collective-permute-start.6 = (bf16[512,1152]{1,0:T(8,128)(2,1)}, bf16[512,1152]{1,0:T(8,128)(2,1)S(1)}, u32[]{:S(2)}, u32[]{:S(2)}) collective-permute-start(bf16[512,1152]{1,0:T(8,128)(2,1)} %collective-permute-done.1.of_other), channel_id=1, source_target_pairs={{0,254},{3,5},{4,2},{7,9},{8,6},{11,13},{12,10},{15,17},{16,14},{1... | collective-permute-start | bytes 3538952 | tf_op jit(solution)/shard_map/ppermute | solution.py:34
  64.3 0.3 collective-permute-start.5
  64.5 0.0 collective-permute-done.4.swapped
  64.5 8.1 %shard_map.69 = (f32[2,512,1152]{2,1,0:T(8,128)S(1)}, f32[512,128]{1,0:T(8,128)S(1)}) custom-call(s32[2]{0:T(128)S(1)} %pad_add_fusion.role_ref, f32[2]{0:T(128)S(1)} %pad_maximum_fusion.numbers_ref, bf16[2,512,1152]{2,1,0:T(8,128)(2,1)S(1)} %get-tuple-element.28.lows, ...), custom_call_target="tpu_custom_call", output_to_operand_aliasing={{0}: (6, {}), {1}: (7, {})} | custom-call | tf_op jit(solution)/shard_map/pallas_call | solution.py:281
  72.6 5.6 %collective-permute-done.6.by_two = bf16[512,1152]{1,0:T(8,128)(2,1)S(1)} collective-permute-done((bf16[512,1152]{1,0:T(8,128)(2,1)}, bf16[512,1152]{1,0:T(8,128)(2,1)S(1)}, u32[]{:S(2)}, u32[]{:S(2)}) %collective-permute-start.6) | collective-permute-done | bytes 1179680 | tf_op jit(solution)/shard_map/ppermute | solution.py:34
  78.2 5.9 %shard_map.70 = (f32[512,1152]{1,0:T(8,128)}, f32[512,1152]{1,0:T(8,128)}, f32[512,128]{1,0:T(8,128)S(1)}) custom-call(s32[2]{0:T(128)S(1)} %pad_add_fusion.role_ref, f32[2]{0:T(128)S(1)} %pad_maximum_fusion.numbers_ref, bf16[2,512,1152]{2,1,0:T(8,128)(2,1)S(1)} %get-tuple-element.28.lows, ...), custom_call_target="tpu_custom_call", output_to_operand_aliasing={{2}: (8, {})} | custom-call | tf_op jit(solution)/shard_map/pallas_call | solution.py:290
  84.1 6.7 %collective-permute-done.5.late_low = bf16[512,1152]{1,0:T(8,128)(2,1)S(1)} collective-permute-done((bf16[512,1152]{1,0:T(8,128)(2,1)S(1)}, bf16[512,1152]{1,0:T(8,128)(2,1)S(1)}, u32[]{:S(2)}, u32[]{:S(2)}) %collective-permute-start.5) | collective-permute-done | bytes 1179680 | tf_op jit(solution)/shard_map/ppermute | solution.py:34
  90.8 5.0 %shard_map.71 = (f32[512,1152]{1,0:T(8,128)}, f32[512,1152]{1,0:T(8,128)}, f32[1,512]{1,0:T(1,128)}) custom-call(s32[2]{0:T(128)S(1)} %pad_add_fusion.role_ref, f32[2]{0:T(128)S(1)} %pad_maximum_fusion.numbers_ref, bf16[2,512,1152]{2,1,0:T(8,128)(2,1)S(1)} %get-tuple-element.28.lows, ...), custom_call_target="tpu_custom_call", output_to_operand_aliasing={{0}: (8, {}), {1}: (9, {})} | custom-call | tf_op jit(solution)/shard_map/pallas_call | solution.py:297
  (3 shorter events, 0.0 us)
Async XLA Ops:
  0.7 1.7 %copy-start = (bf16[512,1152]{1,0:T(8,128)(2,1)S(1)}, bf16[512,1152]{1,0:T(8,128)(2,1)}, u32[]{:S(2)}) copy-start(bf16[512,1152]{1,0:T(8,128)(2,1)} %param.5) | copy-start | bytes 3538948
  0.7 2.0 %copy-start.1 = (bf16[512,1152]{1,0:T(8,128)(2,1)S(1)}, bf16[512,1152]{1,0:T(8,128)(2,1)}, u32[]{:S(2)}) copy-start(bf16[512,1152]{1,0:T(8,128)(2,1)} %param.4) | copy-start | bytes 3538948
  2.3 14.1 %collective-permute-start = (bf16[512,1152]{1,0:T(8,128)(2,1)S(1)}, bf16[512,1152]{1,0:T(8,128)(2,1)}, u32[]{:S(2)}, u32[]{:S(2)}) collective-permute-start(bf16[512,1152]{1,0:T(8,128)(2,1)S(1)} %broadcast_select_fusion.1.other), channel_id=1, source_target_pairs={{0,2},{1,3},{2,0},{3,1},{4,6},{5,7},{6,4},{7,5},{8,10},{9,11},{10,... | collective-permute-start | bytes 3538952 | tf_op jit(solution)/shard_map/ppermute | solution.py:34
  2.8 36.5 %collective-permute-start.3 = (bf16[512,1152]{1,0:T(8,128)(2,1)S(1)}, bf16[512,1152]{1,0:T(8,128)(2,1)}, u32[]{:S(2)}, u32[]{:S(2)}) collective-permute-start(bf16[512,1152]{1,0:T(8,128)(2,1)S(1)} %broadcast_select_fusion.main), channel_id=1, source_target_pairs={{0,255},{3,4},{4,3},{7,8},{8,7},{11,12},{12,11},{15,16},{16,15},{1... | collective-permute-start | bytes 3538952 | tf_op jit(solution)/shard_map/ppermute | solution.py:34
  13.3 40.0 %collective-permute-start.2 = (bf16[512,1152]{1,0:T(8,128)(2,1)S(1)}, bf16[512,1152]{1,0:T(8,128)(2,1)S(1)}, u32[]{:S(2)}, u32[]{:S(2)}) collective-permute-start(bf16[512,1152]{1,0:T(8,128)(2,1)S(1)} %broadcast_select_fusion.main), channel_id=1, source_target_pairs={{0,254},{1,255},{2,4},{3,5},{4,2},{5,3},{6,8},{7,9},{8,6},{9,7},{1... | collective-permute-start | bytes 3538952 | tf_op jit(solution)/shard_map/ppermute | solution.py:34
  13.4 39.9 %collective-permute-start.1 = (bf16[512,1152]{1,0:T(8,128)(2,1)S(1)}, bf16[512,1152]{1,0:T(8,128)(2,1)}, u32[]{:S(2)}, u32[]{:S(2)}) collective-permute-start(bf16[512,1152]{1,0:T(8,128)(2,1)S(1)} %broadcast_select_fusion.1.other), channel_id=1, source_target_pairs={{0,1},{1,4},{2,255},{3,2},{4,5},{5,8},{6,3},{7,6},{8,9},{9,12},{10... | collective-permute-start | bytes 3538952 | tf_op jit(solution)/shard_map/ppermute | solution.py:34
  56.9 7.7 %collective-permute-start.4 = (bf16[512,1152]{1,0:T(8,128)(2,1)S(1)}, bf16[512,1152]{1,0:T(8,128)(2,1)S(1)}, u32[]{:S(2)}, u32[]{:S(2)}) collective-permute-start(bf16[512,1152]{1,0:T(8,128)(2,1)S(1)} %get-tuple-element.35.near_low), channel_id=1, source_target_pairs={{0,2},{1,3},{2,0},{3,1},{4,6},{5,7},{6,4},{7,5},{8,10},{9,11},{10,... | collective-permute-start | bytes 3538952 | tf_op jit(solution)/shard_map/ppermute | solution.py:34
  57.0 21.2 %collective-permute-start.6 = (bf16[512,1152]{1,0:T(8,128)(2,1)}, bf16[512,1152]{1,0:T(8,128)(2,1)S(1)}, u32[]{:S(2)}, u32[]{:S(2)}) collective-permute-start(bf16[512,1152]{1,0:T(8,128)(2,1)} %collective-permute-done.1.of_other), channel_id=1, source_target_pairs={{0,254},{3,5},{4,2},{7,9},{8,6},{11,13},{12,10},{15,17},{16,14},{1... | collective-permute-start | bytes 3538952 | tf_op jit(solution)/shard_map/ppermute | solution.py:34
  64.3 26.6 %collective-permute-start.5 = (bf16[512,1152]{1,0:T(8,128)(2,1)S(1)}, bf16[512,1152]{1,0:T(8,128)(2,1)S(1)}, u32[]{:S(2)}, u32[]{:S(2)}) collective-permute-start(bf16[512,1152]{1,0:T(8,128)(2,1)S(1)} %get-tuple-element.39), channel_id=1, source_target_pairs={{0,255},{1,254},{2,5},{3,4},{4,3},{5,2},{6,9},{7,8},{8,7},{9,6},{1... | collective-permute-start | bytes 3538952 | tf_op jit(solution)/shard_map/ppermute | solution.py:34
where the time goes:
time: 96.2 us; the launch traced here: 95.9 us
  waiting for transfers between devices  39.8 us (41%)
  Pallas kernels  31.9 us (33%)
  starting transfers between devices  19.8 us (21%)
  between operations  2.28 us (2%)
  other arithmetic  1.85 us (2%)
    ppermute x7, waiting for transfers between devices, send(): return lax.ppermute(x, AXES, pairs())  39.8 us
    ppermute x7, starting transfers between devices, send(): return lax.ppermute(x, AXES, pairs())  19.8 us
    pallas_call x1, Pallas kernels, body(): call(first_kernel, 'ssvvv', [('v', both, low), ('v', both, f32), ('v', (2...  9.42 us
    pallas_call x1, Pallas kernels, body(): call(middle_kernel, 'ssvvvvvv', [('v', both, f32), ('v', partial, f32)],...  8.07 us
    pallas_call x1, Pallas kernels, body(): call(early_kernel, 'ssvvvvvvv', [('a', whole, f32), ('a', whole, f32), ('...  5.94 us
    pallas_call x1, Pallas kernels, body(): call(late_kernel, 'ssvvvvvvaa', [('a', whole, f32), ('a', whole, f32), ('...  4.95 us
    pallas_call x1, Pallas kernels, body(): call(sent_kernel, 'svvvv', [('v', whole, low), ('v', whole, low)])  3.56 us
  transfers between devices with their start and end apart: 7, of which 4 were waited for; matrix products, arithmetic and copies ran while one was open for 0% of the time, Pallas kernels for 24%

commit v1 on v0

--- a/solution.py
+++ b/solution.py
@@ -9,8 +9,8 @@
 
 AXES = ("blk", "rep")
 EPSILON = 1e-06
-CHUNK = 256
-STRIP = 64
+COLUMNS = 512
+STRIP = 512
 LANES = 128
 
 
@@ -38,14 +38,6 @@
     return lax.optimization_barrier(arrays)
 
 
-def strips(count, step):
-    def at(k, carry):
-        step(pl.ds(pl.multiple_of(k * STRIP, STRIP), STRIP))
-        return carry
-
-    lax.fori_loop(0, count // STRIP, at, 0)
-
-
 def unit_of(raw_ref, rows):
     values = raw_ref[rows, :].astype(jnp.float32)
     scale = lax.rsqrt(jnp.sum(values * values, axis=-1, keepdims=True) + EPSILON)
@@ -53,10 +45,7 @@
 
 
 def lower(raw_ref, low_ref):
-    def step(rows):
-        low_ref[rows, :] = unit_of(raw_ref, rows)[0].astype(jnp.bfloat16)
-
-    strips(raw_ref.shape[0], step)
+    low_ref[...] = unit_of(raw_ref, slice(None))[0].astype(jnp.bfloat16)
 
 
 def lower_one_of(chosen, this_ref, that_ref, low_ref):
@@ -89,20 +78,22 @@
     )
 
 
-def partner_grad(numbers_ref, own_ref, partner_ref, loss_from, loss_to, counts, rows):
+def partner_grad(numbers_ref, own_ref, partner_ref, loss_from, loss_to, counts):
     temper, bias = numbers_ref[0], numbers_ref[1]
-    logits = temper * product(own_ref[rows, :], partner_ref[...], 1, 1) + bias
-    losses, chances = terms(logits)
-    loss_to[rows, :] = loss_from[rows, :] + counts * folded(losses)
-    weights = (chances * temper).astype(jnp.bfloat16)
-    return product(weights, partner_ref[...], 1, 0)
+    loss, grad = 0.0, 0.0
+    for at in range(0, partner_ref.shape[0], COLUMNS):
+        partner = partner_ref[pl.ds(at, COLUMNS), :]
+        losses, chances = terms(temper * product(own_ref[...], partner, 1, 1) + bias)
+        loss = loss + folded(losses)
+        grad = grad + product((chances * temper).astype(jnp.bfloat16), partner, 1, 0)
+    loss_to[...] = loss_from[...] + counts * loss
+    return grad
 
 
 def pair(numbers_ref, own_ref, partner_ref, acc_from, acc_to, loss_from, loss_to, counts):
-    for at in range(0, own_ref.shape[0], CHUNK):
-        rows = pl.ds(at, CHUNK)
-        grad = partner_grad(numbers_ref, own_ref, partner_ref, loss_from, loss_to, counts, rows)
-        acc_to[rows, :] = acc_from[rows, :] + grad
+    acc_to[...] = acc_from[...] + partner_grad(
+        numbers_ref, own_ref, partner_ref, loss_from, loss_to, counts
+    )
 
 
 def first_kernel(
@@ -113,26 +104,20 @@
     core = role_ref[0]
     count = main.shape[0]
     for side, raw in enumerate((main, other)):
-
-        def step(rows, side=side, raw=raw):
-            unit, scale = unit_of(raw, rows)
-            units[side, rows, :] = unit
-            scales[side, rows, :] = scale
-            lows[side, rows, :] = unit.astype(jnp.bfloat16)
-
-        strips(count, step)
+        unit, scale = unit_of(raw, slice(None))
+        units[side] = unit
+        scales[side] = scale
+        lows[side] = unit.astype(jnp.bfloat16)
     image_low, text_low = lows.at[core], lows.at[1 - core]
-    for at in range(0, count, CHUNK):
-        rows = pl.ds(at, CHUNK)
-        logits = temper * product(image_low[rows, :], text_low[...], 1, 1) + bias
-        row = lax.broadcasted_iota(jnp.int32, (CHUNK, count), 0) + at
-        column = lax.broadcasted_iota(jnp.int32, (CHUNK, count), 1)
-        same = row == column
-        losses, chances = terms(jnp.where(same, -logits, logits))
-        loss_ref[rows, :] = folded(losses)
-        weights = (jnp.where(same, -chances, chances) * temper).astype(jnp.bfloat16)
-        weights_ref[rows, :] = weights
-        accs[core, rows, :] = product(weights, text_low[...], 1, 0)
+    logits = temper * product(image_low[...], text_low[...], 1, 1) + bias
+    row = lax.broadcasted_iota(jnp.int32, (count, count), 0)
+    column = lax.broadcasted_iota(jnp.int32, (count, count), 1)
+    same = row == column
+    losses, chances = terms(jnp.where(same, -logits, logits))
+    loss_ref[...] = folded(losses)
+    weights = (jnp.where(same, -chances, chances) * temper).astype(jnp.bfloat16)
+    weights_ref[...] = weights
+    accs[core] = product(weights, text_low[...], 1, 0)
     accs[1 - core] = product(weights_ref[...], image_low[...], 0, 0)
     lower(swapped, low_ref)
     pair(
@@ -171,17 +156,16 @@
     counts = (side == core).astype(jnp.float32)
     own_low = lows.at[side]
 
-    parts = done_ref.shape[0] // CHUNK
+    parts = done_ref.shape[0] // STRIP
 
     def copy(k, out):
-        rows = pl.ds(k * CHUNK, CHUNK)
+        rows = pl.ds(k * STRIP, STRIP)
         return pltpu.make_async_copy(done_ref.at[rows, :], out.at[rows, :], sems.at[k])
 
+    done_ref[...] = accs[side] + partner_grad(numbers_ref, own_low, partner_ref, loss_from, loss_to, counts)
     for k in range(parts):
-        rows = pl.ds(k * CHUNK, CHUNK)
-        grad = accs[side, rows, :] + partner_grad(
-            numbers_ref, own_low, partner_ref, loss_from, loss_to, counts, rows
-        )
+        rows = pl.ds(k * STRIP, STRIP)
+        grad = done_ref[rows, :]
         unit = units[side, rows, :]
         along = jnp.sum(unit * grad, axis=-1, keepdims=True)
         done_ref[rows, :] = scales[side, rows, :] * (grad - unit * along)
@@ -270,7 +254,7 @@
         [pltpu.VMEM((rows, rows), low), pltpu.VMEM(whole, low)],
     )(role, numbers, main, other, swapped)
 
-    of_other, second, near_main, loss = together(of_other, second, near_main, loss)
+    near_main, second, of_other, loss = together(near_main, second, of_other, loss)
     by_two = send(of_other, ON_BY_TWO)
     near_low, late_low = call(sent_kernel, "svvvv", [("v", whole, low), ("v", whole, low)])(
         role, lows, second, near_main, of_other
@@ -286,7 +270,7 @@
         {6: 0, 7: 1},
     )(role, numbers, lows, second, near_low, swapped, accs, loss)
 
-    copy_sems = pltpu.SemaphoreType.DMA((rows // CHUNK,))
+    copy_sems = pltpu.SemaphoreType.DMA((rows // STRIP,))
     grad_image, grad_text, loss = call(
         early_kernel,
         "ssvvvvvvv",

time: 96.2 us -> 106 us (1.10)
  waiting for transfers between devices: 39.8 us -> 52.1 us
  Pallas kernels: 31.9 us -> 27.1 us
  starting transfers between devices: 19.8 us -> 21.9 us
    ppermute x7, waiting for transfers between devices: 39.8 us -> 52.1 us  [send(): return lax.ppermute(x, AXES, pairs())]
    pallas_call x1, Pallas kernels: 9.42 us -> 7.11 us  [body(): call(first_kernel, 'ssvvv', [('v', both, low), ('v', both, f32), ('v', (2...]
    ppermute x7, starting transfers between devices: 19.8 us -> 21.9 us  [send(): return lax.ppermute(x, AXES, pairs())]
    pallas_call x1, Pallas kernels: 8.07 us -> 6.8 us  [body(): call(middle_kernel, 'ssvvvvvv', [('v', both, f32), ('v', partial, f32)],...]
    pallas_call x1, Pallas kernels: 3.56 us -> 2.38 us  [body(): call(sent_kernel, 'svvvv', [('v', whole, low), ('v', whole, low)])]
  transfers between devices with their start and end apart: 7 -> 7, of which waited for: 4 -> 4; matrix products, arithmetic and copies ran while one was open for 0% -> 0% of each run, Pallas kernels for 24% -> 18%
where the time goes in v1:
time: 106 us; the launch traced here: 105 us
  waiting for transfers between devices  52.1 us (49%)
  Pallas kernels  27.1 us (26%)
  starting transfers between devices  21.9 us (21%)
  between operations  2.25 us (2%)
  other arithmetic  1.85 us (2%)
    ppermute x7, waiting for transfers between devices, send(): return lax.ppermute(x, AXES, pairs())  52.1 us
    ppermute x7, starting transfers between devices, send(): return lax.ppermute(x, AXES, pairs())  21.9 us
    pallas_call x1, Pallas kernels, body(): call(first_kernel, 'ssvvv', [('v', both, low), ('v', both, f32), ('v', (2...  7.11 us
    pallas_call x1, Pallas kernels, body(): call(middle_kernel, 'ssvvvvvv', [('v', both, f32), ('v', partial, f32)],...  6.8 us
    pallas_call x1, Pallas kernels, body(): call(early_kernel, 'ssvvvvvvv', [('a', whole, f32), ('a', whole, f32), ('...  5.56 us
    pallas_call x1, Pallas kernels, body(): call(late_kernel, 'ssvvvvvvaa', [('a', whole, f32), ('a', whole, f32), ('...  5.21 us
    pallas_call x1, Pallas kernels, body(): call(sent_kernel, 'svvvv', [('v', whole, low), ('v', whole, low)])  2.38 us
  transfers between devices with their start and end apart: 7, of which 4 were waited for; matrix products, arithmetic and copies ran while one was open for 0% of the time, Pallas kernels for 18%

profile of v1, /device:TPU:0, one launch (start us, length us, event | category | flops | bytes accessed | tf_op | source)
XLA Modules:
  0.0 105.4 jit_solution(18417764595657882845)
XLA Ops:
  0.7 1.6 %broadcast_select_fusion.1.other = bf16[512,1152]{1,0:T(8,128)(2,1)S(1)} fusion(bf16[512,1152]{1,0:T(8,128)(2,1)} %param.4, bf16[512,1152]{1,0:T(8,128)(2,1)} %param.5, pred[]{:T(512)S(6)} %eq.6), kind=kLoop, calls=%fused_computation.1 | loop fusion | flops 589824 | bytes 3538945 | tf_op jit(solution)/shard_map/jit(_where)/select_n | solution.py:240
  2.3 0.1 collective-permute-start
  2.4 0.3 copy-done.1
  2.6 0.1 broadcast_select_fusion.main
  2.8 7.2 %collective-permute-start.2 = (bf16[512,1152]{1,0:T(8,128)(2,1)S(1)}, bf16[512,1152]{1,0:T(8,128)(2,1)S(1)}, u32[]{:S(2)}, u32[]{:S(2)}) collective-permute-start(bf16[512,1152]{1,0:T(8,128)(2,1)S(1)} %broadcast_select_fusion.main), channel_id=1, source_target_pairs={{0,254},{1,255},{2,4},{3,5},{4,2},{5,3},{6,8},{7,9},{8,6},{9,7},{1... | collective-permute-start | bytes 3538952 | tf_op jit(solution)/shard_map/ppermute | solution.py:34
  10.0 3.4 %collective-permute-start.1 = (bf16[512,1152]{1,0:T(8,128)(2,1)S(1)}, bf16[512,1152]{1,0:T(8,128)(2,1)}, u32[]{:S(2)}, u32[]{:S(2)}) collective-permute-start(bf16[512,1152]{1,0:T(8,128)(2,1)S(1)} %broadcast_select_fusion.main), channel_id=1, source_target_pairs={{0,255},{3,4},{4,3},{7,8},{8,7},{11,12},{12,11},{15,16},{16,15},{1... | collective-permute-start | bytes 3538952 | tf_op jit(solution)/shard_map/ppermute | solution.py:34
  13.4 1.2 %collective-permute-start.3 = (bf16[512,1152]{1,0:T(8,128)(2,1)S(1)}, bf16[512,1152]{1,0:T(8,128)(2,1)}, u32[]{:S(2)}, u32[]{:S(2)}) collective-permute-start(bf16[512,1152]{1,0:T(8,128)(2,1)S(1)} %broadcast_select_fusion.1.other), channel_id=1, source_target_pairs={{0,1},{1,4},{2,255},{3,2},{4,5},{5,8},{6,3},{7,6},{8,9},{9,12},{10... | collective-permute-start | bytes 3538952 | tf_op jit(solution)/shard_map/ppermute | solution.py:34
  15.9 0.1 pad_add_fusion.role_ref
  16.0 0.1 pad_maximum_fusion.numbers_ref
  16.1 0.0 collective-permute-done.swapped
  16.1 7.1 %shard_map.67 = (bf16[2,512,1152]{2,1,0:T(8,128)(2,1)S(1)}, f32[2,512,1152]{2,1,0:T(8,128)S(1)}, f32[2,512,1]{2,1,0:T(8,128)S(1)}, f32[2,512,1152]{2,1,0:T(8,128)S(1)}, f32[512,128]{1,0:T(8,128)S(1)}) custom-call(s32[2]{0:T(128)S(1)} %pad_add_fusion.role_ref, f32[2]{0:T(128)S(1)} %pad_maximum_fusion.numbers_ref, ...), custom_call_target="tpu_custom_call" | custom-call | tf_op jit(solution)/shard_map/pallas_call | solution.py:250
  23.2 4.5 %collective-permute-done.2.second = bf16[512,1152]{1,0:T(8,128)(2,1)S(1)} collective-permute-done((bf16[512,1152]{1,0:T(8,128)(2,1)S(1)}, bf16[512,1152]{1,0:T(8,128)(2,1)S(1)}, u32[]{:S(2)}, u32[]{:S(2)}) %collective-permute-start.2) | collective-permute-done | bytes 1179680 | tf_op jit(solution)/shard_map/ppermute | solution.py:34
  27.7 33.6 %collective-permute-done.1.near_main = bf16[512,1152]{1,0:T(8,128)(2,1)} collective-permute-done((bf16[512,1152]{1,0:T(8,128)(2,1)S(1)}, bf16[512,1152]{1,0:T(8,128)(2,1)}, u32[]{:S(2)}, u32[]{:S(2)}) %collective-permute-start.1) | collective-permute-done | bytes 1179680 | tf_op jit(solution)/shard_map/ppermute | solution.py:34
  61.3 0.0 collective-permute-done.3.of_other
  61.3 2.4 %shard_map.68 = (bf16[512,1152]{1,0:T(8,128)(2,1)S(1)}, bf16[512,1152]{1,0:T(8,128)(2,1)S(1)}) custom-call(s32[2]{0:T(128)S(1)} %pad_add_fusion.role_ref, bf16[2,512,1152]{2,1,0:T(8,128)(2,1)S(1)} %get-tuple-element.28.lows, bf16[512,1152]{1,0:T(8,128)(2,1)S(1)} %collective-permute-done.2.second, bf16[512,1152]{1,0:T(8,128)(2,1)} %collective-permute-done.1.near_main, ...), custom_call_target="tpu_custom_call" | custom-call | tf_op jit(solution)/shard_map/pallas_call | solution.py:259
  63.7 1.7 %collective-permute-start.4 = (bf16[512,1152]{1,0:T(8,128)(2,1)S(1)}, bf16[512,1152]{1,0:T(8,128)(2,1)S(1)}, u32[]{:S(2)}, u32[]{:S(2)}) collective-permute-start(bf16[512,1152]{1,0:T(8,128)(2,1)S(1)} %get-tuple-element.35.near_low), channel_id=1, source_target_pairs={{0,2},{1,3},{2,0},{3,1},{4,6},{5,7},{6,4},{7,5},{8,10},{9,11},{10,... | collective-permute-start | bytes 3538952 | tf_op jit(solution)/shard_map/ppermute | solution.py:34
  65.4 5.6 %collective-permute-start.6 = (bf16[512,1152]{1,0:T(8,128)(2,1)}, bf16[512,1152]{1,0:T(8,128)(2,1)S(1)}, u32[]{:S(2)}, u32[]{:S(2)}) collective-permute-start(bf16[512,1152]{1,0:T(8,128)(2,1)} %collective-permute-done.3.of_other), channel_id=1, source_target_pairs={{0,254},{3,5},{4,2},{7,9},{8,6},{11,13},{12,10},{15,17},{16,14},{1... | collective-permute-start | bytes 3538952 | tf_op jit(solution)/shard_map/ppermute | solution.py:34
  71.0 2.7 %collective-permute-start.5 = (bf16[512,1152]{1,0:T(8,128)(2,1)S(1)}, bf16[512,1152]{1,0:T(8,128)(2,1)S(1)}, u32[]{:S(2)}, u32[]{:S(2)}) collective-permute-start(bf16[512,1152]{1,0:T(8,128)(2,1)S(1)} %get-tuple-element.39), channel_id=1, source_target_pairs={{0,255},{1,254},{2,5},{3,4},{4,3},{5,2},{6,9},{7,8},{8,7},{9,6},{1... | collective-permute-start | bytes 3538952 | tf_op jit(solution)/shard_map/ppermute | solution.py:34
  73.7 0.0 collective-permute-done.4.swapped
  73.7 6.8 %shard_map.69 = (f32[2,512,1152]{2,1,0:T(8,128)S(1)}, f32[512,128]{1,0:T(8,128)S(1)}) custom-call(s32[2]{0:T(128)S(1)} %pad_add_fusion.role_ref, f32[2]{0:T(128)S(1)} %pad_maximum_fusion.numbers_ref, bf16[2,512,1152]{2,1,0:T(8,128)(2,1)S(1)} %get-tuple-element.28.lows, ...), custom_call_target="tpu_custom_call", output_to_operand_aliasing={{0}: (6, {}), {1}: (7, {})} | custom-call | tf_op jit(solution)/shard_map/pallas_call | solution.py:265
  80.5 4.5 %collective-permute-done.6.by_two = bf16[512,1152]{1,0:T(8,128)(2,1)S(1)} collective-permute-done((bf16[512,1152]{1,0:T(8,128)(2,1)}, bf16[512,1152]{1,0:T(8,128)(2,1)S(1)}, u32[]{:S(2)}, u32[]{:S(2)}) %collective-permute-start.6) | collective-permute-done | bytes 1179680 | tf_op jit(solution)/shard_map/ppermute | solution.py:34
  84.9 5.6 %shard_map.70 = (f32[512,1152]{1,0:T(8,128)}, f32[512,1152]{1,0:T(8,128)}, f32[512,128]{1,0:T(8,128)S(1)}) custom-call(s32[2]{0:T(128)S(1)} %pad_add_fusion.role_ref, f32[2]{0:T(128)S(1)} %pad_maximum_fusion.numbers_ref, bf16[2,512,1152]{2,1,0:T(8,128)(2,1)S(1)} %get-tuple-element.28.lows, ...), custom_call_target="tpu_custom_call", output_to_operand_aliasing={{2}: (8, {})} | custom-call | tf_op jit(solution)/shard_map/pallas_call | solution.py:274
  90.5 9.5 %collective-permute-done.5.late_low = bf16[512,1152]{1,0:T(8,128)(2,1)S(1)} collective-permute-done((bf16[512,1152]{1,0:T(8,128)(2,1)S(1)}, bf16[512,1152]{1,0:T(8,128)(2,1)S(1)}, u32[]{:S(2)}, u32[]{:S(2)}) %collective-permute-start.5) | collective-permute-done | bytes 1179680 | tf_op jit(solution)/shard_map/ppermute | solution.py:34
  100.0 5.2 %shard_map.71 = (f32[512,1152]{1,0:T(8,128)}, f32[512,1152]{1,0:T(8,128)}, f32[1,512]{1,0:T(1,128)}) custom-call(s32[2]{0:T(128)S(1)} %pad_add_fusion.role_ref, f32[2]{0:T(128)S(1)} %pad_maximum_fusion.numbers_ref, bf16[2,512,1152]{2,1,0:T(8,128)(2,1)S(1)} %get-tuple-element.28.lows, ...), custom_call_target="tpu_custom_call", output_to_operand_aliasing={{0}: (8, {}), {1}: (9, {})} | custom-call | tf_op jit(solution)/shard_map/pallas_call | solution.py:281
  (3 shorter events, 0.0 us)
Async XLA Ops:
  0.7 1.7 %copy-start = (bf16[512,1152]{1,0:T(8,128)(2,1)S(1)}, bf16[512,1152]{1,0:T(8,128)(2,1)}, u32[]{:S(2)}) copy-start(bf16[512,1152]{1,0:T(8,128)(2,1)} %param.5) | copy-start | bytes 3538948
  0.7 2.0 %copy-start.1 = (bf16[512,1152]{1,0:T(8,128)(2,1)S(1)}, bf16[512,1152]{1,0:T(8,128)(2,1)}, u32[]{:S(2)}) copy-start(bf16[512,1152]{1,0:T(8,128)(2,1)} %param.4) | copy-start | bytes 3538948
  2.3 13.8 %collective-permute-start = (bf16[512,1152]{1,0:T(8,128)(2,1)S(1)}, bf16[512,1152]{1,0:T(8,128)(2,1)}, u32[]{:S(2)}, u32[]{:S(2)}) collective-permute-start(bf16[512,1152]{1,0:T(8,128)(2,1)S(1)} %broadcast_select_fusion.1.other), channel_id=1, source_target_pairs={{0,2},{1,3},{2,0},{3,1},{4,6},{5,7},{6,4},{7,5},{8,10},{9,11},{10,... | collective-permute-start | bytes 3538952 | tf_op jit(solution)/shard_map/ppermute | solution.py:34
  2.8 24.9 %collective-permute-start.2 = (bf16[512,1152]{1,0:T(8,128)(2,1)S(1)}, bf16[512,1152]{1,0:T(8,128)(2,1)S(1)}, u32[]{:S(2)}, u32[]{:S(2)}) collective-permute-start(bf16[512,1152]{1,0:T(8,128)(2,1)S(1)} %broadcast_select_fusion.main), channel_id=1, source_target_pairs={{0,254},{1,255},{2,4},{3,5},{4,2},{5,3},{6,8},{7,9},{8,6},{9,7},{1... | collective-permute-start | bytes 3538952 | tf_op jit(solution)/shard_map/ppermute | solution.py:34
  10.0 51.3 %collective-permute-start.1 = (bf16[512,1152]{1,0:T(8,128)(2,1)S(1)}, bf16[512,1152]{1,0:T(8,128)(2,1)}, u32[]{:S(2)}, u32[]{:S(2)}) collective-permute-start(bf16[512,1152]{1,0:T(8,128)(2,1)S(1)} %broadcast_select_fusion.main), channel_id=1, source_target_pairs={{0,255},{3,4},{4,3},{7,8},{8,7},{11,12},{12,11},{15,16},{16,15},{1... | collective-permute-start | bytes 3538952 | tf_op jit(solution)/shard_map/ppermute | solution.py:34
  13.4 47.9 %collective-permute-start.3 = (bf16[512,1152]{1,0:T(8,128)(2,1)S(1)}, bf16[512,1152]{1,0:T(8,128)(2,1)}, u32[]{:S(2)}, u32[]{:S(2)}) collective-permute-start(bf16[512,1152]{1,0:T(8,128)(2,1)S(1)} %broadcast_select_fusion.1.other), channel_id=1, source_target_pairs={{0,1},{1,4},{2,255},{3,2},{4,5},{5,8},{6,3},{7,6},{8,9},{9,12},{10... | collective-permute-start | bytes 3538952 | tf_op jit(solution)/shard_map/ppermute | solution.py:34
  63.7 10.0 %collective-permute-start.4 = (bf16[512,1152]{1,0:T(8,128)(2,1)S(1)}, bf16[512,1152]{1,0:T(8,128)(2,1)S(1)}, u32[]{:S(2)}, u32[]{:S(2)}) collective-permute-start(bf16[512,1152]{1,0:T(8,128)(2,1)S(1)} %get-tuple-element.35.near_low), channel_id=1, source_target_pairs={{0,2},{1,3},{2,0},{3,1},{4,6},{5,7},{6,4},{7,5},{8,10},{9,11},{10,... | collective-permute-start | bytes 3538952 | tf_op jit(solution)/shard_map/ppermute | solution.py:34
  65.4 19.5 %collective-permute-start.6 = (bf16[512,1152]{1,0:T(8,128)(2,1)}, bf16[512,1152]{1,0:T(8,128)(2,1)S(1)}, u32[]{:S(2)}, u32[]{:S(2)}) collective-permute-start(bf16[512,1152]{1,0:T(8,128)(2,1)} %collective-permute-done.3.of_other), channel_id=1, source_target_pairs={{0,254},{3,5},{4,2},{7,9},{8,6},{11,13},{12,10},{15,17},{16,14},{1... | collective-permute-start | bytes 3538952 | tf_op jit(solution)/shard_map/ppermute | solution.py:34
  71.0 29.0 %collective-permute-start.5 = (bf16[512,1152]{1,0:T(8,128)(2,1)S(1)}, bf16[512,1152]{1,0:T(8,128)(2,1)S(1)}, u32[]{:S(2)}, u32[]{:S(2)}) collective-permute-start(bf16[512,1152]{1,0:T(8,128)(2,1)S(1)} %get-tuple-element.39), channel_id=1, source_target_pairs={{0,255},{1,254},{2,5},{3,4},{4,3},{5,2},{6,9},{7,8},{8,7},{9,6},{1... | collective-permute-start | bytes 3538952 | tf_op jit(solution)/shard_map/ppermute | solution.py:34

commit v2 on v1

--- a/solution.py
+++ b/solution.py
@@ -254,7 +254,7 @@
         [pltpu.VMEM((rows, rows), low), pltpu.VMEM(whole, low)],
     )(role, numbers, main, other, swapped)
 
-    near_main, second, of_other, loss = together(near_main, second, of_other, loss)
+    of_other, second, near_main, loss = together(of_other, second, near_main, loss)
     by_two = send(of_other, ON_BY_TWO)
     near_low, late_low = call(sent_kernel, "svvvv", [("v", whole, low), ("v", whole, low)])(
         role, lows, second, near_main, of_other

time: 106 us -> 95.8 us (0.904)
  waiting for transfers between devices: 52.1 us -> 43.7 us
  starting transfers between devices: 21.9 us -> 20.4 us
    ppermute x7, waiting for transfers between devices: 52.1 us -> 43.7 us  [send(): return lax.ppermute(x, AXES, pairs())]
    ppermute x7, starting transfers between devices: 21.9 us -> 20.4 us  [send(): return lax.ppermute(x, AXES, pairs())]
  transfers between devices with their start and end apart: 7 -> 7, of which waited for: 4 -> 4; matrix products, arithmetic and copies ran while one was open for 0% -> 0% of each run, Pallas kernels for 18% -> 20%
where the time goes in v2:
time: 95.8 us; the launch traced here: 95.6 us
  waiting for transfers between devices  43.7 us (46%)
  Pallas kernels  27.1 us (28%)
  starting transfers between devices  20.4 us (21%)
  between operations  2.28 us (2%)
  other arithmetic  1.85 us (2%)
    ppermute x7, waiting for transfers between devices, send(): return lax.ppermute(x, AXES, pairs())  43.7 us
    ppermute x7, starting transfers between devices, send(): return lax.ppermute(x, AXES, pairs())  20.4 us
    pallas_call x1, Pallas kernels, body(): call(first_kernel, 'ssvvv', [('v', both, low), ('v', both, f32), ('v', (2...  7.11 us
    pallas_call x1, Pallas kernels, body(): call(middle_kernel, 'ssvvvvvv', [('v', both, f32), ('v', partial, f32)],...  6.8 us
    pallas_call x1, Pallas kernels, body(): call(early_kernel, 'ssvvvvvvv', [('a', whole, f32), ('a', whole, f32), ('...  5.56 us
    pallas_call x1, Pallas kernels, body(): call(late_kernel, 'ssvvvvvvaa', [('a', whole, f32), ('a', whole, f32), ('...  5.21 us
    pallas_call x1, Pallas kernels, body(): call(sent_kernel, 'svvvv', [('v', whole, low), ('v', whole, low)])  2.38 us
  transfers between devices with their start and end apart: 7, of which 4 were waited for; matrix products, arithmetic and copies ran while one was open for 0% of the time, Pallas kernels for 20%

profile of v2, /device:TPU:0, one launch (start us, length us, event | category | flops | bytes accessed | tf_op | source)
XLA Modules:
  0.0 95.6 jit_solution(956856629907337112)
XLA Ops:
  0.7 1.6 %broadcast_select_fusion.1.other = bf16[512,1152]{1,0:T(8,128)(2,1)S(1)} fusion(bf16[512,1152]{1,0:T(8,128)(2,1)} %param.4, bf16[512,1152]{1,0:T(8,128)(2,1)} %param.5, pred[]{:T(512)S(6)} %eq.6), kind=kLoop, calls=%fused_computation.1 | loop fusion | flops 589824 | bytes 3538945 | tf_op jit(solution)/shard_map/jit(_where)/select_n | solution.py:240
  2.3 0.1 collective-permute-start
  2.4 0.3 copy-done.1
  2.6 0.1 broadcast_select_fusion.main
  2.8 10.5 %collective-permute-start.3 = (bf16[512,1152]{1,0:T(8,128)(2,1)S(1)}, bf16[512,1152]{1,0:T(8,128)(2,1)}, u32[]{:S(2)}, u32[]{:S(2)}) collective-permute-start(bf16[512,1152]{1,0:T(8,128)(2,1)S(1)} %broadcast_select_fusion.main), channel_id=1, source_target_pairs={{0,255},{3,4},{4,3},{7,8},{8,7},{11,12},{12,11},{15,16},{16,15},{1... | collective-permute-start | bytes 3538952 | tf_op jit(solution)/shard_map/ppermute | solution.py:34
  13.3 0.1 collective-permute-start.2
  13.4 1.5 %collective-permute-start.1 = (bf16[512,1152]{1,0:T(8,128)(2,1)S(1)}, bf16[512,1152]{1,0:T(8,128)(2,1)}, u32[]{:S(2)}, u32[]{:S(2)}) collective-permute-start(bf16[512,1152]{1,0:T(8,128)(2,1)S(1)} %broadcast_select_fusion.1.other), channel_id=1, source_target_pairs={{0,1},{1,4},{2,255},{3,2},{4,5},{5,8},{6,3},{7,6},{8,9},{9,12},{10... | collective-permute-start | bytes 3538952 | tf_op jit(solution)/shard_map/ppermute | solution.py:34
  16.2 0.1 pad_add_fusion.role_ref
  16.3 0.1 pad_maximum_fusion.numbers_ref
  16.3 0.0 collective-permute-done.swapped
  16.3 7.1 %shard_map.67 = (bf16[2,512,1152]{2,1,0:T(8,128)(2,1)S(1)}, f32[2,512,1152]{2,1,0:T(8,128)S(1)}, f32[2,512,1]{2,1,0:T(8,128)S(1)}, f32[2,512,1152]{2,1,0:T(8,128)S(1)}, f32[512,128]{1,0:T(8,128)S(1)}) custom-call(s32[2]{0:T(128)S(1)} %pad_add_fusion.role_ref, f32[2]{0:T(128)S(1)} %pad_maximum_fusion.numbers_ref, ...), custom_call_target="tpu_custom_call" | custom-call | tf_op jit(solution)/shard_map/pallas_call | solution.py:250
  23.5 15.8 %collective-permute-done.3.near_main = bf16[512,1152]{1,0:T(8,128)(2,1)} collective-permute-done((bf16[512,1152]{1,0:T(8,128)(2,1)S(1)}, bf16[512,1152]{1,0:T(8,128)(2,1)}, u32[]{:S(2)}, u32[]{:S(2)}) %collective-permute-start.3) | collective-permute-done | bytes 1179680 | tf_op jit(solution)/shard_map/ppermute | solution.py:34
  39.3 14.0 %collective-permute-done.2.second = bf16[512,1152]{1,0:T(8,128)(2,1)S(1)} collective-permute-done((bf16[512,1152]{1,0:T(8,128)(2,1)S(1)}, bf16[512,1152]{1,0:T(8,128)(2,1)S(1)}, u32[]{:S(2)}, u32[]{:S(2)}) %collective-permute-start.2) | collective-permute-done | bytes 1179680 | tf_op jit(solution)/shard_map/ppermute | solution.py:34
  53.3 0.0 collective-permute-done.1.of_other
  53.3 2.4 %shard_map.68 = (bf16[512,1152]{1,0:T(8,128)(2,1)S(1)}, bf16[512,1152]{1,0:T(8,128)(2,1)S(1)}) custom-call(s32[2]{0:T(128)S(1)} %pad_add_fusion.role_ref, bf16[2,512,1152]{2,1,0:T(8,128)(2,1)S(1)} %get-tuple-element.28.lows, bf16[512,1152]{1,0:T(8,128)(2,1)S(1)} %collective-permute-done.2.second, bf16[512,1152]{1,0:T(8,128)(2,1)} %collective-permute-done.3.near_main, ...), custom_call_target="tpu_custom_call" | custom-call | tf_op jit(solution)/shard_map/pallas_call | solution.py:259
  55.7 0.1 collective-permute-start.4
  55.8 7.9 %collective-permute-start.6 = (bf16[512,1152]{1,0:T(8,128)(2,1)}, bf16[512,1152]{1,0:T(8,128)(2,1)S(1)}, u32[]{:S(2)}, u32[]{:S(2)}) collective-permute-start(bf16[512,1152]{1,0:T(8,128)(2,1)} %collective-permute-done.1.of_other), channel_id=1, source_target_pairs={{0,254},{3,5},{4,2},{7,9},{8,6},{11,13},{12,10},{15,17},{16,14},{1... | collective-permute-start | bytes 3538952 | tf_op jit(solution)/shard_map/ppermute | solution.py:34
  63.7 0.3 collective-permute-start.5
  63.9 0.0 collective-permute-done.4.swapped
  64.0 6.8 %shard_map.69 = (f32[2,512,1152]{2,1,0:T(8,128)S(1)}, f32[512,128]{1,0:T(8,128)S(1)}) custom-call(s32[2]{0:T(128)S(1)} %pad_add_fusion.role_ref, f32[2]{0:T(128)S(1)} %pad_maximum_fusion.numbers_ref, bf16[2,512,1152]{2,1,0:T(8,128)(2,1)S(1)} %get-tuple-element.28.lows, ...), custom_call_target="tpu_custom_call", output_to_operand_aliasing={{0}: (6, {}), {1}: (7, {})} | custom-call | tf_op jit(solution)/shard_map/pallas_call | solution.py:265
  70.8 6.8 %collective-permute-done.6.by_two = bf16[512,1152]{1,0:T(8,128)(2,1)S(1)} collective-permute-done((bf16[512,1152]{1,0:T(8,128)(2,1)}, bf16[512,1152]{1,0:T(8,128)(2,1)S(1)}, u32[]{:S(2)}, u32[]{:S(2)}) %collective-permute-start.6) | collective-permute-done | bytes 1179680 | tf_op jit(solution)/shard_map/ppermute | solution.py:34
  77.6 5.6 %shard_map.70 = (f32[512,1152]{1,0:T(8,128)}, f32[512,1152]{1,0:T(8,128)}, f32[512,128]{1,0:T(8,128)S(1)}) custom-call(s32[2]{0:T(128)S(1)} %pad_add_fusion.role_ref, f32[2]{0:T(128)S(1)} %pad_maximum_fusion.numbers_ref, bf16[2,512,1152]{2,1,0:T(8,128)(2,1)S(1)} %get-tuple-element.28.lows, ...), custom_call_target="tpu_custom_call", output_to_operand_aliasing={{2}: (8, {})} | custom-call | tf_op jit(solution)/shard_map/pallas_call | solution.py:274
  83.2 7.0 %collective-permute-done.5.late_low = bf16[512,1152]{1,0:T(8,128)(2,1)S(1)} collective-permute-done((bf16[512,1152]{1,0:T(8,128)(2,1)S(1)}, bf16[512,1152]{1,0:T(8,128)(2,1)S(1)}, u32[]{:S(2)}, u32[]{:S(2)}) %collective-permute-start.5) | collective-permute-done | bytes 1179680 | tf_op jit(solution)/shard_map/ppermute | solution.py:34
  90.2 5.2 %shard_map.71 = (f32[512,1152]{1,0:T(8,128)}, f32[512,1152]{1,0:T(8,128)}, f32[1,512]{1,0:T(1,128)}) custom-call(s32[2]{0:T(128)S(1)} %pad_add_fusion.role_ref, f32[2]{0:T(128)S(1)} %pad_maximum_fusion.numbers_ref, bf16[2,512,1152]{2,1,0:T(8,128)(2,1)S(1)} %get-tuple-element.28.lows, ...), custom_call_target="tpu_custom_call", output_to_operand_aliasing={{0}: (8, {}), {1}: (9, {})} | custom-call | tf_op jit(solution)/shard_map/pallas_call | solution.py:281
  (3 shorter events, 0.0 us)
Async XLA Ops:
  0.7 1.7 %copy-start = (bf16[512,1152]{1,0:T(8,128)(2,1)S(1)}, bf16[512,1152]{1,0:T(8,128)(2,1)}, u32[]{:S(2)}) copy-start(bf16[512,1152]{1,0:T(8,128)(2,1)} %param.5) | copy-start | bytes 3538948
  0.7 2.0 %copy-start.1 = (bf16[512,1152]{1,0:T(8,128)(2,1)S(1)}, bf16[512,1152]{1,0:T(8,128)(2,1)}, u32[]{:S(2)}) copy-start(bf16[512,1152]{1,0:T(8,128)(2,1)} %param.4) | copy-start | bytes 3538948
  2.3 14.1 %collective-permute-start = (bf16[512,1152]{1,0:T(8,128)(2,1)S(1)}, bf16[512,1152]{1,0:T(8,128)(2,1)}, u32[]{:S(2)}, u32[]{:S(2)}) collective-permute-start(bf16[512,1152]{1,0:T(8,128)(2,1)S(1)} %broadcast_select_fusion.1.other), channel_id=1, source_target_pairs={{0,2},{1,3},{2,0},{3,1},{4,6},{5,7},{6,4},{7,5},{8,10},{9,11},{10,... | collective-permute-start | bytes 3538952 | tf_op jit(solution)/shard_map/ppermute | solution.py:34
  2.8 36.5 %collective-permute-start.3 = (bf16[512,1152]{1,0:T(8,128)(2,1)S(1)}, bf16[512,1152]{1,0:T(8,128)(2,1)}, u32[]{:S(2)}, u32[]{:S(2)}) collective-permute-start(bf16[512,1152]{1,0:T(8,128)(2,1)S(1)} %broadcast_select_fusion.main), channel_id=1, source_target_pairs={{0,255},{3,4},{4,3},{7,8},{8,7},{11,12},{12,11},{15,16},{16,15},{1... | collective-permute-start | bytes 3538952 | tf_op jit(solution)/shard_map/ppermute | solution.py:34
  13.3 40.0 %collective-permute-start.2 = (bf16[512,1152]{1,0:T(8,128)(2,1)S(1)}, bf16[512,1152]{1,0:T(8,128)(2,1)S(1)}, u32[]{:S(2)}, u32[]{:S(2)}) collective-permute-start(bf16[512,1152]{1,0:T(8,128)(2,1)S(1)} %broadcast_select_fusion.main), channel_id=1, source_target_pairs={{0,254},{1,255},{2,4},{3,5},{4,2},{5,3},{6,8},{7,9},{8,6},{9,7},{1... | collective-permute-start | bytes 3538952 | tf_op jit(solution)/shard_map/ppermute | solution.py:34
  13.4 39.9 %collective-permute-start.1 = (bf16[512,1152]{1,0:T(8,128)(2,1)S(1)}, bf16[512,1152]{1,0:T(8,128)(2,1)}, u32[]{:S(2)}, u32[]{:S(2)}) collective-permute-start(bf16[512,1152]{1,0:T(8,128)(2,1)S(1)} %broadcast_select_fusion.1.other), channel_id=1, source_target_pairs={{0,1},{1,4},{2,255},{3,2},{4,5},{5,8},{6,3},{7,6},{8,9},{9,12},{10... | collective-permute-start | bytes 3538952 | tf_op jit(solution)/shard_map/ppermute | solution.py:34
  55.7 8.3 %collective-permute-start.4 = (bf16[512,1152]{1,0:T(8,128)(2,1)S(1)}, bf16[512,1152]{1,0:T(8,128)(2,1)S(1)}, u32[]{:S(2)}, u32[]{:S(2)}) collective-permute-start(bf16[512,1152]{1,0:T(8,128)(2,1)S(1)} %get-tuple-element.35.near_low), channel_id=1, source_target_pairs={{0,2},{1,3},{2,0},{3,1},{4,6},{5,7},{6,4},{7,5},{8,10},{9,11},{10,... | collective-permute-start | bytes 3538952 | tf_op jit(solution)/shard_map/ppermute | solution.py:34
  55.8 21.8 %collective-permute-start.6 = (bf16[512,1152]{1,0:T(8,128)(2,1)}, bf16[512,1152]{1,0:T(8,128)(2,1)S(1)}, u32[]{:S(2)}, u32[]{:S(2)}) collective-permute-start(bf16[512,1152]{1,0:T(8,128)(2,1)} %collective-permute-done.1.of_other), channel_id=1, source_target_pairs={{0,254},{3,5},{4,2},{7,9},{8,6},{11,13},{12,10},{15,17},{16,14},{1... | collective-permute-start | bytes 3538952 | tf_op jit(solution)/shard_map/ppermute | solution.py:34
  63.7 26.6 %collective-permute-start.5 = (bf16[512,1152]{1,0:T(8,128)(2,1)S(1)}, bf16[512,1152]{1,0:T(8,128)(2,1)S(1)}, u32[]{:S(2)}, u32[]{:S(2)}) collective-permute-start(bf16[512,1152]{1,0:T(8,128)(2,1)S(1)} %get-tuple-element.39), channel_id=1, source_target_pairs={{0,255},{1,254},{2,5},{3,4},{4,3},{5,2},{6,9},{7,8},{8,7},{9,6},{1... | collective-permute-start | bytes 3538952 | tf_op jit(solution)/shard_map/ppermute | solution.py:34

commit v3 on v2

--- a/solution.py
+++ b/solution.py
@@ -125,9 +125,8 @@
     )
 
 
-def sent_kernel(role_ref, lows, second, near_main, of_other, near_low, late_low):
+def late_block_kernel(role_ref, lows, second, late_low):
     outer = role_ref[0] == role_ref[1]
-    lower_one_of(outer, near_main, of_other, near_low)
 
     @pl.when(outer)
     def _():
@@ -136,6 +135,10 @@
     @pl.when(jnp.logical_not(outer))
     def _():
         late_low[...] = lows[0]
+
+
+def near_block_kernel(role_ref, near_main, of_other, near_low):
+    lower_one_of(role_ref[0] == role_ref[1], near_main, of_other, near_low)
 
 
 def middle_kernel(
@@ -254,12 +257,12 @@
         [pltpu.VMEM((rows, rows), low), pltpu.VMEM(whole, low)],
     )(role, numbers, main, other, swapped)
 
-    of_other, second, near_main, loss = together(of_other, second, near_main, loss)
+    second, near_main, loss = together(second, near_main, loss)
+    (late_low,) = call(late_block_kernel, "svv", [("v", whole, low)])(role, lows, second)
+    of_other, late_low = together(of_other, late_low)
     by_two = send(of_other, ON_BY_TWO)
-    near_low, late_low = call(sent_kernel, "svvvv", [("v", whole, low), ("v", whole, low)])(
-        role, lows, second, near_main, of_other
-    )
     late_low = send(late_low, FAR_OR_ON_BY_ONE)
+    (near_low,) = call(near_block_kernel, "svv", [("v", whole, low)])(role, near_main, of_other)
     swapped = send(near_low, SWAP)
 
     accs, loss = call(

time: 95.8 us -> 96.3 us (level)
    pallas_call x1 -> x2, Pallas kernels: 2.38 us -> 2.92 us  [the longest x1 2.01 us: body(): call(near_block_kernel, 'svv', [('v', whole, low)])]
  transfers between devices with their start and end apart: 7 -> 7, of which waited for: 4 -> 4; matrix products, arithmetic and copies ran while one was open for 0% -> 0% of each run, Pallas kernels for 20% -> 21%
where the time goes in v3:
time: 96.3 us; the launch traced here: 96.1 us
  waiting for transfers between devices  43.7 us (45%)
  Pallas kernels  27.6 us (29%)
  starting transfers between devices  20.4 us (21%)
  between operations  2.3 us (2%)
  other arithmetic  1.85 us (2%)
    ppermute x7, waiting for transfers between devices, send(): return lax.ppermute(x, AXES, pairs())  43.7 us
    ppermute x7, starting transfers between devices, send(): return lax.ppermute(x, AXES, pairs())  20.4 us
    pallas_call x1, Pallas kernels, body(): call(first_kernel, 'ssvvv', [('v', both, low), ('v', both, f32), ('v', (2...  7.11 us
    pallas_call x1, Pallas kernels, body(): call(middle_kernel, 'ssvvvvvv', [('v', both, f32), ('v', partial, f32)],...  6.79 us
    pallas_call x1, Pallas kernels, body(): call(early_kernel, 'ssvvvvvvv', [('a', whole, f32), ('a', whole, f32), ('...  5.56 us
    pallas_call x1, Pallas kernels, body(): call(late_kernel, 'ssvvvvvvaa', [('a', whole, f32), ('a', whole, f32), ('...  5.21 us
    pallas_call x1, Pallas kernels, body(): call(near_block_kernel, 'svv', [('v', whole, low)])  2.01 us
  transfers between devices with their start and end apart: 7, of which 4 were waited for; matrix products, arithmetic and copies ran while one was open for 0% of the time, Pallas kernels for 21%

profile of v3, /device:TPU:0, one launch (start us, length us, event | category | flops | bytes accessed | tf_op | source)
XLA Modules:
  0.0 96.1 jit_solution(7524371509726390251)
XLA Ops:
  0.7 1.6 %broadcast_select_fusion.1.other = bf16[512,1152]{1,0:T(8,128)(2,1)S(1)} fusion(bf16[512,1152]{1,0:T(8,128)(2,1)} %param.4, bf16[512,1152]{1,0:T(8,128)(2,1)} %param.5, pred[]{:T(512)S(6)} %eq.6), kind=kLoop, calls=%fused_computation.1 | loop fusion | flops 589824 | bytes 3538945 | tf_op jit(solution)/shard_map/jit(_where)/select_n | solution.py:243
  2.3 0.1 collective-permute-start
  2.4 0.3 copy-done.1
  2.6 0.1 broadcast_select_fusion.main
  2.8 10.5 %collective-permute-start.2 = (bf16[512,1152]{1,0:T(8,128)(2,1)S(1)}, bf16[512,1152]{1,0:T(8,128)(2,1)}, u32[]{:S(2)}, u32[]{:S(2)}) collective-permute-start(bf16[512,1152]{1,0:T(8,128)(2,1)S(1)} %broadcast_select_fusion.main), channel_id=1, source_target_pairs={{0,255},{3,4},{4,3},{7,8},{8,7},{11,12},{12,11},{15,16},{16,15},{1... | collective-permute-start | bytes 3538952 | tf_op jit(solution)/shard_map/ppermute | solution.py:34
  13.3 0.1 collective-permute-start.1
  13.4 1.5 %collective-permute-start.3 = (bf16[512,1152]{1,0:T(8,128)(2,1)S(1)}, bf16[512,1152]{1,0:T(8,128)(2,1)}, u32[]{:S(2)}, u32[]{:S(2)}) collective-permute-start(bf16[512,1152]{1,0:T(8,128)(2,1)S(1)} %broadcast_select_fusion.1.other), channel_id=1, source_target_pairs={{0,1},{1,4},{2,255},{3,2},{4,5},{5,8},{6,3},{7,6},{8,9},{9,12},{10... | collective-permute-start | bytes 3538952 | tf_op jit(solution)/shard_map/ppermute | solution.py:34
  16.2 0.1 pad_add_fusion.role_ref
  16.3 0.1 pad_maximum_fusion.numbers_ref
  16.3 0.0 collective-permute-done.swapped
  16.3 7.1 %shard_map.67 = (bf16[2,512,1152]{2,1,0:T(8,128)(2,1)S(1)}, f32[2,512,1152]{2,1,0:T(8,128)S(1)}, f32[2,512,1]{2,1,0:T(8,128)S(1)}, f32[2,512,1152]{2,1,0:T(8,128)S(1)}, f32[512,128]{1,0:T(8,128)S(1)}) custom-call(s32[2]{0:T(128)S(1)} %pad_add_fusion.role_ref, f32[2]{0:T(128)S(1)} %pad_maximum_fusion.numbers_ref, ...), custom_call_target="tpu_custom_call" | custom-call | tf_op jit(solution)/shard_map/pallas_call | solution.py:253
  23.5 15.8 %collective-permute-done.2.near_main = bf16[512,1152]{1,0:T(8,128)(2,1)} collective-permute-done((bf16[512,1152]{1,0:T(8,128)(2,1)S(1)}, bf16[512,1152]{1,0:T(8,128)(2,1)}, u32[]{:S(2)}, u32[]{:S(2)}) %collective-permute-start.2) | collective-permute-done | bytes 1179680 | tf_op jit(solution)/shard_map/ppermute | solution.py:34
  39.3 14.0 %collective-permute-done.1.second = bf16[512,1152]{1,0:T(8,128)(2,1)S(1)} collective-permute-done((bf16[512,1152]{1,0:T(8,128)(2,1)S(1)}, bf16[512,1152]{1,0:T(8,128)(2,1)S(1)}, u32[]{:S(2)}, u32[]{:S(2)}) %collective-permute-start.1) | collective-permute-done | bytes 1179680 | tf_op jit(solution)/shard_map/ppermute | solution.py:34
  53.3 0.9 shard_map.68
  54.2 0.0 collective-permute-done.3.of_other
  54.2 2.0 %shard_map.69.near_low = bf16[512,1152]{1,0:T(8,128)(2,1)S(1)} custom-call(s32[2]{0:T(128)S(1)} %pad_add_fusion.role_ref, bf16[512,1152]{1,0:T(8,128)(2,1)} %collective-permute-done.2.near_main, bf16[512,1152]{1,0:T(8,128)(2,1)} %collective-permute-done.3.of_other), custom_call_target="tpu_custom_call" | custom-call | tf_op jit(solution)/shard_map/pallas_call | solution.py:265
  56.2 0.1 collective-permute-start.4
  56.3 7.9 %collective-permute-start.6 = (bf16[512,1152]{1,0:T(8,128)(2,1)}, bf16[512,1152]{1,0:T(8,128)(2,1)S(1)}, u32[]{:S(2)}, u32[]{:S(2)}) collective-permute-start(bf16[512,1152]{1,0:T(8,128)(2,1)} %collective-permute-done.3.of_other), channel_id=1, source_target_pairs={{0,254},{3,5},{4,2},{7,9},{8,6},{11,13},{12,10},{15,17},{16,14},{1... | collective-permute-start | bytes 3538952 | tf_op jit(solution)/shard_map/ppermute | solution.py:34
  64.2 0.3 collective-permute-start.5
  64.5 6.8 %shard_map.70 = (f32[2,512,1152]{2,1,0:T(8,128)S(1)}, f32[512,128]{1,0:T(8,128)S(1)}) custom-call(s32[2]{0:T(128)S(1)} %pad_add_fusion.role_ref, f32[2]{0:T(128)S(1)} %pad_maximum_fusion.numbers_ref, bf16[2,512,1152]{2,1,0:T(8,128)(2,1)S(1)} %get-tuple-element.27.lows, ...), custom_call_target="tpu_custom_call", output_to_operand_aliasing={{0}: (6, {}), {1}: (7, {})} | custom-call | tf_op jit(solution)/shard_map/pallas_call | solution.py:268
  71.3 6.9 %collective-permute-done.6.by_two = bf16[512,1152]{1,0:T(8,128)(2,1)S(1)} collective-permute-done((bf16[512,1152]{1,0:T(8,128)(2,1)}, bf16[512,1152]{1,0:T(8,128)(2,1)S(1)}, u32[]{:S(2)}, u32[]{:S(2)}) %collective-permute-start.6) | collective-permute-done | bytes 1179680 | tf_op jit(solution)/shard_map/ppermute | solution.py:34
  78.2 5.6 %shard_map.71 = (f32[512,1152]{1,0:T(8,128)}, f32[512,1152]{1,0:T(8,128)}, f32[512,128]{1,0:T(8,128)S(1)}) custom-call(s32[2]{0:T(128)S(1)} %pad_add_fusion.role_ref, f32[2]{0:T(128)S(1)} %pad_maximum_fusion.numbers_ref, bf16[2,512,1152]{2,1,0:T(8,128)(2,1)S(1)} %get-tuple-element.27.lows, ...), custom_call_target="tpu_custom_call", output_to_operand_aliasing={{2}: (8, {})} | custom-call | tf_op jit(solution)/shard_map/pallas_call | solution.py:277
  83.7 7.0 %collective-permute-done.5.late_low = bf16[512,1152]{1,0:T(8,128)(2,1)S(1)} collective-permute-done((bf16[512,1152]{1,0:T(8,128)(2,1)S(1)}, bf16[512,1152]{1,0:T(8,128)(2,1)S(1)}, u32[]{:S(2)}, u32[]{:S(2)}) %collective-permute-start.5) | collective-permute-done | bytes 1179680 | tf_op jit(solution)/shard_map/ppermute | solution.py:34
  90.7 5.2 %shard_map.72 = (f32[512,1152]{1,0:T(8,128)}, f32[512,1152]{1,0:T(8,128)}, f32[1,512]{1,0:T(1,128)}) custom-call(s32[2]{0:T(128)S(1)} %pad_add_fusion.role_ref, f32[2]{0:T(128)S(1)} %pad_maximum_fusion.numbers_ref, bf16[2,512,1152]{2,1,0:T(8,128)(2,1)S(1)} %get-tuple-element.27.lows, ...), custom_call_target="tpu_custom_call", output_to_operand_aliasing={{0}: (8, {}), {1}: (9, {})} | custom-call | tf_op jit(solution)/shard_map/pallas_call | solution.py:284
  (4 shorter events, 0.0 us)
Async XLA Ops:
  0.7 1.7 %copy-start = (bf16[512,1152]{1,0:T(8,128)(2,1)S(1)}, bf16[512,1152]{1,0:T(8,128)(2,1)}, u32[]{:S(2)}) copy-start(bf16[512,1152]{1,0:T(8,128)(2,1)} %param.5) | copy-start | bytes 3538948
  0.7 2.0 %copy-start.1 = (bf16[512,1152]{1,0:T(8,128)(2,1)S(1)}, bf16[512,1152]{1,0:T(8,128)(2,1)}, u32[]{:S(2)}) copy-start(bf16[512,1152]{1,0:T(8,128)(2,1)} %param.4) | copy-start | bytes 3538948
  2.3 14.1 %collective-permute-start = (bf16[512,1152]{1,0:T(8,128)(2,1)S(1)}, bf16[512,1152]{1,0:T(8,128)(2,1)}, u32[]{:S(2)}, u32[]{:S(2)}) collective-permute-start(bf16[512,1152]{1,0:T(8,128)(2,1)S(1)} %broadcast_select_fusion.1.other), channel_id=1, source_target_pairs={{0,2},{1,3},{2,0},{3,1},{4,6},{5,7},{6,4},{7,5},{8,10},{9,11},{10,... | collective-permute-start | bytes 3538952 | tf_op jit(solution)/shard_map/ppermute | solution.py:34
  2.8 36.5 %collective-permute-start.2 = (bf16[512,1152]{1,0:T(8,128)(2,1)S(1)}, bf16[512,1152]{1,0:T(8,128)(2,1)}, u32[]{:S(2)}, u32[]{:S(2)}) collective-permute-start(bf16[512,1152]{1,0:T(8,128)(2,1)S(1)} %broadcast_select_fusion.main), channel_id=1, source_target_pairs={{0,255},{3,4},{4,3},{7,8},{8,7},{11,12},{12,11},{15,16},{16,15},{1... | collective-permute-start | bytes 3538952 | tf_op jit(solution)/shard_map/ppermute | solution.py:34
  13.3 40.0 %collective-permute-start.1 = (bf16[512,1152]{1,0:T(8,128)(2,1)S(1)}, bf16[512,1152]{1,0:T(8,128)(2,1)S(1)}, u32[]{:S(2)}, u32[]{:S(2)}) collective-permute-start(bf16[512,1152]{1,0:T(8,128)(2,1)S(1)} %broadcast_select_fusion.main), channel_id=1, source_target_pairs={{0,254},{1,255},{2,4},{3,5},{4,2},{5,3},{6,8},{7,9},{8,6},{9,7},{1... | collective-permute-start | bytes 3538952 | tf_op jit(solution)/shard_map/ppermute | solution.py:34
  13.4 40.8 %collective-permute-start.3 = (bf16[512,1152]{1,0:T(8,128)(2,1)S(1)}, bf16[512,1152]{1,0:T(8,128)(2,1)}, u32[]{:S(2)}, u32[]{:S(2)}) collective-permute-start(bf16[512,1152]{1,0:T(8,128)(2,1)S(1)} %broadcast_select_fusion.1.other), channel_id=1, source_target_pairs={{0,1},{1,4},{2,255},{3,2},{4,5},{5,8},{6,3},{7,6},{8,9},{9,12},{10... | collective-permute-start | bytes 3538952 | tf_op jit(solution)/shard_map/ppermute | solution.py:34
  56.2 8.3 %collective-permute-start.4 = (bf16[512,1152]{1,0:T(8,128)(2,1)S(1)}, bf16[512,1152]{1,0:T(8,128)(2,1)S(1)}, u32[]{:S(2)}, u32[]{:S(2)}) collective-permute-start(bf16[512,1152]{1,0:T(8,128)(2,1)S(1)} %shard_map.69.near_low), channel_id=1, source_target_pairs={{0,2},{1,3},{2,0},{3,1},{4,6},{5,7},{6,4},{7,5},{8,10},{9,11},{10,... | collective-permute-start | bytes 3538952 | tf_op jit(solution)/shard_map/ppermute | solution.py:34
  56.3 21.8 %collective-permute-start.6 = (bf16[512,1152]{1,0:T(8,128)(2,1)}, bf16[512,1152]{1,0:T(8,128)(2,1)S(1)}, u32[]{:S(2)}, u32[]{:S(2)}) collective-permute-start(bf16[512,1152]{1,0:T(8,128)(2,1)} %collective-permute-done.3.of_other), channel_id=1, source_target_pairs={{0,254},{3,5},{4,2},{7,9},{8,6},{11,13},{12,10},{15,17},{16,14},{1... | collective-permute-start | bytes 3538952 | tf_op jit(solution)/shard_map/ppermute | solution.py:34
  64.2 26.5 %collective-permute-start.5 = (bf16[512,1152]{1,0:T(8,128)(2,1)S(1)}, bf16[512,1152]{1,0:T(8,128)(2,1)S(1)}, u32[]{:S(2)}, u32[]{:S(2)}) collective-permute-start(bf16[512,1152]{1,0:T(8,128)(2,1)S(1)} %shard_map.68), channel_id=1, source_target_pairs={{0,255},{1,254},{2,5},{3,4},{4,3},{5,2},{6,9},{7,8},{8,7},{9,6},{1... | collective-permute-start | bytes 3538952 | tf_op jit(solution)/shard_map/ppermute | solution.py:34

commit v4 on v3

--- a/solution.py
+++ b/solution.py
@@ -10,7 +10,7 @@
 AXES = ("blk", "rep")
 EPSILON = 1e-06
 COLUMNS = 512
-STRIP = 512
+STRIP = 128
 LANES = 128
 
 
@@ -26,6 +26,8 @@
 SECOND = by_role({0: -2, 1: -2, 4: -2, 5: -2, 2: 2, 3: 2, 6: 2, 7: 2})
 OF_OTHER = by_role({1: 3, 5: 3, 2: -3, 6: -3, 0: 1, 4: 1, 3: -1, 7: -1})
 NEAR_OF_MAIN = by_role({0: -1, 4: -1, 3: 1, 7: 1})
+NEAR_TO_INNER = by_role({0: 2, 4: 2, 3: -2, 7: -2})
+NEAR_TO_OUTER = by_role({1: 2, 5: 2, 2: -2, 6: -2})
 ON_BY_TWO = by_role({0: -2, 4: -2, 3: 2, 7: 2})
 FAR_OR_ON_BY_ONE = by_role({1: -3, 5: -3, 2: 3, 6: 3, 0: -1, 4: -1, 3: 1, 7: 1})
 
@@ -137,59 +139,50 @@
         late_low[...] = lows[0]
 
 
-def near_block_kernel(role_ref, near_main, of_other, near_low):
-    lower_one_of(role_ref[0] == role_ref[1], near_main, of_other, near_low)
-
-
 def middle_kernel(
-    role_ref, numbers_ref, lows, second, near_low, swapped, accs_in, loss_in, accs, loss_ref, low_ref
+    role_ref, numbers_ref, lows, second, near_main, of_other, to_inner, to_outer, accs_in, loss_in,
+    accs, loss_ref, low_ref,
 ):
     on_other = role_ref[0].astype(jnp.float32)
     on_main = 1.0 - on_other
-    pair(numbers_ref, lows.at[0], near_low, accs_in.at[0], accs.at[0], loss_in, loss_ref, on_main)
+    outer = role_ref[0] == role_ref[1]
     lower(second, low_ref)
+    pair(numbers_ref, lows.at[0], low_ref, accs_in.at[0], accs.at[0], loss_in, loss_ref, on_main)
+    lower_one_of(outer, near_main, of_other, low_ref)
     pair(numbers_ref, lows.at[0], low_ref, accs.at[0], accs.at[0], loss_ref, loss_ref, on_main)
-    pair(numbers_ref, lows.at[1], swapped, accs_in.at[1], accs.at[1], loss_ref, loss_ref, on_other)
+    lower_one_of(outer, to_outer, to_inner, low_ref)
+    pair(numbers_ref, lows.at[1], low_ref, accs_in.at[1], accs.at[1], loss_ref, loss_ref, on_other)
 
 
 def close_side(
-    side, core, numbers_ref, lows, units, scales, accs, partner_ref, loss_from, loss_to,
+    strip, side, core, numbers_ref, lows, units, scales, accs, partner_ref, loss_from, loss_to,
     image_out, text_out, done_ref, sems,
 ):
     counts = (side == core).astype(jnp.float32)
-    own_low = lows.at[side]
-
-    parts = done_ref.shape[0] // STRIP
-
-    def copy(k, out):
-        rows = pl.ds(k * STRIP, STRIP)
-        return pltpu.make_async_copy(done_ref.at[rows, :], out.at[rows, :], sems.at[k])
-
-    done_ref[...] = accs[side] + partner_grad(numbers_ref, own_low, partner_ref, loss_from, loss_to, counts)
-    for k in range(parts):
-        rows = pl.ds(k * STRIP, STRIP)
-        grad = done_ref[rows, :]
-        unit = units[side, rows, :]
-        along = jnp.sum(unit * grad, axis=-1, keepdims=True)
-        done_ref[rows, :] = scales[side, rows, :] * (grad - unit * along)
-
-        @pl.when(side == core)
-        def _():
-            copy(k, image_out).start()
-
-        @pl.when(side != core)
-        def _():
-            copy(k, text_out).start()
+    done_ref[...] = accs[side] + partner_grad(
+        numbers_ref, lows.at[side], partner_ref, loss_from, loss_to, counts
+    )
+
+    def finish_into(out):
+        copies = []
+        for k in range(done_ref.shape[0] // strip):
+            rows = pl.ds(k * strip, strip)
+            grad = done_ref[rows, :]
+            unit = units[side, rows, :]
+            along = jnp.sum(unit * grad, axis=-1, keepdims=True)
+            done_ref[rows, :] = scales[side, rows, :] * (grad - unit * along)
+            copies.append(pltpu.make_async_copy(done_ref.at[rows, :], out.at[rows, :], sems.at[k]))
+            copies[-1].start()
+        for copy in copies:
+            copy.wait()
 
     @pl.when(side == core)
     def _():
-        for k in range(parts):
-            copy(k, image_out).wait()
+        finish_into(image_out)
 
     @pl.when(side != core)
     def _():
-        for k in range(parts):
-            copy(k, text_out).wait()
+        finish_into(text_out)
 
 
 def early_kernel(
@@ -199,7 +192,7 @@
     outer = role_ref[0] == role_ref[1]
     lower_one_of(outer, of_other, by_two, low_ref)
     close_side(
-        jnp.where(outer, 0, 1), role_ref[0], numbers_ref, lows, units, scales, accs, low_ref,
+        STRIP, jnp.where(outer, 0, 1), role_ref[0], numbers_ref, lows, units, scales, accs, low_ref,
         loss_in, loss_ref, image_out, text_out, done_ref, sems,
     )
 
@@ -210,7 +203,7 @@
 ):
     outer = role_ref[0] == role_ref[1]
     close_side(
-        jnp.where(outer, 1, 0), role_ref[0], numbers_ref, lows, units, scales, accs, late_low,
+        STRIP, jnp.where(outer, 1, 0), role_ref[0], numbers_ref, lows, units, scales, accs, late_low,
         loss_in, loss_ref, image_out, text_out, done_ref, sems,
     )
     row_loss[...] = jnp.sum(loss_ref[...].T, axis=0, keepdims=True)
@@ -257,21 +250,21 @@
         [pltpu.VMEM((rows, rows), low), pltpu.VMEM(whole, low)],
     )(role, numbers, main, other, swapped)
 
-    second, near_main, loss = together(second, near_main, loss)
+    near_main, second, loss = together(near_main, second, loss)
     (late_low,) = call(late_block_kernel, "svv", [("v", whole, low)])(role, lows, second)
     of_other, late_low = together(of_other, late_low)
     by_two = send(of_other, ON_BY_TWO)
     late_low = send(late_low, FAR_OR_ON_BY_ONE)
-    (near_low,) = call(near_block_kernel, "svv", [("v", whole, low)])(role, near_main, of_other)
-    swapped = send(near_low, SWAP)
+    to_inner = send(near_main, NEAR_TO_INNER)
+    to_outer = send(of_other, NEAR_TO_OUTER)
 
     accs, loss = call(
         middle_kernel,
-        "ssvvvvvv",
+        "ssvvvvvvvv",
         [("v", both, f32), ("v", partial, f32)],
         [pltpu.VMEM(whole, low)],
-        {6: 0, 7: 1},
-    )(role, numbers, lows, second, near_low, swapped, accs, loss)
+        {8: 0, 9: 1},
+    )(role, numbers, lows, second, near_main, of_other, to_inner, to_outer, accs, loss)
 
     copy_sems = pltpu.SemaphoreType.DMA((rows // STRIP,))
     grad_image, grad_text, loss = call(

time: 96.3 us -> 98.8 us (1.026)
  starting transfers between devices: 20.4 us -> 24.6 us
  waiting for transfers between devices: 43.7 us -> 40.7 us
  Pallas kernels: 27.6 us -> 28.8 us
    ppermute x7 -> x8, starting transfers between devices: 20.4 us -> 24.6 us  [send(): return lax.ppermute(x, AXES, pairs())]
    ppermute x7 -> x8, waiting for transfers between devices: 43.7 us -> 40.7 us  [send(): return lax.ppermute(x, AXES, pairs())]
    pallas_call x2 -> x1, Pallas kernels: 8.8 us -> 9.78 us  [body(): call(middle_kernel, 'ssvvvvvvvv', [('v', both, f32), ('v', partial, f32)]...]
  transfers between devices with their start and end apart: 7 -> 8, of which waited for: 4 -> 4; matrix products, arithmetic and copies ran while one was open for 0% -> 0% of each run, Pallas kernels for 21% -> 24%
where the time goes in v4:
time: 98.8 us; the launch traced here: 98.5 us
  waiting for transfers between devices  40.7 us (41%)
  Pallas kernels  28.8 us (29%)
  starting transfers between devices  24.6 us (25%)
  between operations  2.31 us (2%)
  other arithmetic  1.85 us (2%)
    ppermute x8, waiting for transfers between devices, send(): return lax.ppermute(x, AXES, pairs())  40.7 us
    ppermute x8, starting transfers between devices, send(): return lax.ppermute(x, AXES, pairs())  24.6 us
    pallas_call x1, Pallas kernels, body(): call(middle_kernel, 'ssvvvvvvvv', [('v', both, f32), ('v', partial, f32)]...  9.78 us
    pallas_call x1, Pallas kernels, body(): call(first_kernel, 'ssvvv', [('v', both, low), ('v', both, f32), ('v', (2...  7.11 us
    pallas_call x1, Pallas kernels, body(): call(early_kernel, 'ssvvvvvvv', [('a', whole, f32), ('a', whole, f32), ('...  5.7 us
    pallas_call x1, Pallas kernels, body(): call(late_kernel, 'ssvvvvvvaa', [('a', whole, f32), ('a', whole, f32), ('...  5.31 us
  transfers between devices with their start and end apart: 8, of which 4 were waited for; matrix products, arithmetic and copies ran while one was open for 0% of the time, Pallas kernels for 24%

profile of v4, /device:TPU:0, one launch (start us, length us, event | category | flops | bytes accessed | tf_op | source)
XLA Modules:
  0.0 98.5 jit_solution(12229533152996513629)
XLA Ops:
  0.7 1.6 %broadcast_select_fusion.1.other = bf16[512,1152]{1,0:T(8,128)(2,1)S(1)} fusion(bf16[512,1152]{1,0:T(8,128)(2,1)} %param.4, bf16[512,1152]{1,0:T(8,128)(2,1)} %param.5, pred[]{:T(512)S(6)} %eq.6), kind=kLoop, calls=%fused_computation.1 | loop fusion | flops 589824 | bytes 3538945 | tf_op jit(solution)/shard_map/jit(_where)/select_n | solution.py:236
  2.3 0.1 collective-permute-start
  2.4 0.3 copy-done.1
  2.6 0.1 broadcast_select_fusion.main
  2.8 10.5 %collective-permute-start.1 = (bf16[512,1152]{1,0:T(8,128)(2,1)S(1)}, bf16[512,1152]{1,0:T(8,128)(2,1)}, u32[]{:S(2)}, u32[]{:S(2)}) collective-permute-start(bf16[512,1152]{1,0:T(8,128)(2,1)S(1)} %broadcast_select_fusion.main), channel_id=1, source_target_pairs={{0,255},{3,4},{4,3},{7,8},{8,7},{11,12},{12,11},{15,16},{16,15},{1... | collective-permute-start | bytes 3538952 | tf_op jit(solution)/shard_map/ppermute | solution.py:36
  13.3 0.1 collective-permute-start.2
  13.4 1.5 %collective-permute-start.3 = (bf16[512,1152]{1,0:T(8,128)(2,1)S(1)}, bf16[512,1152]{1,0:T(8,128)(2,1)}, u32[]{:S(2)}, u32[]{:S(2)}) collective-permute-start(bf16[512,1152]{1,0:T(8,128)(2,1)S(1)} %broadcast_select_fusion.1.other), channel_id=1, source_target_pairs={{0,1},{1,4},{2,255},{3,2},{4,5},{5,8},{6,3},{7,6},{8,9},{9,12},{10... | collective-permute-start | bytes 3538952 | tf_op jit(solution)/shard_map/ppermute | solution.py:36
  16.2 0.1 pad_add_fusion.role_ref
  16.3 0.1 pad_maximum_fusion.numbers_ref
  16.3 7.1 %shard_map.67 = (bf16[2,512,1152]{2,1,0:T(8,128)(2,1)S(1)}, f32[2,512,1152]{2,1,0:T(8,128)S(1)}, f32[2,512,1]{2,1,0:T(8,128)S(1)}, f32[2,512,1152]{2,1,0:T(8,128)S(1)}, f32[512,128]{1,0:T(8,128)S(1)}) custom-call(s32[2]{0:T(128)S(1)} %pad_add_fusion.role_ref, f32[2]{0:T(128)S(1)} %pad_maximum_fusion.numbers_ref, ...), custom_call_target="tpu_custom_call" | custom-call | tf_op jit(solution)/shard_map/pallas_call | solution.py:246
  23.5 15.8 %collective-permute-done.1.near_main = bf16[512,1152]{1,0:T(8,128)(2,1)} collective-permute-done((bf16[512,1152]{1,0:T(8,128)(2,1)S(1)}, bf16[512,1152]{1,0:T(8,128)(2,1)}, u32[]{:S(2)}, u32[]{:S(2)}) %collective-permute-start.1) | collective-permute-done | bytes 1179680 | tf_op jit(solution)/shard_map/ppermute | solution.py:36
  39.3 14.0 %collective-permute-done.2.second = bf16[512,1152]{1,0:T(8,128)(2,1)S(1)} collective-permute-done((bf16[512,1152]{1,0:T(8,128)(2,1)S(1)}, bf16[512,1152]{1,0:T(8,128)(2,1)S(1)}, u32[]{:S(2)}, u32[]{:S(2)}) %collective-permute-start.2) | collective-permute-done | bytes 1179680 | tf_op jit(solution)/shard_map/ppermute | solution.py:36
  53.3 0.9 shard_map.68
  54.2 1.4 %collective-permute-start.4 = (bf16[512,1152]{1,0:T(8,128)(2,1)}, bf16[512,1152]{1,0:T(8,128)(2,1)S(1)}, u32[]{:S(2)}, u32[]{:S(2)}) collective-permute-start(bf16[512,1152]{1,0:T(8,128)(2,1)} %collective-permute-done.1.near_main), channel_id=1, source_target_pairs={{0,2},{3,1},{4,6},{7,5},{8,10},{11,9},{12,14},{15,13},{16,18},{19,... | collective-permute-start | bytes 3538952 | tf_op jit(solution)/shard_map/ppermute | solution.py:36
  55.6 1.3 %collective-permute-start.5 = (bf16[512,1152]{1,0:T(8,128)(2,1)}, bf16[512,1152]{1,0:T(8,128)(2,1)S(1)}, u32[]{:S(2)}, u32[]{:S(2)}) collective-permute-start(bf16[512,1152]{1,0:T(8,128)(2,1)} %collective-permute-done.3.of_other), channel_id=1, source_target_pairs={{1,3},{2,0},{5,7},{6,4},{9,11},{10,8},{13,15},{14,12},{17,19},{18,... | collective-permute-start | bytes 3538952 | tf_op jit(solution)/shard_map/ppermute | solution.py:36
  56.9 9.7 %collective-permute-start.7 = (bf16[512,1152]{1,0:T(8,128)(2,1)}, bf16[512,1152]{1,0:T(8,128)(2,1)S(1)}, u32[]{:S(2)}, u32[]{:S(2)}) collective-permute-start(bf16[512,1152]{1,0:T(8,128)(2,1)} %collective-permute-done.3.of_other), channel_id=1, source_target_pairs={{0,254},{3,5},{4,2},{7,9},{8,6},{11,13},{12,10},{15,17},{16,14},{1... | collective-permute-start | bytes 3538952 | tf_op jit(solution)/shard_map/ppermute | solution.py:36
  66.6 0.1 collective-permute-start.6
  66.7 0.0 collective-permute-done.4.to_inner
  66.7 0.0 collective-permute-done.5.to_outer
  66.7 9.8 %shard_map.69 = (f32[2,512,1152]{2,1,0:T(8,128)S(1)}, f32[512,128]{1,0:T(8,128)S(1)}) custom-call(s32[2]{0:T(128)S(1)} %pad_add_fusion.role_ref, f32[2]{0:T(128)S(1)} %pad_maximum_fusion.numbers_ref, bf16[2,512,1152]{2,1,0:T(8,128)(2,1)S(1)} %get-tuple-element.27.lows, ...), custom_call_target="tpu_custom_call", output_to_operand_aliasing={{0}: (8, {}), {1}: (9, {})} | custom-call | tf_op jit(solution)/shard_map/pallas_call | solution.py:261
  76.5 4.0 %collective-permute-done.7.by_two = bf16[512,1152]{1,0:T(8,128)(2,1)S(1)} collective-permute-done((bf16[512,1152]{1,0:T(8,128)(2,1)}, bf16[512,1152]{1,0:T(8,128)(2,1)S(1)}, u32[]{:S(2)}, u32[]{:S(2)}) %collective-permute-start.7) | collective-permute-done | bytes 1179680 | tf_op jit(solution)/shard_map/ppermute | solution.py:36
  80.5 5.7 %shard_map.70 = (f32[512,1152]{1,0:T(8,128)}, f32[512,1152]{1,0:T(8,128)}, f32[512,128]{1,0:T(8,128)S(1)}) custom-call(s32[2]{0:T(128)S(1)} %pad_add_fusion.role_ref, f32[2]{0:T(128)S(1)} %pad_maximum_fusion.numbers_ref, bf16[2,512,1152]{2,1,0:T(8,128)(2,1)S(1)} %get-tuple-element.27.lows, ...), custom_call_target="tpu_custom_call", output_to_operand_aliasing={{2}: (8, {})} | custom-call | tf_op jit(solution)/shard_map/pallas_call | solution.py:270
  86.2 6.8 %collective-permute-done.6.late_low = bf16[512,1152]{1,0:T(8,128)(2,1)S(1)} collective-permute-done((bf16[512,1152]{1,0:T(8,128)(2,1)S(1)}, bf16[512,1152]{1,0:T(8,128)(2,1)S(1)}, u32[]{:S(2)}, u32[]{:S(2)}) %collective-permute-start.6) | collective-permute-done | bytes 1179680 | tf_op jit(solution)/shard_map/ppermute | solution.py:36
  93.1 5.3 %shard_map.71 = (f32[512,1152]{1,0:T(8,128)}, f32[512,1152]{1,0:T(8,128)}, f32[1,512]{1,0:T(1,128)}) custom-call(s32[2]{0:T(128)S(1)} %pad_add_fusion.role_ref, f32[2]{0:T(128)S(1)} %pad_maximum_fusion.numbers_ref, bf16[2,512,1152]{2,1,0:T(8,128)(2,1)S(1)} %get-tuple-element.27.lows, ...), custom_call_target="tpu_custom_call", output_to_operand_aliasing={{0}: (8, {}), {1}: (9, {})} | custom-call | tf_op jit(solution)/shard_map/pallas_call | solution.py:277
  (5 shorter events, 0.0 us)
Async XLA Ops:
  0.7 1.7 %copy-start = (bf16[512,1152]{1,0:T(8,128)(2,1)S(1)}, bf16[512,1152]{1,0:T(8,128)(2,1)}, u32[]{:S(2)}) copy-start(bf16[512,1152]{1,0:T(8,128)(2,1)} %param.5) | copy-start | bytes 3538948
  0.7 2.0 %copy-start.1 = (bf16[512,1152]{1,0:T(8,128)(2,1)S(1)}, bf16[512,1152]{1,0:T(8,128)(2,1)}, u32[]{:S(2)}) copy-start(bf16[512,1152]{1,0:T(8,128)(2,1)} %param.4) | copy-start | bytes 3538948
  2.3 14.1 %collective-permute-start = (bf16[512,1152]{1,0:T(8,128)(2,1)S(1)}, bf16[512,1152]{1,0:T(8,128)(2,1)}, u32[]{:S(2)}, u32[]{:S(2)}) collective-permute-start(bf16[512,1152]{1,0:T(8,128)(2,1)S(1)} %broadcast_select_fusion.1.other), channel_id=1, source_target_pairs={{0,2},{1,3},{2,0},{3,1},{4,6},{5,7},{6,4},{7,5},{8,10},{9,11},{10,... | collective-permute-start | bytes 3538952 | tf_op jit(solution)/shard_map/ppermute | solution.py:36
  2.8 36.5 %collective-permute-start.1 = (bf16[512,1152]{1,0:T(8,128)(2,1)S(1)}, bf16[512,1152]{1,0:T(8,128)(2,1)}, u32[]{:S(2)}, u32[]{:S(2)}) collective-permute-start(bf16[512,1152]{1,0:T(8,128)(2,1)S(1)} %broadcast_select_fusion.main), channel_id=1, source_target_pairs={{0,255},{3,4},{4,3},{7,8},{8,7},{11,12},{12,11},{15,16},{16,15},{1... | collective-permute-start | bytes 3538952 | tf_op jit(solution)/shard_map/ppermute | solution.py:36
  13.3 40.0 %collective-permute-start.2 = (bf16[512,1152]{1,0:T(8,128)(2,1)S(1)}, bf16[512,1152]{1,0:T(8,128)(2,1)S(1)}, u32[]{:S(2)}, u32[]{:S(2)}) collective-permute-start(bf16[512,1152]{1,0:T(8,128)(2,1)S(1)} %broadcast_select_fusion.main), channel_id=1, source_target_pairs={{0,254},{1,255},{2,4},{3,5},{4,2},{5,3},{6,8},{7,9},{8,6},{9,7},{1... | collective-permute-start | bytes 3538952 | tf_op jit(solution)/shard_map/ppermute | solution.py:36
  13.4 40.8 %collective-permute-start.3 = (bf16[512,1152]{1,0:T(8,128)(2,1)S(1)}, bf16[512,1152]{1,0:T(8,128)(2,1)}, u32[]{:S(2)}, u32[]{:S(2)}) collective-permute-start(bf16[512,1152]{1,0:T(8,128)(2,1)S(1)} %broadcast_select_fusion.1.other), channel_id=1, source_target_pairs={{0,1},{1,4},{2,255},{3,2},{4,5},{5,8},{6,3},{7,6},{8,9},{9,12},{10... | collective-permute-start | bytes 3538952 | tf_op jit(solution)/shard_map/ppermute | solution.py:36
  54.2 12.5 %collective-permute-start.4 = (bf16[512,1152]{1,0:T(8,128)(2,1)}, bf16[512,1152]{1,0:T(8,128)(2,1)S(1)}, u32[]{:S(2)}, u32[]{:S(2)}) collective-permute-start(bf16[512,1152]{1,0:T(8,128)(2,1)} %collective-permute-done.1.near_main), channel_id=1, source_target_pairs={{0,2},{3,1},{4,6},{7,5},{8,10},{11,9},{12,14},{15,13},{16,18},{19,... | collective-permute-start | bytes 3538952 | tf_op jit(solution)/shard_map/ppermute | solution.py:36
  55.6 11.1 %collective-permute-start.5 = (bf16[512,1152]{1,0:T(8,128)(2,1)}, bf16[512,1152]{1,0:T(8,128)(2,1)S(1)}, u32[]{:S(2)}, u32[]{:S(2)}) collective-permute-start(bf16[512,1152]{1,0:T(8,128)(2,1)} %collective-permute-done.3.of_other), channel_id=1, source_target_pairs={{1,3},{2,0},{5,7},{6,4},{9,11},{10,8},{13,15},{14,12},{17,19},{18,... | collective-permute-start | bytes 3538952 | tf_op jit(solution)/shard_map/ppermute | solution.py:36
  56.9 23.6 %collective-permute-start.7 = (bf16[512,1152]{1,0:T(8,128)(2,1)}, bf16[512,1152]{1,0:T(8,128)(2,1)S(1)}, u32[]{:S(2)}, u32[]{:S(2)}) collective-permute-start(bf16[512,1152]{1,0:T(8,128)(2,1)} %collective-permute-done.3.of_other), channel_id=1, source_target_pairs={{0,254},{3,5},{4,2},{7,9},{8,6},{11,13},{12,10},{15,17},{16,14},{1... | collective-permute-start | bytes 3538952 | tf_op jit(solution)/shard_map/ppermute | solution.py:36
  66.6 26.5 %collective-permute-start.6 = (bf16[512,1152]{1,0:T(8,128)(2,1)S(1)}, bf16[512,1152]{1,0:T(8,128)(2,1)S(1)}, u32[]{:S(2)}, u32[]{:S(2)}) collective-permute-start(bf16[512,1152]{1,0:T(8,128)(2,1)S(1)} %shard_map.68), channel_id=1, source_target_pairs={{0,255},{1,254},{2,5},{3,4},{4,3},{5,2},{6,9},{7,8},{8,7},{9,6},{1... | collective-permute-start | bytes 3538952 | tf_op jit(solution)/shard_map/ppermute | solution.py:36

commit v5 on v4

--- a/solution.py
+++ b/solution.py
@@ -9,8 +9,7 @@
 
 AXES = ("blk", "rep")
 EPSILON = 1e-06
-COLUMNS = 512
-STRIP = 128
+STRIP = 256
 LANES = 128
 
 
@@ -26,8 +25,6 @@
 SECOND = by_role({0: -2, 1: -2, 4: -2, 5: -2, 2: 2, 3: 2, 6: 2, 7: 2})
 OF_OTHER = by_role({1: 3, 5: 3, 2: -3, 6: -3, 0: 1, 4: 1, 3: -1, 7: -1})
 NEAR_OF_MAIN = by_role({0: -1, 4: -1, 3: 1, 7: 1})
-NEAR_TO_INNER = by_role({0: 2, 4: 2, 3: -2, 7: -2})
-NEAR_TO_OUTER = by_role({1: 2, 5: 2, 2: -2, 6: -2})
 ON_BY_TWO = by_role({0: -2, 4: -2, 3: 2, 7: 2})
 FAR_OR_ON_BY_ONE = by_role({1: -3, 5: -3, 2: 3, 6: 3, 0: -1, 4: -1, 3: 1, 7: 1})
 
@@ -80,22 +77,16 @@
     )
 
 
-def partner_grad(numbers_ref, own_ref, partner_ref, loss_from, loss_to, counts):
+def partner_weights(numbers_ref, own_ref, partner_ref, loss_from, loss_to, counts):
     temper, bias = numbers_ref[0], numbers_ref[1]
-    loss, grad = 0.0, 0.0
-    for at in range(0, partner_ref.shape[0], COLUMNS):
-        partner = partner_ref[pl.ds(at, COLUMNS), :]
-        losses, chances = terms(temper * product(own_ref[...], partner, 1, 1) + bias)
-        loss = loss + folded(losses)
-        grad = grad + product((chances * temper).astype(jnp.bfloat16), partner, 1, 0)
-    loss_to[...] = loss_from[...] + counts * loss
-    return grad
+    losses, chances = terms(temper * product(own_ref[...], partner_ref[...], 1, 1) + bias)
+    loss_to[...] = loss_from[...] + counts * folded(losses)
+    return (chances * temper).astype(jnp.bfloat16)
 
 
 def pair(numbers_ref, own_ref, partner_ref, acc_from, acc_to, loss_from, loss_to, counts):
-    acc_to[...] = acc_from[...] + partner_grad(
-        numbers_ref, own_ref, partner_ref, loss_from, loss_to, counts
-    )
+    weights = partner_weights(numbers_ref, own_ref, partner_ref, loss_from, loss_to, counts)
+    acc_to[...] = acc_from[...] + product(weights, partner_ref[...], 1, 0)
 
 
 def first_kernel(
@@ -140,34 +131,30 @@
 
 
 def middle_kernel(
-    role_ref, numbers_ref, lows, second, near_main, of_other, to_inner, to_outer, accs_in, loss_in,
-    accs, loss_ref, low_ref,
+    role_ref, numbers_ref, lows, near_main, second, of_other, swapped, accs_in, loss_in, accs, loss_ref, low_ref
 ):
     on_other = role_ref[0].astype(jnp.float32)
     on_main = 1.0 - on_other
-    outer = role_ref[0] == role_ref[1]
+    lower_one_of(role_ref[0] == role_ref[1], near_main, of_other, low_ref)
+    pair(numbers_ref, lows.at[0], low_ref, accs_in.at[0], accs.at[0], loss_in, loss_ref, on_main)
     lower(second, low_ref)
-    pair(numbers_ref, lows.at[0], low_ref, accs_in.at[0], accs.at[0], loss_in, loss_ref, on_main)
-    lower_one_of(outer, near_main, of_other, low_ref)
     pair(numbers_ref, lows.at[0], low_ref, accs.at[0], accs.at[0], loss_ref, loss_ref, on_main)
-    lower_one_of(outer, to_outer, to_inner, low_ref)
+    lower(swapped, low_ref)
     pair(numbers_ref, lows.at[1], low_ref, accs_in.at[1], accs.at[1], loss_ref, loss_ref, on_other)
 
 
 def close_side(
-    strip, side, core, numbers_ref, lows, units, scales, accs, partner_ref, loss_from, loss_to,
-    image_out, text_out, done_ref, sems,
+    side, core, numbers_ref, lows, units, scales, accs, partner_ref, loss_from, loss_to,
+    image_out, text_out, weights_ref, done_ref, sems,
 ):
     counts = (side == core).astype(jnp.float32)
-    done_ref[...] = accs[side] + partner_grad(
-        numbers_ref, lows.at[side], partner_ref, loss_from, loss_to, counts
-    )
+    weights_ref[...] = partner_weights(numbers_ref, lows.at[side], partner_ref, loss_from, loss_to, counts)
 
     def finish_into(out):
         copies = []
-        for k in range(done_ref.shape[0] // strip):
-            rows = pl.ds(k * strip, strip)
-            grad = done_ref[rows, :]
+        for k in range(done_ref.shape[0] // STRIP):
+            rows = pl.ds(k * STRIP, STRIP)
+            grad = accs[side, rows, :] + product(weights_ref[rows, :], partner_ref[...], 1, 0)
             unit = units[side, rows, :]
             along = jnp.sum(unit * grad, axis=-1, keepdims=True)
             done_ref[rows, :] = scales[side, rows, :] * (grad - unit * along)
@@ -187,24 +174,24 @@
 
 def early_kernel(
     role_ref, numbers_ref, lows, units, scales, accs, of_other, by_two, loss_in,
-    image_out, text_out, loss_ref, low_ref, done_ref, sems,
+    image_out, text_out, loss_ref, low_ref, weights_ref, done_ref, sems,
 ):
     outer = role_ref[0] == role_ref[1]
     lower_one_of(outer, of_other, by_two, low_ref)
     close_side(
-        STRIP, jnp.where(outer, 0, 1), role_ref[0], numbers_ref, lows, units, scales, accs, low_ref,
-        loss_in, loss_ref, image_out, text_out, done_ref, sems,
+        jnp.where(outer, 0, 1), role_ref[0], numbers_ref, lows, units, scales, accs, low_ref,
+        loss_in, loss_ref, image_out, text_out, weights_ref, done_ref, sems,
     )
 
 
 def late_kernel(
     role_ref, numbers_ref, lows, units, scales, accs, late_low, loss_in, image_in, text_in,
-    image_out, text_out, row_loss, loss_ref, done_ref, sems,
+    image_out, text_out, row_loss, loss_ref, weights_ref, done_ref, sems,
 ):
     outer = role_ref[0] == role_ref[1]
     close_side(
-        STRIP, jnp.where(outer, 1, 0), role_ref[0], numbers_ref, lows, units, scales, accs, late_low,
-        loss_in, loss_ref, image_out, text_out, done_ref, sems,
+        jnp.where(outer, 1, 0), role_ref[0], numbers_ref, lows, units, scales, accs, late_low,
+        loss_in, loss_ref, image_out, text_out, weights_ref, done_ref, sems,
     )
     row_loss[...] = jnp.sum(loss_ref[...].T, axis=0, keepdims=True)
 
@@ -250,35 +237,34 @@
         [pltpu.VMEM((rows, rows), low), pltpu.VMEM(whole, low)],
     )(role, numbers, main, other, swapped)
 
-    near_main, second, loss = together(near_main, second, loss)
+    second, near_main, loss = together(second, near_main, loss)
     (late_low,) = call(late_block_kernel, "svv", [("v", whole, low)])(role, lows, second)
     of_other, late_low = together(of_other, late_low)
     by_two = send(of_other, ON_BY_TWO)
     late_low = send(late_low, FAR_OR_ON_BY_ONE)
-    to_inner = send(near_main, NEAR_TO_INNER)
-    to_outer = send(of_other, NEAR_TO_OUTER)
+    swapped = send(jnp.where(core == place % 2, near_main, of_other), SWAP)
 
     accs, loss = call(
         middle_kernel,
-        "ssvvvvvvvv",
+        "ssvvvvvvv",
         [("v", both, f32), ("v", partial, f32)],
         [pltpu.VMEM(whole, low)],
-        {8: 0, 9: 1},
-    )(role, numbers, lows, second, near_main, of_other, to_inner, to_outer, accs, loss)
+        {7: 0, 8: 1},
+    )(role, numbers, lows, near_main, second, of_other, swapped, accs, loss)
 
     copy_sems = pltpu.SemaphoreType.DMA((rows // STRIP,))
     grad_image, grad_text, loss = call(
         early_kernel,
         "ssvvvvvvv",
         [("a", whole, f32), ("a", whole, f32), ("v", partial, f32)],
-        [pltpu.VMEM(whole, low), pltpu.VMEM(whole, f32), copy_sems],
+        [pltpu.VMEM(whole, low), pltpu.VMEM((rows, rows), low), pltpu.VMEM(whole, f32), copy_sems],
         {8: 2},
     )(role, numbers, lows, units, scales, accs, of_other, by_two, loss)
     grad_image, grad_text, row_loss = call(
         late_kernel,
         "ssvvvvvvaa",
         [("a", whole, f32), ("a", whole, f32), ("v", (1, rows), f32)],
-        [pltpu.VMEM(partial, f32), pltpu.VMEM(whole, f32), copy_sems],
+        [pltpu.VMEM(partial, f32), pltpu.VMEM((rows, rows), low), pltpu.VMEM(whole, f32), copy_sems],
         {8: 0, 9: 1},
     )(role, numbers, lows, units, scales, accs, late_low, loss, grad_image, grad_text)
     return (row_loss.reshape(rows), grad_image, grad_text)

time: 98.8 us -> 96 us (0.972)
  starting transfers between devices: 24.6 us -> 20.3 us
  Pallas kernels: 28.8 us -> 25.8 us
  waiting for transfers between devices: 40.7 us -> 43.5 us
  other arithmetic: 1.85 us -> 4.01 us
    ppermute x8 -> x7, starting transfers between devices: 24.6 us -> 20.3 us  [send(): return lax.ppermute(x, AXES, pairs())]
    ppermute x8 -> x7, waiting for transfers between devices: 40.7 us -> 43.5 us  [send(): return lax.ppermute(x, AXES, pairs())]
    pallas_call x1, Pallas kernels: 9.78 us -> 7.44 us  [body(): call(middle_kernel, 'ssvvvvvvv', [('v', both, f32), ('v', partial, f32)],...]
    pallas_call x1, Pallas kernels: 5.7 us -> 4.61 us  [body(): call(early_kernel, 'ssvvvvvvv', [('a', whole, f32), ('a', whole, f32), ('...]
    select_n x1, other arithmetic: 0.13 us -> 1.15 us  [body(): main = jnp.where(is_core_1, text_late, image_late)]
    select_n x1, other arithmetic: 1.57 us -> 2.58 us  [body(): jnp.where(is_core_1, image_emb, text_emb)]
  transfers between devices with their start and end apart: 8 -> 7, of which waited for: 4 -> 4; matrix products, arithmetic and copies ran while one was open for 0% -> 1% of each run, Pallas kernels for 24% -> 22%
where the time goes in v5:
time: 96 us; the launch traced here: 95.9 us
  waiting for transfers between devices  43.5 us (45%)
  Pallas kernels  25.8 us (27%)
  starting transfers between devices  20.3 us (21%)
  other arithmetic  4.01 us (4%)
  between operations  2.28 us (2%)
    ppermute x7, waiting for transfers between devices, send(): return lax.ppermute(x, AXES, pairs())  43.5 us
    ppermute x7, starting transfers between devices, send(): return lax.ppermute(x, AXES, pairs())  20.3 us
    pallas_call x1, Pallas kernels, body(): call(first_kernel, 'ssvvv', [('v', both, low), ('v', both, f32), ('v', (2...  7.89 us
    pallas_call x1, Pallas kernels, body(): call(middle_kernel, 'ssvvvvvvv', [('v', both, f32), ('v', partial, f32)],...  7.44 us
    pallas_call x1, Pallas kernels, body(): call(late_kernel, 'ssvvvvvvaa', [('a', whole, f32), ('a', whole, f32), ('...  4.97 us
    pallas_call x1, Pallas kernels, body(): call(early_kernel, 'ssvvvvvvv', [('a', whole, f32), ('a', whole, f32), ('...  4.61 us
    select_n x1, other arithmetic, body(): jnp.where(is_core_1, image_emb, text_emb)  2.58 us
  transfers between devices with their start and end apart: 7, of which 4 were waited for; matrix products, arithmetic and copies ran while one was open for 1% of the time, Pallas kernels for 22%

profile of v5, /device:TPU:0, one launch (start us, length us, event | category | flops | bytes accessed | tf_op | source)
XLA Modules:
  0.0 95.9 jit_solution(4224795821608310294)
XLA Ops:
  0.7 2.6 %broadcast_select_fusion.2.other = bf16[512,1152]{1,0:T(8,128)(2,1)} fusion(bf16[512,1152]{1,0:T(8,128)(2,1)} %param.4, bf16[512,1152]{1,0:T(8,128)(2,1)} %param.5, pred[]{:T(512)S(6)} %eq.10), kind=kLoop, calls=%fused_computation.2 | loop fusion | flops 589824 | bytes 3538945 | tf_op jit(solution)/shard_map/jit(_where)/select_n | solution.py:223
  3.3 0.0 collective-permute-start
  3.3 1.1 %broadcast_select_fusion.1.main = bf16[512,1152]{1,0:T(8,128)(2,1)} fusion(bf16[512,1152]{1,0:T(8,128)(2,1)S(1)} %copy-done, bf16[512,1152]{1,0:T(8,128)(2,1)S(1)} %copy-done.1, pred[]{:T(512)S(6)} %eq.10), kind=kLoop, calls=%fused_computation.1 | loop fusion | flops 589824 | bytes 3538945 | tf_op jit(solution)/shard_map/jit(_where)/select_n | solution.py:224
  4.4 10.8 %collective-permute-start.2 = (bf16[512,1152]{1,0:T(8,128)(2,1)}, bf16[512,1152]{1,0:T(8,128)(2,1)S(1)}, u32[]{:S(2)}, u32[]{:S(2)}) collective-permute-start(bf16[512,1152]{1,0:T(8,128)(2,1)} %broadcast_select_fusion.1.main), channel_id=1, source_target_pairs={{0,255},{3,4},{4,3},{7,8},{8,7},{11,12},{12,11},{15,16},{16,15},{1... | collective-permute-start | bytes 3538952 | tf_op jit(solution)/shard_map/ppermute | solution.py:33
  15.2 0.1 collective-permute-start.1
  15.3 1.5 %collective-permute-start.3 = (bf16[512,1152]{1,0:T(8,128)(2,1)}, bf16[512,1152]{1,0:T(8,128)(2,1)S(1)}, u32[]{:S(2)}, u32[]{:S(2)}) collective-permute-start(bf16[512,1152]{1,0:T(8,128)(2,1)} %broadcast_select_fusion.2.other), channel_id=1, source_target_pairs={{0,1},{1,4},{2,255},{3,2},{4,5},{5,8},{6,3},{7,6},{8,9},{9,12},{10... | collective-permute-start | bytes 3538952 | tf_op jit(solution)/shard_map/ppermute | solution.py:33
  18.1 0.1 pad_add_fusion.role_ref
  18.2 0.1 pad_maximum_fusion.numbers_ref
  18.3 0.0 collective-permute-done.swapped
  18.3 7.9 %shard_map.67 = (bf16[2,512,1152]{2,1,0:T(8,128)(2,1)S(1)}, f32[2,512,1152]{2,1,0:T(8,128)S(1)}, f32[2,512,1]{2,1,0:T(8,128)S(1)}, f32[2,512,1152]{2,1,0:T(8,128)S(1)}, f32[512,128]{1,0:T(8,128)S(1)}) custom-call(s32[2]{0:T(128)S(1)} %pad_add_fusion.role_ref, f32[2]{0:T(128)S(1)} %pad_maximum_fusion.numbers_ref, ...), custom_call_target="tpu_custom_call" | custom-call | tf_op jit(solution)/shard_map/pallas_call | solution.py:233
  26.2 15.3 %collective-permute-done.2.near_main = bf16[512,1152]{1,0:T(8,128)(2,1)S(1)} collective-permute-done((bf16[512,1152]{1,0:T(8,128)(2,1)}, bf16[512,1152]{1,0:T(8,128)(2,1)S(1)}, u32[]{:S(2)}, u32[]{:S(2)}) %collective-permute-start.2) | collective-permute-done | bytes 1179680 | tf_op jit(solution)/shard_map/ppermute | solution.py:33
  41.5 14.0 %collective-permute-done.1.second = bf16[512,1152]{1,0:T(8,128)(2,1)S(1)} collective-permute-done((bf16[512,1152]{1,0:T(8,128)(2,1)}, bf16[512,1152]{1,0:T(8,128)(2,1)S(1)}, u32[]{:S(2)}, u32[]{:S(2)}) %collective-permute-start.1) | collective-permute-done | bytes 1179680 | tf_op jit(solution)/shard_map/ppermute | solution.py:33
  55.5 0.9 shard_map.68
  56.4 0.0 collective-permute-done.3.of_other
  56.5 0.1 broadcast_select_fusion
  56.6 0.1 collective-permute-start.4
  56.7 7.8 %collective-permute-start.6 = (bf16[512,1152]{1,0:T(8,128)(2,1)S(1)}, bf16[512,1152]{1,0:T(8,128)(2,1)S(1)}, u32[]{:S(2)}, u32[]{:S(2)}) collective-permute-start(bf16[512,1152]{1,0:T(8,128)(2,1)S(1)} %collective-permute-done.3.of_other), channel_id=1, source_target_pairs={{0,254},{3,5},{4,2},{7,9},{8,6},{11,13},{12,10},{15,17},{16,14},{1... | collective-permute-start | bytes 3538952 | tf_op jit(solution)/shard_map/ppermute | solution.py:33
  64.5 0.1 collective-permute-start.5
  64.6 0.0 collective-permute-done.4.swapped
  64.6 7.4 %shard_map.69 = (f32[2,512,1152]{2,1,0:T(8,128)S(1)}, f32[512,128]{1,0:T(8,128)S(1)}) custom-call(s32[2]{0:T(128)S(1)} %pad_add_fusion.role_ref, f32[2]{0:T(128)S(1)} %pad_maximum_fusion.numbers_ref, bf16[2,512,1152]{2,1,0:T(8,128)(2,1)S(1)} %get-tuple-element.27.lows, ...), custom_call_target="tpu_custom_call", output_to_operand_aliasing={{0}: (7, {}), {1}: (8, {})} | custom-call | tf_op jit(solution)/shard_map/pallas_call | solution.py:247
  72.0 6.1 %collective-permute-done.6.by_two = bf16[512,1152]{1,0:T(8,128)(2,1)S(1)} collective-permute-done((bf16[512,1152]{1,0:T(8,128)(2,1)S(1)}, bf16[512,1152]{1,0:T(8,128)(2,1)S(1)}, u32[]{:S(2)}, u32[]{:S(2)}) %collective-permute-start.6) | collective-permute-done | bytes 1179680 | tf_op jit(solution)/shard_map/ppermute | solution.py:33
  78.1 4.6 %shard_map.70 = (f32[512,1152]{1,0:T(8,128)}, f32[512,1152]{1,0:T(8,128)}, f32[512,128]{1,0:T(8,128)S(1)}) custom-call(s32[2]{0:T(128)S(1)} %pad_add_fusion.role_ref, f32[2]{0:T(128)S(1)} %pad_maximum_fusion.numbers_ref, bf16[2,512,1152]{2,1,0:T(8,128)(2,1)S(1)} %get-tuple-element.27.lows, ...), custom_call_target="tpu_custom_call", output_to_operand_aliasing={{2}: (8, {})} | custom-call | tf_op jit(solution)/shard_map/pallas_call | solution.py:256
  82.7 8.0 %collective-permute-done.5.late_low = bf16[512,1152]{1,0:T(8,128)(2,1)S(1)} collective-permute-done((bf16[512,1152]{1,0:T(8,128)(2,1)S(1)}, bf16[512,1152]{1,0:T(8,128)(2,1)S(1)}, u32[]{:S(2)}, u32[]{:S(2)}) %collective-permute-start.5) | collective-permute-done | bytes 1179680 | tf_op jit(solution)/shard_map/ppermute | solution.py:33
  90.7 5.0 %shard_map.71 = (f32[512,1152]{1,0:T(8,128)}, f32[512,1152]{1,0:T(8,128)}, f32[1,512]{1,0:T(1,128)}) custom-call(s32[2]{0:T(128)S(1)} %pad_add_fusion.role_ref, f32[2]{0:T(128)S(1)} %pad_maximum_fusion.numbers_ref, bf16[2,512,1152]{2,1,0:T(8,128)(2,1)S(1)} %get-tuple-element.27.lows, ...), custom_call_target="tpu_custom_call", output_to_operand_aliasing={{0}: (8, {}), {1}: (9, {})} | custom-call | tf_op jit(solution)/shard_map/pallas_call | solution.py:263
  (4 shorter events, 0.0 us)
Async XLA Ops:
  0.7 2.6 %copy-start = (bf16[512,1152]{1,0:T(8,128)(2,1)S(1)}, bf16[512,1152]{1,0:T(8,128)(2,1)}, u32[]{:S(2)}) copy-start(bf16[512,1152]{1,0:T(8,128)(2,1)} %param.5) | copy-start | bytes 3538948
  0.7 2.6 %copy-start.1 = (bf16[512,1152]{1,0:T(8,128)(2,1)S(1)}, bf16[512,1152]{1,0:T(8,128)(2,1)}, u32[]{:S(2)}) copy-start(bf16[512,1152]{1,0:T(8,128)(2,1)} %param.4) | copy-start | bytes 3538948
  3.3 15.0 %collective-permute-start = (bf16[512,1152]{1,0:T(8,128)(2,1)}, bf16[512,1152]{1,0:T(8,128)(2,1)}, u32[]{:S(2)}, u32[]{:S(2)}) collective-permute-start(bf16[512,1152]{1,0:T(8,128)(2,1)} %broadcast_select_fusion.2.other), channel_id=1, source_target_pairs={{0,2},{1,3},{2,0},{3,1},{4,6},{5,7},{6,4},{7,5},{8,10},{9,11},{10,... | collective-permute-start | bytes 3538952 | tf_op jit(solution)/shard_map/ppermute | solution.py:33
  4.4 37.1 %collective-permute-start.2 = (bf16[512,1152]{1,0:T(8,128)(2,1)}, bf16[512,1152]{1,0:T(8,128)(2,1)S(1)}, u32[]{:S(2)}, u32[]{:S(2)}) collective-permute-start(bf16[512,1152]{1,0:T(8,128)(2,1)} %broadcast_select_fusion.1.main), channel_id=1, source_target_pairs={{0,255},{3,4},{4,3},{7,8},{8,7},{11,12},{12,11},{15,16},{16,15},{1... | collective-permute-start | bytes 3538952 | tf_op jit(solution)/shard_map/ppermute | solution.py:33
  15.2 40.3 %collective-permute-start.1 = (bf16[512,1152]{1,0:T(8,128)(2,1)}, bf16[512,1152]{1,0:T(8,128)(2,1)S(1)}, u32[]{:S(2)}, u32[]{:S(2)}) collective-permute-start(bf16[512,1152]{1,0:T(8,128)(2,1)} %broadcast_select_fusion.1.main), channel_id=1, source_target_pairs={{0,254},{1,255},{2,4},{3,5},{4,2},{5,3},{6,8},{7,9},{8,6},{9,7},{1... | collective-permute-start | bytes 3538952 | tf_op jit(solution)/shard_map/ppermute | solution.py:33
  15.3 41.1 %collective-permute-start.3 = (bf16[512,1152]{1,0:T(8,128)(2,1)}, bf16[512,1152]{1,0:T(8,128)(2,1)S(1)}, u32[]{:S(2)}, u32[]{:S(2)}) collective-permute-start(bf16[512,1152]{1,0:T(8,128)(2,1)} %broadcast_select_fusion.2.other), channel_id=1, source_target_pairs={{0,1},{1,4},{2,255},{3,2},{4,5},{5,8},{6,3},{7,6},{8,9},{9,12},{10... | collective-permute-start | bytes 3538952 | tf_op jit(solution)/shard_map/ppermute | solution.py:33
  56.6 8.0 %collective-permute-start.4 = (bf16[512,1152]{1,0:T(8,128)(2,1)S(1)}, bf16[512,1152]{1,0:T(8,128)(2,1)S(1)}, u32[]{:S(2)}, u32[]{:S(2)}) collective-permute-start(bf16[512,1152]{1,0:T(8,128)(2,1)S(1)} %broadcast_select_fusion), channel_id=1, source_target_pairs={{0,2},{1,3},{2,0},{3,1},{4,6},{5,7},{6,4},{7,5},{8,10},{9,11},{10,... | collective-permute-start | bytes 3538952 | tf_op jit(solution)/shard_map/ppermute | solution.py:33
  56.7 21.4 %collective-permute-start.6 = (bf16[512,1152]{1,0:T(8,128)(2,1)S(1)}, bf16[512,1152]{1,0:T(8,128)(2,1)S(1)}, u32[]{:S(2)}, u32[]{:S(2)}) collective-permute-start(bf16[512,1152]{1,0:T(8,128)(2,1)S(1)} %collective-permute-done.3.of_other), channel_id=1, source_target_pairs={{0,254},{3,5},{4,2},{7,9},{8,6},{11,13},{12,10},{15,17},{16,14},{1... | collective-permute-start | bytes 3538952 | tf_op jit(solution)/shard_map/ppermute | solution.py:33
  64.5 26.3 %collective-permute-start.5 = (bf16[512,1152]{1,0:T(8,128)(2,1)S(1)}, bf16[512,1152]{1,0:T(8,128)(2,1)S(1)}, u32[]{:S(2)}, u32[]{:S(2)}) collective-permute-start(bf16[512,1152]{1,0:T(8,128)(2,1)S(1)} %shard_map.68), channel_id=1, source_target_pairs={{0,255},{1,254},{2,5},{3,4},{4,3},{5,2},{6,9},{7,8},{8,7},{9,6},{1... | collective-permute-start | bytes 3538952 | tf_op jit(solution)/shard_map/ppermute | solution.py:33

commit v6 on v5

--- a/solution.py
+++ b/solution.py
@@ -131,11 +131,11 @@
 
 
 def middle_kernel(
-    role_ref, numbers_ref, lows, near_main, second, of_other, swapped, accs_in, loss_in, accs, loss_ref, low_ref
+    role_ref, numbers_ref, lows, near, second, swapped, accs_in, loss_in, accs, loss_ref, low_ref
 ):
     on_other = role_ref[0].astype(jnp.float32)
     on_main = 1.0 - on_other
-    lower_one_of(role_ref[0] == role_ref[1], near_main, of_other, low_ref)
+    lower(near, low_ref)
     pair(numbers_ref, lows.at[0], low_ref, accs_in.at[0], accs.at[0], loss_in, loss_ref, on_main)
     lower(second, low_ref)
     pair(numbers_ref, lows.at[0], low_ref, accs.at[0], accs.at[0], loss_ref, loss_ref, on_main)
@@ -220,8 +220,9 @@
     role = jnp.stack([core, place % 2]).astype(jnp.int32)
     numbers = jnp.stack([jnp.exp(log_temp), bias])
     is_core_1 = core == 1
-    other, image_late, text_late = together(jnp.where(is_core_1, image_emb, text_emb), image_emb, text_emb)
-    main = jnp.where(is_core_1, text_late, image_late)
+    main = jnp.where(is_core_1, text_emb, image_emb)
+    other = jnp.where(is_core_1, image_emb, text_emb)
+    main, other = together(main, other)
 
     swapped = send(other, SWAP)
     of_other = send(other, OF_OTHER)
@@ -242,15 +243,16 @@
     of_other, late_low = together(of_other, late_low)
     by_two = send(of_other, ON_BY_TWO)
     late_low = send(late_low, FAR_OR_ON_BY_ONE)
-    swapped = send(jnp.where(core == place % 2, near_main, of_other), SWAP)
+    near = jnp.where(core == place % 2, near_main, of_other)
+    swapped = send(near, SWAP)
 
     accs, loss = call(
         middle_kernel,
-        "ssvvvvvvv",
+        "ssvvvvvv",
         [("v", both, f32), ("v", partial, f32)],
         [pltpu.VMEM(whole, low)],
-        {7: 0, 8: 1},
-    )(role, numbers, lows, near_main, second, of_other, swapped, accs, loss)
+        {6: 0, 7: 1},
+    )(role, numbers, lows, near, second, swapped, accs, loss)
 
     copy_sems = pltpu.SemaphoreType.DMA((rows // STRIP,))
     grad_image, grad_text, loss = call(

time: 96 us -> 95.6 us (level)
    select_n x3 -> x2, other arithmetic: 3.86 us -> 3.26 us  [the longest x1 1.84 us: body(): other = jnp.where(is_core_1, image_emb, text_emb)]
  transfers between devices with their start and end apart: 7 -> 7, of which waited for: 4 -> 4; matrix products, arithmetic and copies ran while one was open for 1% -> 0% of each run, Pallas kernels for 22% -> 22%
where the time goes in v6:
time: 95.6 us; the launch traced here: 95.3 us
  waiting for transfers between devices  43.3 us (45%)
  Pallas kernels  25.7 us (27%)
  starting transfers between devices  20.7 us (22%)
  other arithmetic  3.41 us (4%)
  between operations  2.27 us (2%)
    ppermute x7, waiting for transfers between devices, send(): return lax.ppermute(x, AXES, pairs())  43.3 us
    ppermute x7, starting transfers between devices, send(): return lax.ppermute(x, AXES, pairs())  20.7 us
    pallas_call x1, Pallas kernels, body(): call(middle_kernel, 'ssvvvvvv', [('v', both, f32), ('v', partial, f32)],...  7.24 us
    pallas_call x1, Pallas kernels, body(): call(first_kernel, 'ssvvv', [('v', both, low), ('v', both, f32), ('v', (2...  7.18 us
    pallas_call x1, Pallas kernels, body(): call(early_kernel, 'ssvvvvvvv', [('a', whole, f32), ('a', whole, f32), ('...  5.35 us
    pallas_call x1, Pallas kernels, body(): call(late_kernel, 'ssvvvvvvaa', [('a', whole, f32), ('a', whole, f32), ('...  4.97 us
  transfers between devices with their start and end apart: 7, of which 4 were waited for; matrix products, arithmetic and copies ran while one was open for 0% of the time, Pallas kernels for 22%

profile of v6, /device:TPU:0, one launch (start us, length us, event | category | flops | bytes accessed | tf_op | source)
XLA Modules:
  0.0 95.3 jit_solution(11120969565630752570)
XLA Ops:
  0.7 1.8 %broadcast_select_fusion.1 = (bf16[512,1152]{1,0:T(8,128)(2,1)S(1)}, bf16[512,1152]{1,0:T(8,128)(2,1)S(1)}) fusion(bf16[512,1152]{1,0:T(8,128)(2,1)} %param.4, bf16[512,1152]{1,0:T(8,128)(2,1)} %param.5, pred[]{:T(512)S(6)} %eq.10), kind=kLoop, calls=%fused_computation.1 | loop fusion | flops 1179648 | bytes 4718593 | tf_op jit(solution)/shard_map/jit(_where)/select_n | solution.py:224
  2.5 0.1 collective-permute-start
  2.6 10.8 %collective-permute-start.2 = (bf16[512,1152]{1,0:T(8,128)(2,1)S(1)}, bf16[512,1152]{1,0:T(8,128)(2,1)}, u32[]{:S(2)}, u32[]{:S(2)}) collective-permute-start(bf16[512,1152]{1,0:T(8,128)(2,1)S(1)} %get-tuple-element.23.main), channel_id=1, source_target_pairs={{0,255},{3,4},{4,3},{7,8},{8,7},{11,12},{12,11},{15,16},{16,15},{1... | collective-permute-start | bytes 3538952 | tf_op jit(solution)/shard_map/ppermute | solution.py:33
  13.4 0.1 collective-permute-start.1
  13.5 1.5 %collective-permute-start.3 = (bf16[512,1152]{1,0:T(8,128)(2,1)S(1)}, bf16[512,1152]{1,0:T(8,128)(2,1)}, u32[]{:S(2)}, u32[]{:S(2)}) collective-permute-start(bf16[512,1152]{1,0:T(8,128)(2,1)S(1)} %get-tuple-element.24.other), channel_id=1, source_target_pairs={{0,1},{1,4},{2,255},{3,2},{4,5},{5,8},{6,3},{7,6},{8,9},{9,12},{10... | collective-permute-start | bytes 3538952 | tf_op jit(solution)/shard_map/ppermute | solution.py:33
  16.3 0.1 pad_add_fusion.role_ref
  16.4 0.1 pad_maximum_fusion.numbers_ref
  16.4 0.0 collective-permute-done.swapped
  16.4 7.2 %shard_map.67 = (bf16[2,512,1152]{2,1,0:T(8,128)(2,1)S(1)}, f32[2,512,1152]{2,1,0:T(8,128)S(1)}, f32[2,512,1]{2,1,0:T(8,128)S(1)}, f32[2,512,1152]{2,1,0:T(8,128)S(1)}, f32[512,128]{1,0:T(8,128)S(1)}) custom-call(s32[2]{0:T(128)S(1)} %pad_add_fusion.role_ref, f32[2]{0:T(128)S(1)} %pad_maximum_fusion.numbers_ref, ...), custom_call_target="tpu_custom_call" | custom-call | tf_op jit(solution)/shard_map/pallas_call | solution.py:234
  23.6 15.7 %collective-permute-done.2 = bf16[512,1152]{1,0:T(8,128)(2,1)} collective-permute-done((bf16[512,1152]{1,0:T(8,128)(2,1)S(1)}, bf16[512,1152]{1,0:T(8,128)(2,1)}, u32[]{:S(2)}, u32[]{:S(2)}) %collective-permute-start.2) | collective-permute-done | bytes 1179680 | tf_op jit(solution)/shard_map/ppermute | solution.py:33
  39.4 14.0 %collective-permute-done.1.second = bf16[512,1152]{1,0:T(8,128)(2,1)S(1)} collective-permute-done((bf16[512,1152]{1,0:T(8,128)(2,1)S(1)}, bf16[512,1152]{1,0:T(8,128)(2,1)S(1)}, u32[]{:S(2)}, u32[]{:S(2)}) %collective-permute-start.1) | collective-permute-done | bytes 1179680 | tf_op jit(solution)/shard_map/ppermute | solution.py:33
  53.4 0.9 shard_map.68
  54.3 0.0 collective-permute-done.3.of_other
  54.3 1.4 %broadcast_select_fusion.near = bf16[512,1152]{1,0:T(8,128)(2,1)S(1)} fusion(bf16[512,1152]{1,0:T(8,128)(2,1)} %collective-permute-done.2, bf16[512,1152]{1,0:T(8,128)(2,1)} %collective-permute-done.3.of_other, pred[]{:T(512)S(6)} %eq.11), kind=kLoop, calls=%fused_computation | loop fusion | flops 589824 | bytes 3538945 | tf_op jit(solution)/shard_map/jit(_where)/select_n | solution.py:246
  55.7 0.1 collective-permute-start.4
  55.8 7.9 %collective-permute-start.6 = (bf16[512,1152]{1,0:T(8,128)(2,1)}, bf16[512,1152]{1,0:T(8,128)(2,1)S(1)}, u32[]{:S(2)}, u32[]{:S(2)}) collective-permute-start(bf16[512,1152]{1,0:T(8,128)(2,1)} %collective-permute-done.3.of_other), channel_id=1, source_target_pairs={{0,254},{3,5},{4,2},{7,9},{8,6},{11,13},{12,10},{15,17},{16,14},{1... | collective-permute-start | bytes 3538952 | tf_op jit(solution)/shard_map/ppermute | solution.py:33
  63.7 0.3 collective-permute-start.5
  64.0 0.0 collective-permute-done.4.swapped
  64.0 7.2 %shard_map.69 = (f32[2,512,1152]{2,1,0:T(8,128)S(1)}, f32[512,128]{1,0:T(8,128)S(1)}) custom-call(s32[2]{0:T(128)S(1)} %pad_add_fusion.role_ref, f32[2]{0:T(128)S(1)} %pad_maximum_fusion.numbers_ref, bf16[2,512,1152]{2,1,0:T(8,128)(2,1)S(1)} %get-tuple-element.25.lows, ...), custom_call_target="tpu_custom_call", output_to_operand_aliasing={{0}: (6, {}), {1}: (7, {})} | custom-call | tf_op jit(solution)/shard_map/pallas_call | solution.py:249
  71.3 6.4 %collective-permute-done.6.by_two = bf16[512,1152]{1,0:T(8,128)(2,1)S(1)} collective-permute-done((bf16[512,1152]{1,0:T(8,128)(2,1)}, bf16[512,1152]{1,0:T(8,128)(2,1)S(1)}, u32[]{:S(2)}, u32[]{:S(2)}) %collective-permute-start.6) | collective-permute-done | bytes 1179680 | tf_op jit(solution)/shard_map/ppermute | solution.py:33
  77.7 5.4 %shard_map.70 = (f32[512,1152]{1,0:T(8,128)}, f32[512,1152]{1,0:T(8,128)}, f32[512,128]{1,0:T(8,128)S(1)}) custom-call(s32[2]{0:T(128)S(1)} %pad_add_fusion.role_ref, f32[2]{0:T(128)S(1)} %pad_maximum_fusion.numbers_ref, bf16[2,512,1152]{2,1,0:T(8,128)(2,1)S(1)} %get-tuple-element.25.lows, ...), custom_call_target="tpu_custom_call", output_to_operand_aliasing={{2}: (8, {})} | custom-call | tf_op jit(solution)/shard_map/pallas_call | solution.py:258
  83.0 7.2 %collective-permute-done.5.late_low = bf16[512,1152]{1,0:T(8,128)(2,1)S(1)} collective-permute-done((bf16[512,1152]{1,0:T(8,128)(2,1)S(1)}, bf16[512,1152]{1,0:T(8,128)(2,1)S(1)}, u32[]{:S(2)}, u32[]{:S(2)}) %collective-permute-start.5) | collective-permute-done | bytes 1179680 | tf_op jit(solution)/shard_map/ppermute | solution.py:33
  90.2 5.0 %shard_map.71 = (f32[512,1152]{1,0:T(8,128)}, f32[512,1152]{1,0:T(8,128)}, f32[1,512]{1,0:T(1,128)}) custom-call(s32[2]{0:T(128)S(1)} %pad_add_fusion.role_ref, f32[2]{0:T(128)S(1)} %pad_maximum_fusion.numbers_ref, bf16[2,512,1152]{2,1,0:T(8,128)(2,1)S(1)} %get-tuple-element.25.lows, ...), custom_call_target="tpu_custom_call", output_to_operand_aliasing={{0}: (8, {}), {1}: (9, {})} | custom-call | tf_op jit(solution)/shard_map/pallas_call | solution.py:265
Async XLA Ops:
  2.5 13.9 %collective-permute-start = (bf16[512,1152]{1,0:T(8,128)(2,1)S(1)}, bf16[512,1152]{1,0:T(8,128)(2,1)}, u32[]{:S(2)}, u32[]{:S(2)}) collective-permute-start(bf16[512,1152]{1,0:T(8,128)(2,1)S(1)} %get-tuple-element.24.other), channel_id=1, source_target_pairs={{0,2},{1,3},{2,0},{3,1},{4,6},{5,7},{6,4},{7,5},{8,10},{9,11},{10,... | collective-permute-start | bytes 3538952 | tf_op jit(solution)/shard_map/ppermute | solution.py:33
  2.6 36.7 %collective-permute-start.2 = (bf16[512,1152]{1,0:T(8,128)(2,1)S(1)}, bf16[512,1152]{1,0:T(8,128)(2,1)}, u32[]{:S(2)}, u32[]{:S(2)}) collective-permute-start(bf16[512,1152]{1,0:T(8,128)(2,1)S(1)} %get-tuple-element.23.main), channel_id=1, source_target_pairs={{0,255},{3,4},{4,3},{7,8},{8,7},{11,12},{12,11},{15,16},{16,15},{1... | collective-permute-start | bytes 3538952 | tf_op jit(solution)/shard_map/ppermute | solution.py:33
  13.4 40.0 %collective-permute-start.1 = (bf16[512,1152]{1,0:T(8,128)(2,1)S(1)}, bf16[512,1152]{1,0:T(8,128)(2,1)S(1)}, u32[]{:S(2)}, u32[]{:S(2)}) collective-permute-start(bf16[512,1152]{1,0:T(8,128)(2,1)S(1)} %get-tuple-element.23.main), channel_id=1, source_target_pairs={{0,254},{1,255},{2,4},{3,5},{4,2},{5,3},{6,8},{7,9},{8,6},{9,7},{1... | collective-permute-start | bytes 3538952 | tf_op jit(solution)/shard_map/ppermute | solution.py:33
  13.5 40.8 %collective-permute-start.3 = (bf16[512,1152]{1,0:T(8,128)(2,1)S(1)}, bf16[512,1152]{1,0:T(8,128)(2,1)}, u32[]{:S(2)}, u32[]{:S(2)}) collective-permute-start(bf16[512,1152]{1,0:T(8,128)(2,1)S(1)} %get-tuple-element.24.other), channel_id=1, source_target_pairs={{0,1},{1,4},{2,255},{3,2},{4,5},{5,8},{6,3},{7,6},{8,9},{9,12},{10... | collective-permute-start | bytes 3538952 | tf_op jit(solution)/shard_map/ppermute | solution.py:33
  55.7 8.3 %collective-permute-start.4 = (bf16[512,1152]{1,0:T(8,128)(2,1)S(1)}, bf16[512,1152]{1,0:T(8,128)(2,1)S(1)}, u32[]{:S(2)}, u32[]{:S(2)}) collective-permute-start(bf16[512,1152]{1,0:T(8,128)(2,1)S(1)} %broadcast_select_fusion.near), channel_id=1, source_target_pairs={{0,2},{1,3},{2,0},{3,1},{4,6},{5,7},{6,4},{7,5},{8,10},{9,11},{10,... | collective-permute-start | bytes 3538952 | tf_op jit(solution)/shard_map/ppermute | solution.py:33
  55.8 21.8 %collective-permute-start.6 = (bf16[512,1152]{1,0:T(8,128)(2,1)}, bf16[512,1152]{1,0:T(8,128)(2,1)S(1)}, u32[]{:S(2)}, u32[]{:S(2)}) collective-permute-start(bf16[512,1152]{1,0:T(8,128)(2,1)} %collective-permute-done.3.of_other), channel_id=1, source_target_pairs={{0,254},{3,5},{4,2},{7,9},{8,6},{11,13},{12,10},{15,17},{16,14},{1... | collective-permute-start | bytes 3538952 | tf_op jit(solution)/shard_map/ppermute | solution.py:33
  63.7 26.5 %collective-permute-start.5 = (bf16[512,1152]{1,0:T(8,128)(2,1)S(1)}, bf16[512,1152]{1,0:T(8,128)(2,1)S(1)}, u32[]{:S(2)}, u32[]{:S(2)}) collective-permute-start(bf16[512,1152]{1,0:T(8,128)(2,1)S(1)} %shard_map.68), channel_id=1, source_target_pairs={{0,255},{1,254},{2,5},{3,4},{4,3},{5,2},{6,9},{7,8},{8,7},{9,6},{1... | collective-permute-start | bytes 3538952 | tf_op jit(solution)/shard_map/ppermute | solution.py:33

commit v7 on v6

--- a/solution.py
+++ b/solution.py
@@ -25,7 +25,8 @@
 SECOND = by_role({0: -2, 1: -2, 4: -2, 5: -2, 2: 2, 3: 2, 6: 2, 7: 2})
 OF_OTHER = by_role({1: 3, 5: 3, 2: -3, 6: -3, 0: 1, 4: 1, 3: -1, 7: -1})
 NEAR_OF_MAIN = by_role({0: -1, 4: -1, 3: 1, 7: 1})
-ON_BY_TWO = by_role({0: -2, 4: -2, 3: 2, 7: 2})
+NEAR_TO_INNER = by_role({0: 2, 4: 2, 3: -2, 7: -2})
+ON_OR_TO_OUTER = by_role({0: -2, 4: -2, 3: 2, 7: 2, 1: 2, 5: 2, 2: -2, 6: -2})
 FAR_OR_ON_BY_ONE = by_role({1: -3, 5: -3, 2: 3, 6: 3, 0: -1, 4: -1, 3: 1, 7: 1})
 
 
@@ -131,16 +132,14 @@
 
 
 def middle_kernel(
-    role_ref, numbers_ref, lows, near, second, swapped, accs_in, loss_in, accs, loss_ref, low_ref
-):
-    on_other = role_ref[0].astype(jnp.float32)
-    on_main = 1.0 - on_other
-    lower(near, low_ref)
+    role_ref, numbers_ref, lows, near_main, second, of_other, accs_in, loss_in, accs, loss_ref, low_ref
+):
+    on_main = 1.0 - role_ref[0].astype(jnp.float32)
+    lower_one_of(role_ref[0] == role_ref[1], near_main, of_other, low_ref)
     pair(numbers_ref, lows.at[0], low_ref, accs_in.at[0], accs.at[0], loss_in, loss_ref, on_main)
     lower(second, low_ref)
     pair(numbers_ref, lows.at[0], low_ref, accs.at[0], accs.at[0], loss_ref, loss_ref, on_main)
-    lower(swapped, low_ref)
-    pair(numbers_ref, lows.at[1], low_ref, accs_in.at[1], accs.at[1], loss_ref, loss_ref, on_other)
+    accs[1] = accs_in[1]
 
 
 def close_side(
@@ -173,14 +172,20 @@
 
 
 def early_kernel(
-    role_ref, numbers_ref, lows, units, scales, accs, of_other, by_two, loss_in,
-    image_out, text_out, loss_ref, low_ref, weights_ref, done_ref, sems,
+    role_ref, numbers_ref, lows, units, scales, of_other, by_two, to_inner, accs_in, loss_in,
+    image_out, text_out, accs, loss_ref, low_ref, weights_ref, done_ref, sems,
 ):
     outer = role_ref[0] == role_ref[1]
+    lower_one_of(outer, by_two, to_inner, low_ref)
+    accs[0] = accs_in[0]
+    pair(
+        numbers_ref, lows.at[1], low_ref, accs_in.at[1], accs.at[1], loss_in, loss_ref,
+        role_ref[0].astype(jnp.float32),
+    )
     lower_one_of(outer, of_other, by_two, low_ref)
     close_side(
         jnp.where(outer, 0, 1), role_ref[0], numbers_ref, lows, units, scales, accs, low_ref,
-        loss_in, loss_ref, image_out, text_out, weights_ref, done_ref, sems,
+        loss_ref, loss_ref, image_out, text_out, weights_ref, done_ref, sems,
     )
 
 
@@ -241,10 +246,9 @@
     second, near_main, loss = together(second, near_main, loss)
     (late_low,) = call(late_block_kernel, "svv", [("v", whole, low)])(role, lows, second)
     of_other, late_low = together(of_other, late_low)
-    by_two = send(of_other, ON_BY_TWO)
+    by_two = send(of_other, ON_OR_TO_OUTER)
     late_low = send(late_low, FAR_OR_ON_BY_ONE)
-    near = jnp.where(core == place % 2, near_main, of_other)
-    swapped = send(near, SWAP)
+    to_inner = send(near_main, NEAR_TO_INNER)
 
     accs, loss = call(
         middle_kernel,
@@ -252,16 +256,16 @@
         [("v", both, f32), ("v", partial, f32)],
         [pltpu.VMEM(whole, low)],
         {6: 0, 7: 1},
-    )(role, numbers, lows, near, second, swapped, accs, loss)
+    )(role, numbers, lows, near_main, second, of_other, accs, loss)
 
     copy_sems = pltpu.SemaphoreType.DMA((rows // STRIP,))
-    grad_image, grad_text, loss = call(
+    grad_image, grad_text, accs, loss = call(
         early_kernel,
-        "ssvvvvvvv",
-        [("a", whole, f32), ("a", whole, f32), ("v", partial, f32)],
+        "ssvvvvvvvv",
+        [("a", whole, f32), ("a", whole, f32), ("v", both, f32), ("v", partial, f32)],
         [pltpu.VMEM(whole, low), pltpu.VMEM((rows, rows), low), pltpu.VMEM(whole, f32), copy_sems],
-        {8: 2},
-    )(role, numbers, lows, units, scales, accs, of_other, by_two, loss)
+        {8: 2, 9: 3},
+    )(role, numbers, lows, units, scales, of_other, by_two, to_inner, accs, loss)
     grad_image, grad_text, row_loss = call(
         late_kernel,
         "ssvvvvvvaa",

time: 95.6 us -> 92.9 us (0.972)
  waiting for transfers between devices: 43.3 us -> 40 us
  Pallas kernels: 25.7 us -> 27.3 us
    ppermute x7, waiting for transfers between devices: 43.3 us -> 40 us  [send(): return lax.ppermute(x, AXES, pairs())]
    pallas_call x1, Pallas kernels: 5.35 us -> 7.35 us  [body(): call(early_kernel, 'ssvvvvvvvv', [('a', whole, f32), ('a', whole, f32), (...]
    select_n x1 -> x0, other arithmetic: 1.42 us -> none  [body(): near = jnp.where(core == place % 2, near_main, of_other)]
    select_n x1, other arithmetic: 1.84 us -> 2.86 us  [body(): other = jnp.where(is_core_1, image_emb, text_emb)]
  transfers between devices with their start and end apart: 7 -> 7, of which waited for: 4 -> 4; matrix products, arithmetic and copies ran while one was open for 0% -> 0% of each run, Pallas kernels for 22% -> 24%
where the time goes in v7:
time: 92.9 us; the launch traced here: 92.6 us
  waiting for transfers between devices  40 us (43%)
  Pallas kernels  27.3 us (29%)
  starting transfers between devices  20.1 us (22%)
  other arithmetic  3.01 us (3%)
  between operations  2.23 us (2%)
    ppermute x7, waiting for transfers between devices, send(): return lax.ppermute(x, AXES, pairs())  40 us
    ppermute x7, starting transfers between devices, send(): return lax.ppermute(x, AXES, pairs())  20.1 us
    pallas_call x1, Pallas kernels, body(): call(first_kernel, 'ssvvv', [('v', both, low), ('v', both, f32), ('v', (2...  7.54 us
    pallas_call x1, Pallas kernels, body(): call(early_kernel, 'ssvvvvvvvv', [('a', whole, f32), ('a', whole, f32), (...  7.35 us
    pallas_call x1, Pallas kernels, body(): call(middle_kernel, 'ssvvvvvv', [('v', both, f32), ('v', partial, f32)],...  6.55 us
    pallas_call x1, Pallas kernels, body(): call(late_kernel, 'ssvvvvvvaa', [('a', whole, f32), ('a', whole, f32), ('...  4.98 us
    select_n x1, other arithmetic, body(): other = jnp.where(is_core_1, image_emb, text_emb)  2.86 us
  transfers between devices with their start and end apart: 7, of which 4 were waited for; matrix products, arithmetic and copies ran while one was open for 0% of the time, Pallas kernels for 24%

profile of v7, /device:TPU:0, one launch (start us, length us, event | category | flops | bytes accessed | tf_op | source)
XLA Modules:
  0.0 92.6 jit_solution(15197000532329664562)
XLA Ops:
  0.7 2.9 %broadcast_select_fusion = (bf16[512,1152]{1,0:T(8,128)(2,1)S(1)}, bf16[512,1152]{1,0:T(8,128)(2,1)}) fusion(bf16[512,1152]{1,0:T(8,128)(2,1)} %param.4, bf16[512,1152]{1,0:T(8,128)(2,1)} %param.5, pred[]{:T(512)S(6)} %eq.6), kind=kLoop, calls=%fused_computation | loop fusion | flops 1179648 | bytes 4718593 | tf_op jit(solution)/shard_map/jit(_where)/select_n | solution.py:229
  3.5 0.0 collective-permute-start
  3.5 10.8 %collective-permute-start.3 = (bf16[512,1152]{1,0:T(8,128)(2,1)}, bf16[512,1152]{1,0:T(8,128)(2,1)}, u32[]{:S(2)}, u32[]{:S(2)}) collective-permute-start(bf16[512,1152]{1,0:T(8,128)(2,1)} %get-tuple-element.24.main), channel_id=1, source_target_pairs={{0,255},{3,4},{4,3},{7,8},{8,7},{11,12},{12,11},{15,16},{16,15},{1... | collective-permute-start | bytes 3538952 | tf_op jit(solution)/shard_map/ppermute | solution.py:34
  14.3 0.1 collective-permute-start.2
  14.4 1.5 %collective-permute-start.1 = (bf16[512,1152]{1,0:T(8,128)(2,1)S(1)}, bf16[512,1152]{1,0:T(8,128)(2,1)S(1)}, u32[]{:S(2)}, u32[]{:S(2)}) collective-permute-start(bf16[512,1152]{1,0:T(8,128)(2,1)S(1)} %get-tuple-element.25.other), channel_id=1, source_target_pairs={{0,1},{1,4},{2,255},{3,2},{4,5},{5,8},{6,3},{7,6},{8,9},{9,12},{10... | collective-permute-start | bytes 3538952 | tf_op jit(solution)/shard_map/ppermute | solution.py:34
  17.2 0.1 pad_add_fusion.role_ref
  17.3 0.1 pad_maximum_fusion.numbers_ref
  17.4 0.0 collective-permute-done.swapped
  17.4 7.5 %shard_map.67 = (bf16[2,512,1152]{2,1,0:T(8,128)(2,1)S(1)}, f32[2,512,1152]{2,1,0:T(8,128)S(1)}, f32[2,512,1]{2,1,0:T(8,128)S(1)}, f32[2,512,1152]{2,1,0:T(8,128)S(1)}, f32[512,128]{1,0:T(8,128)S(1)}) custom-call(s32[2]{0:T(128)S(1)} %pad_add_fusion.role_ref, f32[2]{0:T(128)S(1)} %pad_maximum_fusion.numbers_ref, bf16[512,1152]{1,0:T(8,128)(2,1)} %get-tuple-element.24.main, ...), custom_call_target="tpu_custom_call" | custom-call | tf_op jit(solution)/shard_map/pallas_call | solution.py:239
  24.9 15.5 %collective-permute-done.3.near_main = bf16[512,1152]{1,0:T(8,128)(2,1)} collective-permute-done((bf16[512,1152]{1,0:T(8,128)(2,1)}, bf16[512,1152]{1,0:T(8,128)(2,1)}, u32[]{:S(2)}, u32[]{:S(2)}) %collective-permute-start.3) | collective-permute-done | bytes 1179680 | tf_op jit(solution)/shard_map/ppermute | solution.py:34
  40.4 13.9 %collective-permute-done.2.second = bf16[512,1152]{1,0:T(8,128)(2,1)S(1)} collective-permute-done((bf16[512,1152]{1,0:T(8,128)(2,1)}, bf16[512,1152]{1,0:T(8,128)(2,1)S(1)}, u32[]{:S(2)}, u32[]{:S(2)}) %collective-permute-start.2) | collective-permute-done | bytes 1179680 | tf_op jit(solution)/shard_map/ppermute | solution.py:34
  54.3 0.9 shard_map.68
  55.2 0.0 collective-permute-done.1.of_other
  55.2 5.9 %collective-permute-start.4 = (bf16[512,1152]{1,0:T(8,128)(2,1)S(1)}, bf16[512,1152]{1,0:T(8,128)(2,1)S(1)}, u32[]{:S(2)}, u32[]{:S(2)}) collective-permute-start(bf16[512,1152]{1,0:T(8,128)(2,1)S(1)} %collective-permute-done.1.of_other), channel_id=1, source_target_pairs={{0,254},{1,3},{2,0},{3,5},{4,2},{5,7},{6,4},{7,9},{8,6},{9,11},{10... | collective-permute-start | bytes 3538952 | tf_op jit(solution)/shard_map/ppermute | solution.py:34
  61.1 1.4 %collective-permute-start.5 = (bf16[512,1152]{1,0:T(8,128)(2,1)}, bf16[512,1152]{1,0:T(8,128)(2,1)S(1)}, u32[]{:S(2)}, u32[]{:S(2)}) collective-permute-start(bf16[512,1152]{1,0:T(8,128)(2,1)} %collective-permute-done.3.near_main), channel_id=1, source_target_pairs={{0,2},{3,1},{4,6},{7,5},{8,10},{11,9},{12,14},{15,13},{16,18},{19,... | collective-permute-start | bytes 3538952 | tf_op jit(solution)/shard_map/ppermute | solution.py:34
  62.5 0.5 collective-permute-start.6
  63.0 6.6 %shard_map.69 = (f32[2,512,1152]{2,1,0:T(8,128)S(1)}, f32[512,128]{1,0:T(8,128)S(1)}) custom-call(s32[2]{0:T(128)S(1)} %pad_add_fusion.role_ref, f32[2]{0:T(128)S(1)} %pad_maximum_fusion.numbers_ref, bf16[2,512,1152]{2,1,0:T(8,128)(2,1)S(1)} %get-tuple-element.26.lows, ...), custom_call_target="tpu_custom_call", output_to_operand_aliasing={{0}: (6, {}), {1}: (7, {})} | custom-call | tf_op jit(solution)/shard_map/pallas_call | solution.py:253
  69.6 5.3 %collective-permute-done.4.by_two = bf16[512,1152]{1,0:T(8,128)(2,1)S(1)} collective-permute-done((bf16[512,1152]{1,0:T(8,128)(2,1)S(1)}, bf16[512,1152]{1,0:T(8,128)(2,1)S(1)}, u32[]{:S(2)}, u32[]{:S(2)}) %collective-permute-start.4) | collective-permute-done | bytes 1179680 | tf_op jit(solution)/shard_map/ppermute | solution.py:34
  74.8 0.0 collective-permute-done.5.to_inner
  74.8 7.3 %shard_map.70 = (f32[512,1152]{1,0:T(8,128)}, f32[512,1152]{1,0:T(8,128)}, f32[2,512,1152]{2,1,0:T(8,128)S(1)}, f32[512,128]{1,0:T(8,128)S(1)}) custom-call(s32[2]{0:T(128)S(1)} %pad_add_fusion.role_ref, f32[2]{0:T(128)S(1)} %pad_maximum_fusion.numbers_ref, ...), custom_call_target="tpu_custom_call", output_to_operand_aliasing={{2}: (8, {}), {3}: (9, {})} | custom-call | tf_op jit(solution)/shard_map/pallas_call | solution.py:262
  82.2 5.3 %collective-permute-done.6.late_low = bf16[512,1152]{1,0:T(8,128)(2,1)S(1)} collective-permute-done((bf16[512,1152]{1,0:T(8,128)(2,1)S(1)}, bf16[512,1152]{1,0:T(8,128)(2,1)S(1)}, u32[]{:S(2)}, u32[]{:S(2)}) %collective-permute-start.6) | collective-permute-done | bytes 1179680 | tf_op jit(solution)/shard_map/ppermute | solution.py:34
  87.5 5.0 %shard_map.71 = (f32[512,1152]{1,0:T(8,128)}, f32[512,1152]{1,0:T(8,128)}, f32[1,512]{1,0:T(1,128)}) custom-call(s32[2]{0:T(128)S(1)} %pad_add_fusion.role_ref, f32[2]{0:T(128)S(1)} %pad_maximum_fusion.numbers_ref, bf16[2,512,1152]{2,1,0:T(8,128)(2,1)S(1)} %get-tuple-element.26.lows, ...), custom_call_target="tpu_custom_call", output_to_operand_aliasing={{0}: (8, {}), {1}: (9, {})} | custom-call | tf_op jit(solution)/shard_map/pallas_call | solution.py:269
Async XLA Ops:
  3.5 13.8 %collective-permute-start = (bf16[512,1152]{1,0:T(8,128)(2,1)S(1)}, bf16[512,1152]{1,0:T(8,128)(2,1)}, u32[]{:S(2)}, u32[]{:S(2)}) collective-permute-start(bf16[512,1152]{1,0:T(8,128)(2,1)S(1)} %get-tuple-element.25.other), channel_id=1, source_target_pairs={{0,2},{1,3},{2,0},{3,1},{4,6},{5,7},{6,4},{7,5},{8,10},{9,11},{10,... | collective-permute-start | bytes 3538952 | tf_op jit(solution)/shard_map/ppermute | solution.py:34
  3.5 36.9 %collective-permute-start.3 = (bf16[512,1152]{1,0:T(8,128)(2,1)}, bf16[512,1152]{1,0:T(8,128)(2,1)}, u32[]{:S(2)}, u32[]{:S(2)}) collective-permute-start(bf16[512,1152]{1,0:T(8,128)(2,1)} %get-tuple-element.24.main), channel_id=1, source_target_pairs={{0,255},{3,4},{4,3},{7,8},{8,7},{11,12},{12,11},{15,16},{16,15},{1... | collective-permute-start | bytes 3538952 | tf_op jit(solution)/shard_map/ppermute | solution.py:34
  14.3 40.0 %collective-permute-start.2 = (bf16[512,1152]{1,0:T(8,128)(2,1)}, bf16[512,1152]{1,0:T(8,128)(2,1)S(1)}, u32[]{:S(2)}, u32[]{:S(2)}) collective-permute-start(bf16[512,1152]{1,0:T(8,128)(2,1)} %get-tuple-element.24.main), channel_id=1, source_target_pairs={{0,254},{1,255},{2,4},{3,5},{4,2},{5,3},{6,8},{7,9},{8,6},{9,7},{1... | collective-permute-start | bytes 3538952 | tf_op jit(solution)/shard_map/ppermute | solution.py:34
  14.4 40.8 %collective-permute-start.1 = (bf16[512,1152]{1,0:T(8,128)(2,1)S(1)}, bf16[512,1152]{1,0:T(8,128)(2,1)S(1)}, u32[]{:S(2)}, u32[]{:S(2)}) collective-permute-start(bf16[512,1152]{1,0:T(8,128)(2,1)S(1)} %get-tuple-element.25.other), channel_id=1, source_target_pairs={{0,1},{1,4},{2,255},{3,2},{4,5},{5,8},{6,3},{7,6},{8,9},{9,12},{10... | collective-permute-start | bytes 3538952 | tf_op jit(solution)/shard_map/ppermute | solution.py:34
  55.2 19.6 %collective-permute-start.4 = (bf16[512,1152]{1,0:T(8,128)(2,1)S(1)}, bf16[512,1152]{1,0:T(8,128)(2,1)S(1)}, u32[]{:S(2)}, u32[]{:S(2)}) collective-permute-start(bf16[512,1152]{1,0:T(8,128)(2,1)S(1)} %collective-permute-done.1.of_other), channel_id=1, source_target_pairs={{0,254},{1,3},{2,0},{3,5},{4,2},{5,7},{6,4},{7,9},{8,6},{9,11},{10... | collective-permute-start | bytes 3538952 | tf_op jit(solution)/shard_map/ppermute | solution.py:34
  61.1 13.7 %collective-permute-start.5 = (bf16[512,1152]{1,0:T(8,128)(2,1)}, bf16[512,1152]{1,0:T(8,128)(2,1)S(1)}, u32[]{:S(2)}, u32[]{:S(2)}) collective-permute-start(bf16[512,1152]{1,0:T(8,128)(2,1)} %collective-permute-done.3.near_main), channel_id=1, source_target_pairs={{0,2},{3,1},{4,6},{7,5},{8,10},{11,9},{12,14},{15,13},{16,18},{19,... | collective-permute-start | bytes 3538952 | tf_op jit(solution)/shard_map/ppermute | solution.py:34
  62.5 25.0 %collective-permute-start.6 = (bf16[512,1152]{1,0:T(8,128)(2,1)S(1)}, bf16[512,1152]{1,0:T(8,128)(2,1)S(1)}, u32[]{:S(2)}, u32[]{:S(2)}) collective-permute-start(bf16[512,1152]{1,0:T(8,128)(2,1)S(1)} %shard_map.68), channel_id=1, source_target_pairs={{0,255},{1,254},{2,5},{3,4},{4,3},{5,2},{6,9},{7,8},{8,7},{9,6},{1... | collective-permute-start | bytes 3538952 | tf_op jit(solution)/shard_map/ppermute | solution.py:34

commit v8 on v7

--- a/solution.py
+++ b/solution.py
@@ -245,11 +245,10 @@
 
     second, near_main, loss = together(second, near_main, loss)
     (late_low,) = call(late_block_kernel, "svv", [("v", whole, low)])(role, lows, second)
-    of_other, late_low = together(of_other, late_low)
+    to_inner = send(near_main, NEAR_TO_INNER)
+    of_other, late_low, to_inner = together(of_other, late_low, to_inner)
     by_two = send(of_other, ON_OR_TO_OUTER)
     late_low = send(late_low, FAR_OR_ON_BY_ONE)
-    to_inner = send(near_main, NEAR_TO_INNER)
-
     accs, loss = call(
         middle_kernel,
         "ssvvvvvv",

time: 92.9 us -> 97.1 us (1.045)
  waiting for transfers between devices: 40 us -> 43.5 us
    ppermute x7, waiting for transfers between devices: 40 us -> 43.5 us  [send(): return lax.ppermute(x, AXES, pairs())]
  transfers between devices with their start and end apart: 7 -> 7, of which waited for: 4 -> 5; matrix products, arithmetic and copies ran while one was open for 0% -> 0% of each run, Pallas kernels for 24% -> 23%
where the time goes in v8:
time: 97.1 us; the launch traced here: 96.8 us
  waiting for transfers between devices  43.5 us (45%)
  Pallas kernels  27.3 us (28%)
  starting transfers between devices  20.8 us (21%)
  other arithmetic  3.01 us (3%)
  between operations  2.23 us (2%)
    ppermute x7, waiting for transfers between devices, send(): return lax.ppermute(x, AXES, pairs())  43.5 us
    ppermute x7, starting transfers between devices, send(): return lax.ppermute(x, AXES, pairs())  20.8 us
    pallas_call x1, Pallas kernels, body(): call(first_kernel, 'ssvvv', [('v', both, low), ('v', both, f32), ('v', (2...  7.54 us
    pallas_call x1, Pallas kernels, body(): call(early_kernel, 'ssvvvvvvvv', [('a', whole, f32), ('a', whole, f32), (...  7.35 us
    pallas_call x1, Pallas kernels, body(): call(middle_kernel, 'ssvvvvvv', [('v', both, f32), ('v', partial, f32)],...  6.53 us
    pallas_call x1, Pallas kernels, body(): call(late_kernel, 'ssvvvvvvaa', [('a', whole, f32), ('a', whole, f32), ('...  4.97 us
    select_n x1, other arithmetic, body(): other = jnp.where(is_core_1, image_emb, text_emb)  2.86 us
  transfers between devices with their start and end apart: 7, of which 5 were waited for; matrix products, arithmetic and copies ran while one was open for 0% of the time, Pallas kernels for 23%

profile of v8, /device:TPU:0, one launch (start us, length us, event | category | flops | bytes accessed | tf_op | source)
XLA Modules:
  0.0 96.8 jit_solution(882826391716728465)
XLA Ops:
  0.7 2.9 %broadcast_select_fusion = (bf16[512,1152]{1,0:T(8,128)(2,1)S(1)}, bf16[512,1152]{1,0:T(8,128)(2,1)}) fusion(bf16[512,1152]{1,0:T(8,128)(2,1)} %param.4, bf16[512,1152]{1,0:T(8,128)(2,1)} %param.5, pred[]{:T(512)S(6)} %eq.6), kind=kLoop, calls=%fused_computation | loop fusion | flops 1179648 | bytes 4718593 | tf_op jit(solution)/shard_map/jit(_where)/select_n | solution.py:229
  3.5 0.0 collective-permute-start
  3.5 10.8 %collective-permute-start.3 = (bf16[512,1152]{1,0:T(8,128)(2,1)}, bf16[512,1152]{1,0:T(8,128)(2,1)}, u32[]{:S(2)}, u32[]{:S(2)}) collective-permute-start(bf16[512,1152]{1,0:T(8,128)(2,1)} %get-tuple-element.25.main), channel_id=1, source_target_pairs={{0,255},{3,4},{4,3},{7,8},{8,7},{11,12},{12,11},{15,16},{16,15},{1... | collective-permute-start | bytes 3538952 | tf_op jit(solution)/shard_map/ppermute | solution.py:34
  14.3 0.1 collective-permute-start.2
  14.4 1.5 %collective-permute-start.1 = (bf16[512,1152]{1,0:T(8,128)(2,1)S(1)}, bf16[512,1152]{1,0:T(8,128)(2,1)S(1)}, u32[]{:S(2)}, u32[]{:S(2)}) collective-permute-start(bf16[512,1152]{1,0:T(8,128)(2,1)S(1)} %get-tuple-element.26.other), channel_id=1, source_target_pairs={{0,1},{1,4},{2,255},{3,2},{4,5},{5,8},{6,3},{7,6},{8,9},{9,12},{10... | collective-permute-start | bytes 3538952 | tf_op jit(solution)/shard_map/ppermute | solution.py:34
  17.2 0.1 pad_add_fusion.role_ref
  17.3 0.1 pad_maximum_fusion.numbers_ref
  17.4 0.0 collective-permute-done.swapped
  17.4 7.5 %shard_map.67 = (bf16[2,512,1152]{2,1,0:T(8,128)(2,1)S(1)}, f32[2,512,1152]{2,1,0:T(8,128)S(1)}, f32[2,512,1]{2,1,0:T(8,128)S(1)}, f32[2,512,1152]{2,1,0:T(8,128)S(1)}, f32[512,128]{1,0:T(8,128)S(1)}) custom-call(s32[2]{0:T(128)S(1)} %pad_add_fusion.role_ref, f32[2]{0:T(128)S(1)} %pad_maximum_fusion.numbers_ref, bf16[512,1152]{1,0:T(8,128)(2,1)} %get-tuple-element.25.main, ...), custom_call_target="tpu_custom_call" | custom-call | tf_op jit(solution)/shard_map/pallas_call | solution.py:239
  24.9 15.5 %collective-permute-done.3.near_main = bf16[512,1152]{1,0:T(8,128)(2,1)} collective-permute-done((bf16[512,1152]{1,0:T(8,128)(2,1)}, bf16[512,1152]{1,0:T(8,128)(2,1)}, u32[]{:S(2)}, u32[]{:S(2)}) %collective-permute-start.3) | collective-permute-done | bytes 1179680 | tf_op jit(solution)/shard_map/ppermute | solution.py:34
  40.4 13.9 %collective-permute-done.2.second = bf16[512,1152]{1,0:T(8,128)(2,1)S(1)} collective-permute-done((bf16[512,1152]{1,0:T(8,128)(2,1)}, bf16[512,1152]{1,0:T(8,128)(2,1)S(1)}, u32[]{:S(2)}, u32[]{:S(2)}) %collective-permute-start.2) | collective-permute-done | bytes 1179680 | tf_op jit(solution)/shard_map/ppermute | solution.py:34
  54.3 1.4 %collective-permute-start.4 = (bf16[512,1152]{1,0:T(8,128)(2,1)}, bf16[512,1152]{1,0:T(8,128)(2,1)S(1)}, u32[]{:S(2)}, u32[]{:S(2)}) collective-permute-start(bf16[512,1152]{1,0:T(8,128)(2,1)} %collective-permute-done.3.near_main), channel_id=1, source_target_pairs={{0,2},{3,1},{4,6},{7,5},{8,10},{11,9},{12,14},{15,13},{16,18},{19,... | collective-permute-start | bytes 3538952 | tf_op jit(solution)/shard_map/ppermute | solution.py:34
  55.7 0.9 shard_map.68
  56.6 0.0 collective-permute-done.1.of_other
  56.6 1.7 %collective-permute-done.4.to_inner = bf16[512,1152]{1,0:T(8,128)(2,1)S(1)} collective-permute-done((bf16[512,1152]{1,0:T(8,128)(2,1)}, bf16[512,1152]{1,0:T(8,128)(2,1)S(1)}, u32[]{:S(2)}, u32[]{:S(2)}) %collective-permute-start.4) | collective-permute-done | bytes 1179680 | tf_op jit(solution)/shard_map/ppermute | solution.py:34
  58.3 7.1 %collective-permute-start.5 = (bf16[512,1152]{1,0:T(8,128)(2,1)S(1)}, bf16[512,1152]{1,0:T(8,128)(2,1)S(1)}, u32[]{:S(2)}, u32[]{:S(2)}) collective-permute-start(bf16[512,1152]{1,0:T(8,128)(2,1)S(1)} %collective-permute-done.1.of_other), channel_id=1, source_target_pairs={{0,254},{1,3},{2,0},{3,5},{4,2},{5,7},{6,4},{7,9},{8,6},{9,11},{10... | collective-permute-start | bytes 3538952 | tf_op jit(solution)/shard_map/ppermute | solution.py:34
  65.3 0.0 collective-permute-start.6
  65.3 6.5 %shard_map.69 = (f32[2,512,1152]{2,1,0:T(8,128)S(1)}, f32[512,128]{1,0:T(8,128)S(1)}) custom-call(s32[2]{0:T(128)S(1)} %pad_add_fusion.role_ref, f32[2]{0:T(128)S(1)} %pad_maximum_fusion.numbers_ref, bf16[2,512,1152]{2,1,0:T(8,128)(2,1)S(1)} %get-tuple-element.27.lows, ...), custom_call_target="tpu_custom_call", output_to_operand_aliasing={{0}: (6, {}), {1}: (7, {})} | custom-call | tf_op jit(solution)/shard_map/pallas_call | solution.py:252
  71.9 7.2 %collective-permute-done.5.by_two = bf16[512,1152]{1,0:T(8,128)(2,1)S(1)} collective-permute-done((bf16[512,1152]{1,0:T(8,128)(2,1)S(1)}, bf16[512,1152]{1,0:T(8,128)(2,1)S(1)}, u32[]{:S(2)}, u32[]{:S(2)}) %collective-permute-start.5) | collective-permute-done | bytes 1179680 | tf_op jit(solution)/shard_map/ppermute | solution.py:34
  79.1 7.3 %shard_map.70 = (f32[512,1152]{1,0:T(8,128)}, f32[512,1152]{1,0:T(8,128)}, f32[2,512,1152]{2,1,0:T(8,128)S(1)}, f32[512,128]{1,0:T(8,128)S(1)}) custom-call(s32[2]{0:T(128)S(1)} %pad_add_fusion.role_ref, f32[2]{0:T(128)S(1)} %pad_maximum_fusion.numbers_ref, ...), custom_call_target="tpu_custom_call", output_to_operand_aliasing={{2}: (8, {}), {3}: (9, {})} | custom-call | tf_op jit(solution)/shard_map/pallas_call | solution.py:261
  86.4 5.3 %collective-permute-done.6.late_low = bf16[512,1152]{1,0:T(8,128)(2,1)S(1)} collective-permute-done((bf16[512,1152]{1,0:T(8,128)(2,1)S(1)}, bf16[512,1152]{1,0:T(8,128)(2,1)S(1)}, u32[]{:S(2)}, u32[]{:S(2)}) %collective-permute-start.6) | collective-permute-done | bytes 1179680 | tf_op jit(solution)/shard_map/ppermute | solution.py:34
  91.7 5.0 %shard_map.71 = (f32[512,1152]{1,0:T(8,128)}, f32[512,1152]{1,0:T(8,128)}, f32[1,512]{1,0:T(1,128)}) custom-call(s32[2]{0:T(128)S(1)} %pad_add_fusion.role_ref, f32[2]{0:T(128)S(1)} %pad_maximum_fusion.numbers_ref, bf16[2,512,1152]{2,1,0:T(8,128)(2,1)S(1)} %get-tuple-element.27.lows, ...), custom_call_target="tpu_custom_call", output_to_operand_aliasing={{0}: (8, {}), {1}: (9, {})} | custom-call | tf_op jit(solution)/shard_map/pallas_call | solution.py:268
Async XLA Ops:
  3.5 13.8 %collective-permute-start = (bf16[512,1152]{1,0:T(8,128)(2,1)S(1)}, bf16[512,1152]{1,0:T(8,128)(2,1)}, u32[]{:S(2)}, u32[]{:S(2)}) collective-permute-start(bf16[512,1152]{1,0:T(8,128)(2,1)S(1)} %get-tuple-element.26.other), channel_id=1, source_target_pairs={{0,2},{1,3},{2,0},{3,1},{4,6},{5,7},{6,4},{7,5},{8,10},{9,11},{10,... | collective-permute-start | bytes 3538952 | tf_op jit(solution)/shard_map/ppermute | solution.py:34
  3.5 36.9 %collective-permute-start.3 = (bf16[512,1152]{1,0:T(8,128)(2,1)}, bf16[512,1152]{1,0:T(8,128)(2,1)}, u32[]{:S(2)}, u32[]{:S(2)}) collective-permute-start(bf16[512,1152]{1,0:T(8,128)(2,1)} %get-tuple-element.25.main), channel_id=1, source_target_pairs={{0,255},{3,4},{4,3},{7,8},{8,7},{11,12},{12,11},{15,16},{16,15},{1... | collective-permute-start | bytes 3538952 | tf_op jit(solution)/shard_map/ppermute | solution.py:34
  14.3 40.0 %collective-permute-start.2 = (bf16[512,1152]{1,0:T(8,128)(2,1)}, bf16[512,1152]{1,0:T(8,128)(2,1)S(1)}, u32[]{:S(2)}, u32[]{:S(2)}) collective-permute-start(bf16[512,1152]{1,0:T(8,128)(2,1)} %get-tuple-element.25.main), channel_id=1, source_target_pairs={{0,254},{1,255},{2,4},{3,5},{4,2},{5,3},{6,8},{7,9},{8,6},{9,7},{1... | collective-permute-start | bytes 3538952 | tf_op jit(solution)/shard_map/ppermute | solution.py:34
  14.4 42.2 %collective-permute-start.1 = (bf16[512,1152]{1,0:T(8,128)(2,1)S(1)}, bf16[512,1152]{1,0:T(8,128)(2,1)S(1)}, u32[]{:S(2)}, u32[]{:S(2)}) collective-permute-start(bf16[512,1152]{1,0:T(8,128)(2,1)S(1)} %get-tuple-element.26.other), channel_id=1, source_target_pairs={{0,1},{1,4},{2,255},{3,2},{4,5},{5,8},{6,3},{7,6},{8,9},{9,12},{10... | collective-permute-start | bytes 3538952 | tf_op jit(solution)/shard_map/ppermute | solution.py:34
  54.3 4.0 %collective-permute-start.4 = (bf16[512,1152]{1,0:T(8,128)(2,1)}, bf16[512,1152]{1,0:T(8,128)(2,1)S(1)}, u32[]{:S(2)}, u32[]{:S(2)}) collective-permute-start(bf16[512,1152]{1,0:T(8,128)(2,1)} %collective-permute-done.3.near_main), channel_id=1, source_target_pairs={{0,2},{3,1},{4,6},{7,5},{8,10},{11,9},{12,14},{15,13},{16,18},{19,... | collective-permute-start | bytes 3538952 | tf_op jit(solution)/shard_map/ppermute | solution.py:34
  58.3 20.8 %collective-permute-start.5 = (bf16[512,1152]{1,0:T(8,128)(2,1)S(1)}, bf16[512,1152]{1,0:T(8,128)(2,1)S(1)}, u32[]{:S(2)}, u32[]{:S(2)}) collective-permute-start(bf16[512,1152]{1,0:T(8,128)(2,1)S(1)} %collective-permute-done.1.of_other), channel_id=1, source_target_pairs={{0,254},{1,3},{2,0},{3,5},{4,2},{5,7},{6,4},{7,9},{8,6},{9,11},{10... | collective-permute-start | bytes 3538952 | tf_op jit(solution)/shard_map/ppermute | solution.py:34
  65.3 26.4 %collective-permute-start.6 = (bf16[512,1152]{1,0:T(8,128)(2,1)S(1)}, bf16[512,1152]{1,0:T(8,128)(2,1)S(1)}, u32[]{:S(2)}, u32[]{:S(2)}) collective-permute-start(bf16[512,1152]{1,0:T(8,128)(2,1)S(1)} %shard_map.68), channel_id=1, source_target_pairs={{0,255},{1,254},{2,5},{3,4},{4,3},{5,2},{6,9},{7,8},{8,7},{9,6},{1... | collective-permute-start | bytes 3538952 | tf_op jit(solution)/shard_map/ppermute | solution.py:34

commit v9 on v7

--- a/solution.py
+++ b/solution.py
@@ -225,9 +225,8 @@
     role = jnp.stack([core, place % 2]).astype(jnp.int32)
     numbers = jnp.stack([jnp.exp(log_temp), bias])
     is_core_1 = core == 1
-    main = jnp.where(is_core_1, text_emb, image_emb)
-    other = jnp.where(is_core_1, image_emb, text_emb)
-    main, other = together(main, other)
+    other, image_late, text_late = together(jnp.where(is_core_1, image_emb, text_emb), image_emb, text_emb)
+    main = jnp.where(is_core_1, text_late, image_late)
 
     swapped = send(other, SWAP)
     of_other = send(other, OF_OTHER)

time: 92.9 us -> 92.8 us (level)
    select_n x1 -> x2, other arithmetic: 2.86 us -> 2.71 us  [the longest x1 1.57 us: body(): jnp.where(is_core_1, image_emb, text_emb)]
  transfers between devices with their start and end apart: 7 -> 7, of which waited for: 4 -> 4; matrix products, arithmetic and copies ran while one was open for 0% -> 1% of each run, Pallas kernels for 24% -> 24%
where the time goes in v9:
time: 92.8 us; the launch traced here: 92.6 us
  waiting for transfers between devices  40 us (43%)
  Pallas kernels  27.3 us (29%)
  starting transfers between devices  19.9 us (21%)
  other arithmetic  2.86 us (3%)
  between operations  2.27 us (2%)
    ppermute x7, waiting for transfers between devices, send(): return lax.ppermute(x, AXES, pairs())  40 us
    ppermute x7, starting transfers between devices, send(): return lax.ppermute(x, AXES, pairs())  19.9 us
    pallas_call x1, Pallas kernels, body(): call(first_kernel, 'ssvvv', [('v', both, low), ('v', both, f32), ('v', (2...  7.54 us
    pallas_call x1, Pallas kernels, body(): call(early_kernel, 'ssvvvvvvvv', [('a', whole, f32), ('a', whole, f32), (...  7.35 us
    pallas_call x1, Pallas kernels, body(): call(middle_kernel, 'ssvvvvvv', [('v', both, f32), ('v', partial, f32)],...  6.54 us
    pallas_call x1, Pallas kernels, body(): call(late_kernel, 'ssvvvvvvaa', [('a', whole, f32), ('a', whole, f32), ('...  4.98 us
  transfers between devices with their start and end apart: 7, of which 4 were waited for; matrix products, arithmetic and copies ran while one was open for 1% of the time, Pallas kernels for 24%

profile of v9, /device:TPU:0, one launch (start us, length us, event | category | flops | bytes accessed | tf_op | source)
XLA Modules:
  0.0 92.6 jit_solution(3737825787026591627)
XLA Ops:
  0.7 1.6 %broadcast_select_fusion.1.other = bf16[512,1152]{1,0:T(8,128)(2,1)S(1)} fusion(bf16[512,1152]{1,0:T(8,128)(2,1)} %param.4, bf16[512,1152]{1,0:T(8,128)(2,1)} %param.5, pred[]{:T(512)S(6)} %eq.6), kind=kLoop, calls=%fused_computation.1 | loop fusion | flops 589824 | bytes 3538945 | tf_op jit(solution)/shard_map/jit(_where)/select_n | solution.py:228
  2.3 0.1 collective-permute-start
  2.4 0.3 copy-done.1
  2.6 1.1 %broadcast_select_fusion.main = bf16[512,1152]{1,0:T(8,128)(2,1)} fusion(bf16[512,1152]{1,0:T(8,128)(2,1)S(1)} %copy-done, bf16[512,1152]{1,0:T(8,128)(2,1)S(1)} %copy-done.1, pred[]{:T(512)S(6)} %eq.6), kind=kLoop, calls=%fused_computation | loop fusion | flops 589824 | bytes 3538945 | tf_op jit(solution)/shard_map/jit(_where)/select_n | solution.py:229
  3.8 10.5 %collective-permute-start.3 = (bf16[512,1152]{1,0:T(8,128)(2,1)}, bf16[512,1152]{1,0:T(8,128)(2,1)}, u32[]{:S(2)}, u32[]{:S(2)}) collective-permute-start(bf16[512,1152]{1,0:T(8,128)(2,1)} %broadcast_select_fusion.main), channel_id=1, source_target_pairs={{0,255},{3,4},{4,3},{7,8},{8,7},{11,12},{12,11},{15,16},{16,15},{1... | collective-permute-start | bytes 3538952 | tf_op jit(solution)/shard_map/ppermute | solution.py:34
  14.3 0.1 collective-permute-start.2
  14.4 1.5 %collective-permute-start.1 = (bf16[512,1152]{1,0:T(8,128)(2,1)S(1)}, bf16[512,1152]{1,0:T(8,128)(2,1)S(1)}, u32[]{:S(2)}, u32[]{:S(2)}) collective-permute-start(bf16[512,1152]{1,0:T(8,128)(2,1)S(1)} %broadcast_select_fusion.1.other), channel_id=1, source_target_pairs={{0,1},{1,4},{2,255},{3,2},{4,5},{5,8},{6,3},{7,6},{8,9},{9,12},{10... | collective-permute-start | bytes 3538952 | tf_op jit(solution)/shard_map/ppermute | solution.py:34
  17.2 0.1 pad_add_fusion.role_ref
  17.3 0.1 pad_maximum_fusion.numbers_ref
  17.3 0.0 collective-permute-done.swapped
  17.3 7.5 %shard_map.67 = (bf16[2,512,1152]{2,1,0:T(8,128)(2,1)S(1)}, f32[2,512,1152]{2,1,0:T(8,128)S(1)}, f32[2,512,1]{2,1,0:T(8,128)S(1)}, f32[2,512,1152]{2,1,0:T(8,128)S(1)}, f32[512,128]{1,0:T(8,128)S(1)}) custom-call(s32[2]{0:T(128)S(1)} %pad_add_fusion.role_ref, f32[2]{0:T(128)S(1)} %pad_maximum_fusion.numbers_ref, ...), custom_call_target="tpu_custom_call" | custom-call | tf_op jit(solution)/shard_map/pallas_call | solution.py:238
  24.9 15.5 %collective-permute-done.3.near_main = bf16[512,1152]{1,0:T(8,128)(2,1)} collective-permute-done((bf16[512,1152]{1,0:T(8,128)(2,1)}, bf16[512,1152]{1,0:T(8,128)(2,1)}, u32[]{:S(2)}, u32[]{:S(2)}) %collective-permute-start.3) | collective-permute-done | bytes 1179680 | tf_op jit(solution)/shard_map/ppermute | solution.py:34
  40.4 13.9 %collective-permute-done.2.second = bf16[512,1152]{1,0:T(8,128)(2,1)S(1)} collective-permute-done((bf16[512,1152]{1,0:T(8,128)(2,1)}, bf16[512,1152]{1,0:T(8,128)(2,1)S(1)}, u32[]{:S(2)}, u32[]{:S(2)}) %collective-permute-start.2) | collective-permute-done | bytes 1179680 | tf_op jit(solution)/shard_map/ppermute | solution.py:34
  54.3 0.9 shard_map.68
  55.2 0.0 collective-permute-done.1.of_other
  55.2 5.9 %collective-permute-start.4 = (bf16[512,1152]{1,0:T(8,128)(2,1)S(1)}, bf16[512,1152]{1,0:T(8,128)(2,1)S(1)}, u32[]{:S(2)}, u32[]{:S(2)}) collective-permute-start(bf16[512,1152]{1,0:T(8,128)(2,1)S(1)} %collective-permute-done.1.of_other), channel_id=1, source_target_pairs={{0,254},{1,3},{2,0},{3,5},{4,2},{5,7},{6,4},{7,9},{8,6},{9,11},{10... | collective-permute-start | bytes 3538952 | tf_op jit(solution)/shard_map/ppermute | solution.py:34
  61.1 1.4 %collective-permute-start.5 = (bf16[512,1152]{1,0:T(8,128)(2,1)}, bf16[512,1152]{1,0:T(8,128)(2,1)S(1)}, u32[]{:S(2)}, u32[]{:S(2)}) collective-permute-start(bf16[512,1152]{1,0:T(8,128)(2,1)} %collective-permute-done.3.near_main), channel_id=1, source_target_pairs={{0,2},{3,1},{4,6},{7,5},{8,10},{11,9},{12,14},{15,13},{16,18},{19,... | collective-permute-start | bytes 3538952 | tf_op jit(solution)/shard_map/ppermute | solution.py:34
  62.5 0.5 collective-permute-start.6
  63.0 6.5 %shard_map.69 = (f32[2,512,1152]{2,1,0:T(8,128)S(1)}, f32[512,128]{1,0:T(8,128)S(1)}) custom-call(s32[2]{0:T(128)S(1)} %pad_add_fusion.role_ref, f32[2]{0:T(128)S(1)} %pad_maximum_fusion.numbers_ref, bf16[2,512,1152]{2,1,0:T(8,128)(2,1)S(1)} %get-tuple-element.28.lows, ...), custom_call_target="tpu_custom_call", output_to_operand_aliasing={{0}: (6, {}), {1}: (7, {})} | custom-call | tf_op jit(solution)/shard_map/pallas_call | solution.py:252
  69.5 5.3 %collective-permute-done.4.by_two = bf16[512,1152]{1,0:T(8,128)(2,1)S(1)} collective-permute-done((bf16[512,1152]{1,0:T(8,128)(2,1)S(1)}, bf16[512,1152]{1,0:T(8,128)(2,1)S(1)}, u32[]{:S(2)}, u32[]{:S(2)}) %collective-permute-start.4) | collective-permute-done | bytes 1179680 | tf_op jit(solution)/shard_map/ppermute | solution.py:34
  74.8 0.0 collective-permute-done.5.to_inner
  74.8 7.3 %shard_map.70 = (f32[512,1152]{1,0:T(8,128)}, f32[512,1152]{1,0:T(8,128)}, f32[2,512,1152]{2,1,0:T(8,128)S(1)}, f32[512,128]{1,0:T(8,128)S(1)}) custom-call(s32[2]{0:T(128)S(1)} %pad_add_fusion.role_ref, f32[2]{0:T(128)S(1)} %pad_maximum_fusion.numbers_ref, ...), custom_call_target="tpu_custom_call", output_to_operand_aliasing={{2}: (8, {}), {3}: (9, {})} | custom-call | tf_op jit(solution)/shard_map/pallas_call | solution.py:261
  82.2 5.3 %collective-permute-done.6.late_low = bf16[512,1152]{1,0:T(8,128)(2,1)S(1)} collective-permute-done((bf16[512,1152]{1,0:T(8,128)(2,1)S(1)}, bf16[512,1152]{1,0:T(8,128)(2,1)S(1)}, u32[]{:S(2)}, u32[]{:S(2)}) %collective-permute-start.6) | collective-permute-done | bytes 1179680 | tf_op jit(solution)/shard_map/ppermute | solution.py:34
  87.5 5.0 %shard_map.71 = (f32[512,1152]{1,0:T(8,128)}, f32[512,1152]{1,0:T(8,128)}, f32[1,512]{1,0:T(1,128)}) custom-call(s32[2]{0:T(128)S(1)} %pad_add_fusion.role_ref, f32[2]{0:T(128)S(1)} %pad_maximum_fusion.numbers_ref, bf16[2,512,1152]{2,1,0:T(8,128)(2,1)S(1)} %get-tuple-element.28.lows, ...), custom_call_target="tpu_custom_call", output_to_operand_aliasing={{0}: (8, {}), {1}: (9, {})} | custom-call | tf_op jit(solution)/shard_map/pallas_call | solution.py:268
  (3 shorter events, 0.0 us)
Async XLA Ops:
  0.7 1.7 %copy-start = (bf16[512,1152]{1,0:T(8,128)(2,1)S(1)}, bf16[512,1152]{1,0:T(8,128)(2,1)}, u32[]{:S(2)}) copy-start(bf16[512,1152]{1,0:T(8,128)(2,1)} %param.5) | copy-start | bytes 3538948
  0.7 2.0 %copy-start.1 = (bf16[512,1152]{1,0:T(8,128)(2,1)S(1)}, bf16[512,1152]{1,0:T(8,128)(2,1)}, u32[]{:S(2)}) copy-start(bf16[512,1152]{1,0:T(8,128)(2,1)} %param.4) | copy-start | bytes 3538948
  2.3 15.1 %collective-permute-start = (bf16[512,1152]{1,0:T(8,128)(2,1)S(1)}, bf16[512,1152]{1,0:T(8,128)(2,1)}, u32[]{:S(2)}, u32[]{:S(2)}) collective-permute-start(bf16[512,1152]{1,0:T(8,128)(2,1)S(1)} %broadcast_select_fusion.1.other), channel_id=1, source_target_pairs={{0,2},{1,3},{2,0},{3,1},{4,6},{5,7},{6,4},{7,5},{8,10},{9,11},{10,... | collective-permute-start | bytes 3538952 | tf_op jit(solution)/shard_map/ppermute | solution.py:34
  3.8 36.6 %collective-permute-start.3 = (bf16[512,1152]{1,0:T(8,128)(2,1)}, bf16[512,1152]{1,0:T(8,128)(2,1)}, u32[]{:S(2)}, u32[]{:S(2)}) collective-permute-start(bf16[512,1152]{1,0:T(8,128)(2,1)} %broadcast_select_fusion.main), channel_id=1, source_target_pairs={{0,255},{3,4},{4,3},{7,8},{8,7},{11,12},{12,11},{15,16},{16,15},{1... | collective-permute-start | bytes 3538952 | tf_op jit(solution)/shard_map/ppermute | solution.py:34
  14.3 40.0 %collective-permute-start.2 = (bf16[512,1152]{1,0:T(8,128)(2,1)}, bf16[512,1152]{1,0:T(8,128)(2,1)S(1)}, u32[]{:S(2)}, u32[]{:S(2)}) collective-permute-start(bf16[512,1152]{1,0:T(8,128)(2,1)} %broadcast_select_fusion.main), channel_id=1, source_target_pairs={{0,254},{1,255},{2,4},{3,5},{4,2},{5,3},{6,8},{7,9},{8,6},{9,7},{1... | collective-permute-start | bytes 3538952 | tf_op jit(solution)/shard_map/ppermute | solution.py:34
  14.4 40.8 %collective-permute-start.1 = (bf16[512,1152]{1,0:T(8,128)(2,1)S(1)}, bf16[512,1152]{1,0:T(8,128)(2,1)S(1)}, u32[]{:S(2)}, u32[]{:S(2)}) collective-permute-start(bf16[512,1152]{1,0:T(8,128)(2,1)S(1)} %broadcast_select_fusion.1.other), channel_id=1, source_target_pairs={{0,1},{1,4},{2,255},{3,2},{4,5},{5,8},{6,3},{7,6},{8,9},{9,12},{10... | collective-permute-start | bytes 3538952 | tf_op jit(solution)/shard_map/ppermute | solution.py:34
  55.2 19.6 %collective-permute-start.4 = (bf16[512,1152]{1,0:T(8,128)(2,1)S(1)}, bf16[512,1152]{1,0:T(8,128)(2,1)S(1)}, u32[]{:S(2)}, u32[]{:S(2)}) collective-permute-start(bf16[512,1152]{1,0:T(8,128)(2,1)S(1)} %collective-permute-done.1.of_other), channel_id=1, source_target_pairs={{0,254},{1,3},{2,0},{3,5},{4,2},{5,7},{6,4},{7,9},{8,6},{9,11},{10... | collective-permute-start | bytes 3538952 | tf_op jit(solution)/shard_map/ppermute | solution.py:34
  61.1 13.7 %collective-permute-start.5 = (bf16[512,1152]{1,0:T(8,128)(2,1)}, bf16[512,1152]{1,0:T(8,128)(2,1)S(1)}, u32[]{:S(2)}, u32[]{:S(2)}) collective-permute-start(bf16[512,1152]{1,0:T(8,128)(2,1)} %collective-permute-done.3.near_main), channel_id=1, source_target_pairs={{0,2},{3,1},{4,6},{7,5},{8,10},{11,9},{12,14},{15,13},{16,18},{19,... | collective-permute-start | bytes 3538952 | tf_op jit(solution)/shard_map/ppermute | solution.py:34
  62.5 25.0 %collective-permute-start.6 = (bf16[512,1152]{1,0:T(8,128)(2,1)S(1)}, bf16[512,1152]{1,0:T(8,128)(2,1)S(1)}, u32[]{:S(2)}, u32[]{:S(2)}) collective-permute-start(bf16[512,1152]{1,0:T(8,128)(2,1)S(1)} %shard_map.68), channel_id=1, source_target_pairs={{0,255},{1,254},{2,5},{3,4},{4,3},{5,2},{6,9},{7,8},{8,7},{9,6},{1... | collective-permute-start | bytes 3538952 | tf_op jit(solution)/shard_map/ppermute | solution.py:34
